TPU v7x, 512 devices: a whole 4x8x8 slice. The times are simulated.
512 devices in a mesh: group: 16 (over y, core), member: 32 (over z, x).
Axes of the slice: x: 4, y: 8, z: 8, core: 2. Of those that a mesh axis runs over, the one named last changes fastest.
Arguments:
- teacher_patches: bfloat16 [131072, 256], P(('group', 'member')), may hold values from -16 to 16
- student_patches: bfloat16 [131072, 256], P(('group', 'member')), may hold values from -16 to 16
- mask_index: int32 [65536], P(('group', 'member')), may hold values from 0 to 255, as said below
- teacher_weight: bfloat16 [256, 32768], P(None, 'member'), may hold values from -2 to 2
- student_weight: bfloat16 [256, 32768], P(None, 'member'), may hold values from -2 to 2
Outputs:
- grad_weight: bfloat16 [256, 32768], P(None, 'member')
Inputs may be any that keep to these rules, and one draw needn't show every extreme that they name: `mask_index`: within each aligned block of 128 entries the entries are distinct, and each names one of the 256 patch rows of that block's own device shard.
All inputs are finite; a program needn't handle non-finite values.
Results may differ from a plain program's by a relative error of at most 0.0065.
Values may be sent and summed in bfloat16 or wider, within the bound.
No kernel may reach another device: no remote copies, remote signals or barrier semaphores. Data moves between devices by JAX's collectives and lax.ppermute only.
A program may use at most 128 MiB of HBM per device.

v0:
```python
import math

import jax
import jax.numpy as jnp
from jax import lax
from jax.sharding import PartitionSpec as P

ITERS = 3


epsilon = 1e-06
teacher_scale = 1.0 / 0.07
student_scale = 1.0 / 0.1
grad_factor = 256.0 / 0.1


def unit_rows(values):
    values = values.astype(jnp.float32)
    return (values * lax.rsqrt(jnp.sum(values * values, axis=1, keepdims=True) + epsilon)).astype(
        jnp.bfloat16
    )


def unit_columns(values):
    values = values.astype(jnp.float32)
    return (values * lax.rsqrt(jnp.sum(values * values, axis=0, keepdims=True) + epsilon)).astype(
        jnp.bfloat16
    )


def exp_scores(rows, protos, scale):
    return jnp.exp(jnp.dot(rows, protos, preferred_element_type=jnp.float32) * scale).astype(
        jnp.bfloat16
    )


def weight_back(grad_sum, weight):
    weight = weight.astype(jnp.float32)
    inverse = lax.rsqrt(jnp.sum(weight * weight, axis=0, keepdims=True) + epsilon)
    along = jnp.sum(grad_sum * weight, axis=0, keepdims=True)
    return (grad_sum * inverse - weight * (inverse * inverse * inverse * along)).astype(
        jnp.bfloat16
    )


def block_map(func, rows):
    count = rows.shape[0]
    width = math.gcd(count, 512)
    blocks = count // width
    result = lax.map(func, rows.reshape(blocks, width, rows.shape[1]))
    return result.reshape(count, result.shape[2])


def shards(teacher_patches, student_patches, mask_index, teacher_weight, student_weight):
    teach_local = unit_rows(teacher_patches[mask_index])
    stud_local = unit_rows(student_patches[mask_index])
    teach_rows, stud_rows = (
        lax.all_gather(teach_local, "member", axis=0, tiled=True),
        lax.all_gather(stud_local, "member", axis=0, tiled=True),
    )
    teach_protos = unit_columns(teacher_weight)
    stud_protos = unit_columns(student_weight)
    codes = block_map(lambda rows: exp_scores(rows, teach_protos, teacher_scale), teach_rows)
    expo = block_map(lambda rows: exp_scores(rows, stud_protos, student_scale), stud_rows)
    local_norm = jnp.sum(expo.astype(jnp.float32), axis=1)
    student_norm = lax.psum(local_norm, "member")
    local_cols = jnp.sum(codes.astype(jnp.float32), axis=0)
    row_scale = jnp.ones((codes.shape[0],), jnp.float32)
    col_scale = jnp.ones((codes.shape[1],), jnp.float32)
    for sweep in range(ITERS):
        if sweep > 0:
            local_cols = jnp.sum(codes.astype(jnp.float32) * row_scale[:, None], axis=0)
        col_mass = lax.psum(local_cols, "group")
        col_scale = 1.0 / col_mass
        local_rows = jnp.sum(codes.astype(jnp.float32) * col_scale[None, :], axis=1)
        if sweep == 0:
            row_mass = lax.psum(local_rows, "member")
        else:
            row_mass = lax.psum(local_rows, "member")
        row_scale = 1.0 / row_mass
    target = codes.astype(jnp.float32) * row_scale[:, None] * col_scale[None, :]
    probs = expo.astype(jnp.float32) / student_norm[:, None]
    slope = (grad_factor * (probs - target)).astype(jnp.bfloat16)
    local_grad = lax.dot_general(
        stud_rows, slope, (((0,), (0,)), ((), ())), preferred_element_type=jnp.float32
    )
    grad_sum = lax.psum(local_grad, "group")
    return weight_back(grad_sum, student_weight)


def solution(mesh):
    in_specs = (
        P(("group", "member"), None),
        P(("group", "member"), None),
        P(("group", "member")),
        P(None, "member"),
        P(None, "member"),
    )
    out_specs = P(None, "member")
    return jax.shard_map(shards, mesh=mesh, in_specs=in_specs, out_specs=out_specs, check_vma=False)
```

profile of v0, /device:TPU:1, one launch (start us, length us, event | category | flops | bytes accessed | tf_op | source)
XLA Modules:
  0.0 796.2 jit_solution(17891083586426366708)
XLA Ops:
  6.5 0.0 copy-start
  6.5 0.0 all-gather.5.cloned.1.call-start
  6.5 0.7 compare_select_fusion
  7.2 0.2 copy-done
  7.5 0.8 gather_fusion.1
  8.3 0.1 fusion.28
  8.4 0.7 fusion.29
  9.1 0.0 all-gather.5.cloned.1.call-update
  9.2 0.0 all-gather.3.cloned.1.call-start
  9.2 1.7 gather_fusion
  10.9 0.1 fusion.26
  11.0 0.7 fusion.27
  11.7 0.0 all-gather.3.cloned.1.call-update
  11.8 0.0 all-reduce.3.cloned.1.call-start
  11.8 1.2 fusion.21
  13.0 1.2 fusion.19
  14.2 1.1 fusion.20
  15.3 1.1 fusion.22
  16.5 79.5 %all-gather.5.cloned.1.call-done = bf16[4096,256]{1,0:T(8,128)(2,1)} async-done(((bf16[128,256]{1,0:T(8,128)(2,1)}), bf16[4096,256]{1,0:T(8,128)(2,1)}) %all-gather.5.cloned.1.call-update) | async-done | bytes 2097168 | tf_op jit(solution)/shard_map/all_gather | solution.py:58
  96.0 4.3 broadcast.74.clone
  100.3 19.3 %while.21 = (s32[]{:T(128)}, bf16[8,512,1024]{2,1,0:T(8,128)(2,1)}, bf16[8,512,256]{2,1,0:T(8,128)(2,1)}, bf16[256,1024]{1,0:T(8,128)(2,1)S(1)}, s32[]{:T(128)}) while((s32[]{:T(128)}, bf16[8,512,1024]{2,1,0:T(8,128)(2,1)}, bf16[8,512,256]{2,1,0:T(8,128)(2,1)}, bf16[256,1024]{1,0:T(8,128)(2,1)S(1)}, s32[]{:T(128)}) %tuple.44), condition=%wide.region_9.10_spmd, body=%wide.region_8.9_spmd.sunk | while | flops 269484032 | bytes 1836101 | solution.py:50
  100.3 2.5 fusion.47
  102.8 2.4 fusion.47
  105.2 2.4 fusion.47
  107.6 2.4 fusion.47
  110.0 2.5 fusion.47
  112.4 2.4 fusion.47
  114.8 2.4 fusion.47
  117.2 2.4 fusion.47
  119.6 4.6 convert_reduce_fusion
  124.2 28.0 %psum.57 = f32[1024]{0:T(1024)S(1)} all-reduce(f32[1024]{0:T(1024)S(1)} %convert_reduce_fusion), channel_id=1, replica_groups=mesh['group'=16,'member'=32] {'group'}, use_global_device_ids=true, to_apply=%region_11.12 | all-reduce | flops 1024 | bytes 8192 | tf_op jit(solution)/shard_map/psum | solution.py:73
  152.2 5.2 fusion.10
  157.5 112.1 %psum.58 = f32[4096]{0:T(1024)S(1)} all-reduce(f32[4096]{0:T(1024)S(1)} %bitcast.62), channel_id=1, replica_groups=mesh['group'=16,'member'=32] {'member'}, use_global_device_ids=true, to_apply=%region_13.14 | all-reduce | flops 4096 | bytes 32768 | tf_op jit(solution)/shard_map/psum | solution.py:77
  269.6 5.1 fusion.11
  274.7 51.4 %psum.59 = f32[1024]{0:T(1024)S(1)} all-reduce(f32[1024]{0:T(1024)S(1)} %fusion.11), channel_id=1, replica_groups=mesh['group'=16,'member'=32] {'group'}, use_global_device_ids=true, to_apply=%region_15.16 | all-reduce | flops 1024 | bytes 8192 | tf_op jit(solution)/shard_map/psum | solution.py:73
  326.2 5.1 fusion.12
  331.3 109.9 %psum.60 = f32[4096]{0:T(1024)S(1)} all-reduce(f32[4096]{0:T(1024)S(1)} %bitcast.63), channel_id=1, replica_groups=mesh['group'=16,'member'=32] {'member'}, use_global_device_ids=true, to_apply=%region_17.18 | all-reduce | flops 4096 | bytes 32768 | tf_op jit(solution)/shard_map/psum | solution.py:79
  441.2 5.1 fusion.13
  446.3 51.5 %psum.61 = f32[1024]{0:T(1024)S(1)} all-reduce(f32[1024]{0:T(1024)S(1)} %fusion.13), channel_id=1, replica_groups=mesh['group'=16,'member'=32] {'group'}, use_global_device_ids=true, to_apply=%region_19.20 | all-reduce | flops 1024 | bytes 8192 | tf_op jit(solution)/shard_map/psum | solution.py:73
  497.8 5.1 fusion.14
  503.0 0.0 all-gather.3.cloned.1.call-done
  503.0 0.0 copy-start.2
  503.0 4.3 broadcast.74.clone.1
  507.3 0.0 copy-done.2
  507.3 11.6 %while.20 = (s32[]{:T(128)}, bf16[8,512,1024]{2,1,0:T(8,128)(2,1)}, bf16[8,512,256]{2,1,0:T(8,128)(2,1)S(1)}, bf16[256,1024]{1,0:T(8,128)(2,1)S(1)}, s32[]{:T(128)}) while((s32[]{:T(128)}, bf16[8,512,1024]{2,1,0:T(8,128)(2,1)}, bf16[8,512,256]{2,1,0:T(8,128)(2,1)S(1)}, bf16[256,1024]{1,0:T(8,128)(2,1)S(1)}, s32[]{:T(128)}) %tuple.43), condition=%wide.region_3.0_spmd, body=%wide.region_2.0_spmd.sunk | while | flops 269484032 | bytes 1836101 | solution.py:50
  507.3 1.4 fusion.44
  508.7 1.5 fusion.44
  510.2 1.4 fusion.44
  511.7 1.4 fusion.44
  513.1 1.4 fusion.44
  514.5 1.5 fusion.44
  516.0 1.5 fusion.44
  517.4 1.4 fusion.44
  518.9 4.5 convert_reduce_fusion.1
  523.4 109.9 %all-reduce = (f32[4096]{0:T(1024)S(1)}, f32[4096]{0:T(1024)S(1)}) all-reduce(f32[4096]{0:T(1024)S(1)} %bitcast.60, f32[4096]{0:T(1024)S(1)} %bitcast.61), channel_id=1, replica_groups=mesh['group'=16,'member'=32] {'member'}, use_global_device_ids=true, to_apply=%region_21.22 | all-reduce | flops 8192 | bytes 65536 | tf_op jit(solution)/shard_map/psum | solution.py:79
  633.3 8.2 %fusion.18 = bf16[4096,1024]{1,0:T(8,128)(2,1)S(1)} fusion(bf16[8,512,1024]{2,1,0:T(8,128)(2,1)} %get-tuple-element.50, f32[1024]{0:T(1024)S(1)} %broadcast_divide_fusion.3, f32[4096]{0:T(1024)S(1)} %broadcast_divide_fusion, f32[4096]{0:T(1024)S(1)} %get-tuple-element.68, bf16[8,512,1024]{2,1,0:T(8,128)(2,1)} %get-tuple-element.49), kind=kLoop, calls=%fused_computation.29 | loop fusion | flops 33554432 | bytes 25202688 | tf_op jit(solution)/shard_map/convert_element_type | solution.py:83
  641.5 0.0 copy-start.1
  641.5 3.4 fusion.31
  644.9 0.0 all-reduce.3.cloned.1.call-update
  644.9 141.1 %all-reduce.3.cloned.1.call-done = f32[256,1024]{1,0:T(8,128)} async-done(((f32[256,1024]{1,0:T(8,128)}), f32[256,1024]{1,0:T(8,128)}) %all-reduce.3.cloned.1.call-update) | async-done | bytes 1048592 | tf_op jit(solution)/shard_map/psum | solution.py:87
  786.1 0.0 copy-done.1
  786.1 1.4 fusion.23
  787.5 2.2 fusion.25
  (18 shorter events, 0.1 us)
Async XLA Ops:
  6.5 0.9 copy-start
  6.5 89.5 %all-gather.5.cloned.1.call-start = ((), (), s32[]{:S(2)}) async-start(), calls=%async_computation.1 | async-start | bytes 2162688 | tf_op jit(solution)/shard_map/all_gather | solution.py:58
  9.2 493.8 %all-gather.3.cloned.1.call-start = ((), (), s32[]{:S(2)}) async-start(), calls=%async_computation | async-start | bytes 2162688 | tf_op jit(solution)/shard_map/all_gather | solution.py:59
  11.8 774.3 %all-reduce.3.cloned.1.call-start = ((), (), s32[]{:S(2)}) async-start(), calls=%async_computation.2 | async-start | bytes 2097152 | tf_op jit(solution)/shard_map/psum | solution.py:87
  503.0 4.3 copy-start.2
  641.5 144.6 %copy-start.1 = (bf16[256,1024]{1,0:T(8,128)(2,1)S(1)}, bf16[256,1024]{1,0:T(8,128)(2,1)}, u32[]{:S(2)}) copy-start(bf16[256,1024]{1,0:T(8,128)(2,1)} %param.13) | copy-start | bytes 1572868
Sparse Core Ops, SparseCore 0:
  10.5 85.4 all-gather.4
  99.2 80.8 all-gather.2
  645.1 140.9 all-reduce.2
where the time goes:
time: 797 us; the launch traced here: 796 us
  blocking collectives  463 us (58%)
  waiting for transfers between devices  221 us (28%)
  other arithmetic  53.6 us (7%)
  matrix products  34.3 us (4%)
  between operations  13.3 us (2%)
  local copies, waits for them, and re-layouts  11.4 us (1%)
    psum x3, blocking collectives, shards(): row_mass = lax.psum(local_rows, 'member')  332 us
    psum x1, waiting for transfers between devices, shards(): grad_sum = lax.psum(local_grad, 'group')  141 us
    psum x3, blocking collectives, shards(): col_mass = lax.psum(local_cols, 'group')  131 us
    all_gather x1, waiting for transfers between devices, shards(): lax.all_gather(teach_local, 'member', axis=0, tiled=True)  79.5 us
    dot_general x16, matrix products, exp_scores(): jnp.dot(rows, protos, preferred_element_type=jnp.float32) * scale  30.9 us
  transfers between devices with their start and end apart: 3, of which 2 were waited for; matrix products, arithmetic and copies ran while one was open for 8% of the time, Pallas kernels for 0%

commit v1 on v0

v1 whole, which is shorter than its diff:
```python
import functools

import jax
import jax.numpy as jnp
from jax import lax
from jax.experimental import pallas as pl
from jax.experimental.pallas import tpu as pltpu
from jax.sharding import Mesh
from jax.sharding import PartitionSpec as P

GROUP = ("y", "core")
MEMBER = ("z", "x")
ITERS = 3
LANES = 128
CHUNK = 512
VMEM_LIMIT = 48 * 1024 * 1024

epsilon = 1e-06
teacher_scale = 1.0 / 0.07
student_scale = 1.0 / 0.1
grad_factor = 256.0 / 0.1
NT = (((1,), (1,)), ((), ()))
TN = (((0,), (0,)), ((), ()))
f32 = jnp.float32
bf16 = jnp.bfloat16


def params():
    return pltpu.CompilerParams(vmem_limit_bytes=VMEM_LIMIT)


def cost(flops, transcendentals, nbytes):
    return pl.CostEstimate(flops=flops, transcendentals=transcendentals, bytes_accessed=nbytes)


def whole(shape):
    return pl.BlockSpec(shape, lambda *_: (0,) * len(shape))


def lane_row(block, start, count):
    return jnp.concatenate([block[start + j : start + j + 1, :] for j in range(count)], axis=1)


def split_rows(row):
    high = row.astype(bf16).astype(f32)
    low = row - high
    index = lax.broadcasted_iota(jnp.int32, (16, row.shape[1]), 0)
    return jnp.where(index == 0, high, jnp.where(index == 1, low, 0.0)).astype(bf16)


def rows_kernel(teacher_ref, student_ref, mask_ref, out_ref):
    patches = teacher_ref.shape[0]
    count = mask_ref.shape[1]
    chosen = lax.broadcasted_iota(jnp.int32, (patches, count), 0) == mask_ref[...]
    chosen = chosen.astype(f32).astype(bf16)
    for part, ref in enumerate((teacher_ref, student_ref)):
        rows = lax.dot_general(chosen, ref[...], TN, preferred_element_type=f32)
        square = jnp.sum(rows * rows, axis=1, keepdims=True)
        out_ref[part] = (rows * lax.rsqrt(square + epsilon)).astype(bf16)


def masked_rows(teacher, student, mask):
    count = mask.shape[1]
    return pl.pallas_call(
        rows_kernel,
        out_shape=jax.ShapeDtypeStruct((2, count, teacher.shape[1]), bf16),
        compiler_params=params(),
        name="masked_rows",
    )(teacher, student, mask)


def pack_piece(block, piece, pieces):
    rows, columns = block.shape
    width = columns // pieces
    part = block[:, piece * width : (piece + 1) * width]
    return jnp.concatenate([part[: rows // 2], part[rows // 2 :]], axis=1)


def protos_kernel(pieces, teacher_ref, student_ref, teach_ref, stud_ref, pack_ref):
    for source, out in ((teacher_ref, teach_ref), (student_ref, stud_ref)):
        values = source[...].astype(f32)
        square = jnp.sum(values * values, axis=0, keepdims=True)
        out[...] = (values * lax.rsqrt(square + epsilon)).astype(bf16)
    weight = student_ref[...].astype(f32)
    for piece in range(pieces):
        pack_ref[piece] = pack_piece(weight, piece, pieces)


def prototypes(teacher, student, pieces):
    rows, columns = teacher.shape
    like = jax.ShapeDtypeStruct(teacher.shape, bf16)
    return pl.pallas_call(
        functools.partial(protos_kernel, pieces),
        out_shape=(like, like, jax.ShapeDtypeStruct((pieces, rows // 2, 2 * columns // pieces), f32)),
        compiler_params=params(),
        name="prototypes",
    )(teacher, student)


def codes_kernel(rows_ref, protos_ref, codes_ref, cols_ref, total_ref):
    step = pl.program_id(0)

    @pl.when(step == 0)
    def _():
        total_ref[...] = jnp.zeros_like(total_ref)

    scores = jnp.dot(rows_ref[...], protos_ref[...], preferred_element_type=f32)
    codes = jnp.exp(scores * teacher_scale)
    codes_ref[...] = codes.astype(bf16)
    total_ref[...] += jnp.sum(codes, axis=0, keepdims=True)

    @pl.when(step == pl.num_programs(0) - 1)
    def _():
        spread_cols(total_ref[...], cols_ref)


def spread_cols(total, cols_ref):
    for j in range(cols_ref.shape[1]):
        part = total[:, j * LANES : (j + 1) * LANES]
        cols_ref[:, j, :] = jnp.broadcast_to(part, (cols_ref.shape[0], LANES))


def first_codes(rows, protos, groups):
    count, width = rows.shape
    columns = protos.shape[1]
    tiles = columns // LANES
    return pl.pallas_call(
        codes_kernel,
        grid=(count // CHUNK,),
        in_specs=[pl.BlockSpec((CHUNK, width), lambda i: (i, 0)), whole(protos.shape)],
        out_specs=(pl.BlockSpec((CHUNK, columns), lambda i: (i, 0)), whole((groups, tiles, LANES))),
        out_shape=(
            jax.ShapeDtypeStruct((count, columns), bf16),
            jax.ShapeDtypeStruct((groups, tiles, LANES), f32),
        ),
        scratch_shapes=[pltpu.VMEM((1, columns), f32)],
        compiler_params=params(),
        cost_estimate=cost(2 * count * width * columns, count * columns, 2 * count * columns),
        name="first_codes",
    )(rows, protos)


def row_pass_kernel(extra, *refs):
    recv_ref, codes_ref = refs[:2]
    out_ref, scale_ref = refs[-2:]
    step = pl.program_id(0)
    tiles = recv_ref.shape[1]

    @pl.when(step == 0)
    def _():
        mass = jnp.sum(recv_ref[...], axis=0)
        scale_ref[...] = split_rows(lane_row(1.0 / mass, 0, tiles))
        if extra:
            out_ref[:, 1, :, :] = jnp.broadcast_to(refs[2][...][None], out_ref.shape[:1] + out_ref.shape[2:])

    sums = lax.dot_general(scale_ref[...], codes_ref[...], NT, preferred_element_type=f32)
    sums = sums[0:1] + sums[1:2]
    lines = CHUNK // LANES
    block = jnp.concatenate([sums[:, j * LANES : (j + 1) * LANES] for j in range(lines)], axis=0)
    block = jnp.broadcast_to(block[None], (out_ref.shape[0], lines, LANES))
    out_ref[:, 0, pl.ds(step * lines, lines), :] = block


def row_pass(recv, codes, members, norm=None):
    count, columns = codes.shape
    lines = count // LANES
    extra = norm is not None
    parts = 2 if extra else 1
    shape = (members, parts, lines, LANES)
    return pl.pallas_call(
        functools.partial(row_pass_kernel, extra),
        grid=(count // CHUNK,),
        in_specs=[whole(recv.shape), pl.BlockSpec((CHUNK, columns), lambda i: (i, 0))]
        + ([whole(norm.shape)] if extra else []),
        out_specs=whole(shape),
        out_shape=jax.ShapeDtypeStruct(shape, f32),
        scratch_shapes=[pltpu.VMEM((16, columns), bf16)],
        compiler_params=params(),
        cost_estimate=cost(32 * count * columns, 0, 2 * count * columns),
        name="row_pass",
    )(recv, codes, *((norm,) if extra else ()))


def col_pass_kernel(recv_ref, codes_ref, cols_ref, scale_ref, total_ref):
    step = pl.program_id(0)
    lines = CHUNK // LANES

    @pl.when(step == 0)
    def _():
        scale_ref[...] = 1.0 / jnp.sum(recv_ref[:, 0], axis=0)
        total_ref[...] = jnp.zeros_like(total_ref)

    scale = split_rows(lane_row(scale_ref[pl.ds(step * lines, lines), :], 0, lines))
    total_ref[...] += jnp.dot(scale, codes_ref[...], preferred_element_type=f32)

    @pl.when(step == pl.num_programs(0) - 1)
    def _():
        spread_cols(total_ref[0:1] + total_ref[1:2], cols_ref)


def col_pass(recv, codes, groups):
    count, columns = codes.shape
    tiles = columns // LANES
    return pl.pallas_call(
        col_pass_kernel,
        grid=(count // CHUNK,),
        in_specs=[whole(recv.shape), pl.BlockSpec((CHUNK, columns), lambda i: (i, 0))],
        out_specs=whole((groups, tiles, LANES)),
        out_shape=jax.ShapeDtypeStruct((groups, tiles, LANES), f32),
        scratch_shapes=[pltpu.VMEM((count // LANES, LANES), f32), pltpu.VMEM((16, columns), f32)],
        compiler_params=params(),
        cost_estimate=cost(32 * count * columns, 0, 2 * count * columns),
        name="col_pass",
    )(recv, codes)


def student_kernel(rows_ref, protos_ref, expo_ref, norm_ref, turned_ref):
    step = pl.program_id(0)
    lines = CHUNK // LANES
    rows = rows_ref[...]
    scores = jnp.dot(rows, protos_ref[...], preferred_element_type=f32)
    expo = jnp.exp(scores * student_scale).astype(bf16)
    expo_ref[...] = expo
    sums = lax.dot_general(jnp.ones((16, expo.shape[1]), bf16), expo, NT, preferred_element_type=f32)[0:1]
    for j in range(lines):
        norm_ref[pl.ds(step * lines + j, 1), :] = sums[:, j * LANES : (j + 1) * LANES]
    turned_ref[...] = rows.T


def student_expo(rows, protos):
    count, width = rows.shape
    columns = protos.shape[1]
    return pl.pallas_call(
        student_kernel,
        grid=(count // CHUNK,),
        in_specs=[pl.BlockSpec((CHUNK, width), lambda i: (i, 0)), whole(protos.shape)],
        out_specs=(
            pl.BlockSpec((CHUNK, columns), lambda i: (i, 0)),
            whole((count // LANES, LANES)),
            pl.BlockSpec((width, CHUNK), lambda i: (0, i)),
        ),
        out_shape=(
            jax.ShapeDtypeStruct((count, columns), bf16),
            jax.ShapeDtypeStruct((count // LANES, LANES), f32),
            jax.ShapeDtypeStruct((width, count), bf16),
        ),
        compiler_params=params(),
        cost_estimate=cost(2 * count * width * columns, count * columns, 2 * count * columns),
        name="student_expo",
    )(rows, protos)


def grad_kernel(recv_ref, cols_ref, turned_ref, codes_ref, expo_ref, out_ref, scale_ref, teach_ref, stud_ref):
    step = pl.program_id(0)
    lines = CHUNK // LANES

    @pl.when(step == 0)
    def _():
        scale_ref[...] = 1.0 / jnp.sum(recv_ref[...], axis=0)
        teach_ref[...] = jnp.zeros_like(teach_ref)
        stud_ref[...] = jnp.zeros_like(stud_ref)

    turned = turned_ref[...].astype(f32)
    for part, (source, total) in enumerate(((codes_ref, teach_ref), (expo_ref, stud_ref))):
        scale = lane_row(scale_ref[part, pl.ds(step * lines, lines), :], 0, lines)
        total[...] += jnp.dot((turned * scale).astype(bf16), source[...], preferred_element_type=f32)

    @pl.when(step == pl.num_programs(0) - 1)
    def _():
        mass = jnp.sum(cols_ref[...], axis=0)
        col_scale = lane_row(1.0 / mass, 0, cols_ref.shape[1])
        grad = grad_factor * (stud_ref[...] - teach_ref[...] * col_scale)
        for piece in range(out_ref.shape[0]):
            out_ref[piece] = pack_piece(grad, piece, out_ref.shape[0]).astype(bf16)


def grad_pieces(recv, cols, turned, codes, expo):
    count, columns = codes.shape
    width = turned.shape[0]
    pieces = cols.shape[0]
    shape = (pieces, width // 2, 2 * columns // pieces)
    return pl.pallas_call(
        grad_kernel,
        grid=(count // CHUNK,),
        in_specs=[
            whole(recv.shape),
            whole(cols.shape),
            pl.BlockSpec((width, CHUNK), lambda i: (0, i)),
            pl.BlockSpec((CHUNK, columns), lambda i: (i, 0)),
            pl.BlockSpec((CHUNK, columns), lambda i: (i, 0)),
        ],
        out_specs=whole(shape),
        out_shape=jax.ShapeDtypeStruct(shape, bf16),
        scratch_shapes=[
            pltpu.VMEM(recv.shape[1:], f32),
            pltpu.VMEM((width, columns), f32),
            pltpu.VMEM((width, columns), f32),
        ],
        compiler_params=params(),
        cost_estimate=cost(4 * count * width * columns, 0, 4 * count * columns),
        name="grad_pieces",
    )(recv, cols, turned, codes, expo)


def back_kernel(recv_ref, weight_ref, out_ref):
    grad = jnp.sum(recv_ref[...].astype(f32), axis=0)
    weight = weight_ref[...]
    half = weight.shape[1] // 2

    def column_sum(values):
        total = jnp.sum(values, axis=0, keepdims=True)
        return total + jnp.concatenate([total[:, half:], total[:, :half]], axis=1)

    inverse = lax.rsqrt(column_sum(weight * weight) + epsilon)
    along = column_sum(grad * weight)
    out_ref[...] = (grad * inverse - weight * (inverse * inverse * inverse * along)).astype(bf16)


def weight_back(recv, weight):
    return pl.pallas_call(
        back_kernel,
        out_shape=jax.ShapeDtypeStruct(weight.shape, bf16),
        compiler_params=params(),
        name="weight_back",
    )(recv, weight)


def join_kernel(pieces_ref, out_ref):
    pieces, rows, lanes = pieces_ref.shape
    half = lanes // 2
    for pair in range(pieces // 2):
        left, right = pieces_ref[2 * pair], pieces_ref[2 * pair + 1]
        columns = pl.ds(pair * lanes, lanes)
        out_ref[:rows, columns] = jnp.concatenate([left[:, :half], right[:, :half]], axis=1)
        out_ref[rows:, columns] = jnp.concatenate([left[:, half:], right[:, half:]], axis=1)


def join_pieces(pieces):
    count, rows, lanes = pieces.shape
    return pl.pallas_call(
        join_kernel,
        out_shape=jax.ShapeDtypeStruct((2 * rows, count * lanes // 2), pieces.dtype),
        compiler_params=params(),
        name="join_pieces",
    )(pieces)


def exchange(values, axes):
    return lax.all_to_all(values, axes, 0, 0, tiled=True)


def shards(groups, members, teacher_patches, student_patches, mask_index, teacher_weight, student_weight):
    local = masked_rows(teacher_patches, student_patches, mask_index.reshape(1, -1))
    count, width = local.shape[1:]
    along_x = lax.all_gather(local, "x", axis=1, tiled=True)
    teach_rows = lax.all_gather(along_x[0], "z", axis=0, tiled=True)
    stud_x, teach_rows = lax.optimization_barrier((along_x[1], teach_rows))
    stud_rows = lax.all_gather(stud_x, "z", axis=0, tiled=True)
    teach_protos, stud_protos, packed = prototypes(teacher_weight, student_weight, groups)
    own_weight = lax.dynamic_index_in_dim(packed, lax.axis_index(GROUP), 0, keepdims=False)

    codes, cols = first_codes(teach_rows, teach_protos, groups)
    for sweep in range(ITERS):
        cols = exchange(cols, GROUP)
        if sweep < ITERS - 1:
            rows = exchange(row_pass(cols, codes, members), MEMBER)
            cols = col_pass(rows, codes, groups)
    expo, norm, turned = student_expo(stud_rows, stud_protos)
    rows = exchange(row_pass(cols, codes, members, norm), MEMBER)
    pieces = exchange(grad_pieces(rows, cols, turned, codes, expo), GROUP)
    return join_pieces(lax.all_gather(weight_back(pieces, own_weight), GROUP, axis=0))


def solution(mesh):
    groups, members = mesh.devices.shape
    split = Mesh(mesh.devices.reshape(8, 2, 8, 4), GROUP + MEMBER)
    rows = P(GROUP + MEMBER, None)
    columns = P(None, MEMBER)
    return jax.shard_map(
        functools.partial(shards, groups, members),
        mesh=split,
        in_specs=(rows, rows, P(GROUP + MEMBER), columns, columns),
        out_specs=columns,
        check_vma=False,
    )
```

time: 797 us -> 302 us (0.38)
  blocking collectives: 463 us -> 137 us
  waiting for transfers between devices: 221 us -> 65.6 us
  Pallas kernels: 0 us -> 62.4 us
  other arithmetic: 53.6 us -> 0 us
  matrix products: 34.3 us -> 0 us
  starting transfers between devices: 0.09 us -> 14.2 us
    psum x6 -> x0, blocking collectives: 463 us -> none  [the longest x3 332 us: shards(): row_mass = lax.psum(local_rows, 'member')]
    psum x1 -> x0, waiting for transfers between devices: 141 us -> none  [shards(): grad_sum = lax.psum(local_grad, 'group')]
    all_to_all x0 -> x5, blocking collectives: none -> 110 us  [exchange(): return lax.all_to_all(values, axes, 0, 0, tiled=True)]
    pallas_call x0 -> x12, Pallas kernels: none -> 62.4 us  [the longest x3 21.7 us: row_pass(): pl.pallas_call(functools.partial(row_pass_kernel, extra), grid=(count //...]
    reduce_sum x12 -> x0, other arithmetic: 38.8 us -> none  [the longest x3 15.4 us: shards(): local_rows = jnp.sum(codes.astype(jnp.float32) * col_scale[None, :], axis=1)]
    dot_general x17 -> x0, matrix products: 34.3 us -> none  [the longest x16 30.9 us: exp_scores(): jnp.dot(rows, protos, preferred_element_type=jnp.float32) * scale]
    all_gather x2, waiting for transfers between devices: 79.6 us -> 48.3 us  [the longest x1 48.2 us: shards(): teach_rows = lax.all_gather(along_x[0], 'z', axis=0, tiled=True)]
    all_gather x0 -> x2, blocking collectives: none -> 27 us  [the longest x1 15.9 us: shards(): lax.all_gather(weight_back(pieces, own_weight), GROUP, axis=0)]
  transfers between devices with their start and end apart: 3 -> 4, of which waited for: 2 -> 2; matrix products, arithmetic and copies ran while one was open for 8% -> 0% of each run, Pallas kernels for 0% -> 14%
where the time goes in v1:
time: 302 us; the launch traced here: 301 us
  blocking collectives  137 us (45%)
  waiting for transfers between devices  65.6 us (22%)
  Pallas kernels  62.4 us (21%)
  starting transfers between devices  14.2 us (5%)
  between operations  13.5 us (4%)
  local copies, waits for them, and re-layouts  8.4 us (3%)
    all_to_all x5, blocking collectives, exchange(): return lax.all_to_all(values, axes, 0, 0, tiled=True)  110 us
    all_gather x1, waiting for transfers between devices, shards(): teach_rows = lax.all_gather(along_x[0], 'z', axis=0, tiled=True)  48.2 us
    pallas_call x3, Pallas kernels, row_pass(): pl.pallas_call(functools.partial(row_pass_kernel, extra), grid=(count //...  21.7 us
    all_to_all x2, waiting for transfers between devices, exchange(): return lax.all_to_all(values, axes, 0, 0, tiled=True)  17.3 us
    all_gather x1, blocking collectives, shards(): lax.all_gather(weight_back(pieces, own_weight), GROUP, axis=0)  15.9 us
    all_to_all x2, starting transfers between devices, exchange(): return lax.all_to_all(values, axes, 0, 0, tiled=True)  14.2 us
    pallas_call x2, Pallas kernels, col_pass(): pl.pallas_call(col_pass_kernel, grid=(count // CHUNK,), in_specs=[whole(r...  13.7 us
    pallas_call x1, Pallas kernels, grad_pieces(): pl.pallas_call(grad_kernel, grid=(count // CHUNK,), in_specs=[whole(recv....  11.7 us
  transfers between devices with their start and end apart: 4, of which 2 were waited for; matrix products, arithmetic and copies ran while one was open for 0% of the time, Pallas kernels for 14%

profile of v1, /device:TPU:1, one launch (start us, length us, event | category | flops | bytes accessed | tf_op | source)
XLA Modules:
  0.0 301.1 jit_solution(3759175974503440036)
XLA Ops:
  6.5 0.0 copy-start.1
  6.5 0.0 copy-start
  6.5 0.0 all-gather.7.cloned.1.call-start
  6.5 0.0 copy-start.2
  6.5 1.0 copy-done.2
  7.5 0.0 copy-start.3
  7.5 0.9 copy-done.3
  8.4 0.0 copy-start.4
  8.4 0.7 copy-done.4
  9.1 0.3 masked_rows.1
  9.4 11.1 %all_gather.15 = bf16[2,512,256]{2,1,0:T(8,128)(2,1)S(1)} all-gather(bf16[2,128,256]{2,1,0:T(8,128)(2,1)S(1)} %masked_rows.1), channel_id=1, replica_groups=mesh['y'=8,'core'=2,'z'=8,'x'=4] {'x'}, dimensions={1}, use_global_device_ids=true | all-gather | bytes 655360 | tf_op jit(solution)/shard_map/all_gather | solution.py:355
  20.5 0.8 fusion
  21.3 0.0 all-gather.7.cloned.1.call-update
  21.3 0.0 all-gather.5.cloned.1.call-start
  21.4 48.2 %all-gather.7.cloned.1.call-done = bf16[1,4096,256]{2,1,0:T(8,128)(2,1)} async-done(((bf16[1,512,256]{2,1,0:T(8,128)(2,1)}), bf16[1,4096,256]{2,1,0:T(8,128)(2,1)}) %all-gather.7.cloned.1.call-update) | async-done | bytes 2097168 | tf_op jit(solution)/shard_map/all_gather | solution.py:356
  69.6 0.0 all-gather.5.cloned.1.call-update
  69.7 0.0 copy-done.1
  69.7 0.0 copy-done
  69.7 0.5 prototypes.1
  70.2 0.0 copy-start.7
  70.2 0.8 copy-done.7
  71.0 0.0 copy-start.6
  71.0 1.6 copy-done.6
  72.6 6.6 %first_codes.1 = (bf16[4096,1024]{1,0:T(8,128)(2,1)}, f32[16,8,128]{2,1,0:T(8,128)S(1)}) custom-call(bf16[4096,256]{1,0:T(8,128)(2,1)S(1)} %bitcast.9, bf16[256,1024]{1,0:T(8,128)(2,1)S(1)} %get-tuple-element.16.protos_ref), custom_call_target="tpu_custom_call" | custom-call | flops 2147483648 | bytes 8388608 | tf_op jit(solution)/shard_map/first_codes/pallas_call | solution.py:127
  79.2 19.1 %all_to_all.35.refs_0_ = f32[16,8,128]{2,1,0:T(8,128)S(1)} all-to-all(f32[16,8,128]{2,1,0:T(8,128)S(1)} %get-tuple-element.17), channel_id=1, replica_groups=mesh['y'=8,'core'=2,'z'=8,'x'=4] {'y','core'}, dimensions={0} | all-to-all | bytes 131072 | tf_op jit(solution)/shard_map/all_to_all | solution.py:349
  98.3 7.3 %row_pass.3 = f32[32,1,32,128]{3,2,1,0:T(8,128)S(1)} custom-call(f32[16,8,128]{2,1,0:T(8,128)S(1)} %all_to_all.35.refs_0_, bf16[4096,1024]{1,0:T(8,128)(2,1)} %get-tuple-element.18.refs_1_.codes_ref), custom_call_target="tpu_custom_call" | custom-call | flops 134217728 | bytes 8388608 | tf_op jit(solution)/shard_map/row_pass/pallas_call | solution.py:170
  105.6 24.1 %all_to_all.36.recv_ref = f32[32,1,32,128]{3,2,1,0:T(8,128)S(1)} all-to-all(f32[32,1,32,128]{3,2,1,0:T(8,128)S(1)} %row_pass.3), channel_id=1, replica_groups=mesh['y'=8,'core'=2,'z'=8,'x'=4] {'z','x'}, dimensions={0} | all-to-all | bytes 1048576 | tf_op jit(solution)/shard_map/all_to_all | solution.py:349
  129.7 6.6 %col_pass.2 = f32[16,8,128]{2,1,0:T(8,128)S(1)} custom-call(f32[32,1,32,128]{3,2,1,0:T(8,128)S(1)} %all_to_all.36.recv_ref, bf16[4096,1024]{1,0:T(8,128)(2,1)} %get-tuple-element.18.refs_1_.codes_ref), custom_call_target="tpu_custom_call" | custom-call | flops 134217728 | bytes 8388608 | tf_op jit(solution)/shard_map/col_pass/pallas_call | solution.py:204
  136.3 14.2 %all_to_all.37.refs_0_ = f32[16,8,128]{2,1,0:T(8,128)S(1)} all-to-all(f32[16,8,128]{2,1,0:T(8,128)S(1)} %col_pass.2), channel_id=1, replica_groups=mesh['y'=8,'core'=2,'z'=8,'x'=4] {'y','core'}, dimensions={0} | all-to-all | bytes 131072 | tf_op jit(solution)/shard_map/all_to_all | solution.py:349
  150.5 7.2 %row_pass.4 = f32[32,1,32,128]{3,2,1,0:T(8,128)S(1)} custom-call(f32[16,8,128]{2,1,0:T(8,128)S(1)} %all_to_all.37.refs_0_, bf16[4096,1024]{1,0:T(8,128)(2,1)} %get-tuple-element.18.refs_1_.codes_ref), custom_call_target="tpu_custom_call" | custom-call | flops 134217728 | bytes 8388608 | tf_op jit(solution)/shard_map/row_pass/pallas_call | solution.py:170
  157.7 21.5 %all_to_all.38.recv_ref = f32[32,1,32,128]{3,2,1,0:T(8,128)S(1)} all-to-all(f32[32,1,32,128]{3,2,1,0:T(8,128)S(1)} %row_pass.4), channel_id=1, replica_groups=mesh['y'=8,'core'=2,'z'=8,'x'=4] {'z','x'}, dimensions={0} | all-to-all | bytes 1048576 | tf_op jit(solution)/shard_map/all_to_all | solution.py:349
  179.2 7.2 %col_pass.3 = f32[16,8,128]{2,1,0:T(8,128)} custom-call(f32[32,1,32,128]{3,2,1,0:T(8,128)S(1)} %all_to_all.38.recv_ref, bf16[4096,1024]{1,0:T(8,128)(2,1)} %get-tuple-element.18.refs_1_.codes_ref), custom_call_target="tpu_custom_call" | custom-call | flops 134217728 | bytes 8388608 | tf_op jit(solution)/shard_map/col_pass/pallas_call | solution.py:204
  186.3 5.2 %all-to-all-start.4 = ((f32[16,8,128]{2,1,0:T(8,128)}), f32[16,8,128]{2,1,0:T(8,128)S(1)}, u32[]{:S(2)}, u32[]{:S(2)}) async-start(f32[16,8,128]{2,1,0:T(8,128)} %col_pass.3), calls=%async_computation.4 | async-start | bytes 131072 | tf_op jit(solution)/shard_map/all_to_all | solution.py:349
  191.6 0.0 all-gather.5.cloned.1.call-done.rows_ref
  191.6 0.0 copy-start.5
  191.6 1.6 copy-done.5
  193.2 0.0 copy-start.8
  193.2 1.0 copy-done.8
  194.2 6.6 %student_expo.1 = (bf16[4096,1024]{1,0:T(8,128)(2,1)}, f32[32,128]{1,0:T(8,128)S(1)}, bf16[256,4096]{1,0:T(8,128)(2,1)S(1)}) custom-call(bf16[4096,256]{1,0:T(8,128)(2,1)S(1)} %copy-done.5, bf16[256,1024]{1,0:T(8,128)(2,1)S(1)} %copy-done.8), custom_call_target="tpu_custom_call" | custom-call | flops 2147483648 | bytes 8388608 | tf_op jit(solution)/shard_map/student_expo/pallas_call | solution.py:233
  200.8 0.0 all-to-all-done.4.refs_0_.cols_ref
  200.8 7.2 %row_pass.5 = f32[32,2,32,128]{3,2,1,0:T(8,128)S(1)} custom-call(f32[16,8,128]{2,1,0:T(8,128)S(1)} %all-to-all-done.4.refs_0_.cols_ref, bf16[4096,1024]{1,0:T(8,128)(2,1)} %get-tuple-element.18.refs_1_.codes_ref, f32[32,128]{1,0:T(8,128)S(1)} %get-tuple-element.21.refs_2_), custom_call_target="tpu_custom_call" | custom-call | flops 134217728 | bytes 8388608 | tf_op jit(solution)/shard_map/row_pass/pallas_call | solution.py:170
  208.1 31.1 %all_to_all.39.recv_ref = f32[32,2,32,128]{3,2,1,0:T(8,128)S(1)} all-to-all(f32[32,2,32,128]{3,2,1,0:T(8,128)S(1)} %row_pass.5), channel_id=1, replica_groups=mesh['y'=8,'core'=2,'z'=8,'x'=4] {'z','x'}, dimensions={0} | all-to-all | bytes 2097152 | tf_op jit(solution)/shard_map/all_to_all | solution.py:349
  239.2 11.7 %grad_pieces.1 = bf16[16,128,128]{2,1,0:T(8,128)(2,1)} custom-call(f32[32,2,32,128]{3,2,1,0:T(8,128)S(1)} %all_to_all.39.recv_ref, f32[16,8,128]{2,1,0:T(8,128)S(1)} %all-to-all-done.4.refs_0_.cols_ref, bf16[256,4096]{1,0:T(8,128)(2,1)S(1)} %get-tuple-element.22.turned_ref, bf16[4096,1024]{1,0:T(8,128)(2,1)} %get-tuple-element.18.refs_1_.codes_ref, ...), custom_call_target="tpu_custom_call" | custom-call | flops 4294967296 | bytes 16777216 | tf_op jit(solution)/shard_map/grad_pieces/pallas_call | solution.py:282
  250.9 9.0 %all-to-all-start.6 = ((bf16[16,128,128]{2,1,0:T(8,128)(2,1)}), bf16[16,128,128]{2,1,0:T(8,128)(2,1)S(1)}, u32[]{:S(2)}, u32[]{:S(2)}) async-start(bf16[16,128,128]{2,1,0:T(8,128)(2,1)} %grad_pieces.1), calls=%async_computation.6 | async-start | bytes 1048576 | tf_op jit(solution)/shard_map/all_to_all | solution.py:349
  259.9 17.3 %all-to-all-done.6.recv_ref = bf16[16,128,128]{2,1,0:T(8,128)(2,1)S(1)} async-done(((bf16[16,128,128]{2,1,0:T(8,128)(2,1)}), bf16[16,128,128]{2,1,0:T(8,128)(2,1)S(1)}, u32[]{:S(2)}, u32[]{:S(2)}) %all-to-all-start.6) | async-done | bytes 524320 | tf_op jit(solution)/shard_map/all_to_all | solution.py:349
  277.2 0.2 weight_back.1
  277.4 15.9 %all-gather.1 = bf16[2048,128]{1,0:T(8,128)(2,1)S(1)} all-gather(bf16[128,128]{1,0:T(8,128)(2,1)S(1)} %weight_back.1), channel_id=3, replica_groups=mesh['y'=8,'core'=2,'z'=8,'x'=4] {'y','core'}, dimensions={0}, use_global_device_ids=true | all-gather | bytes 557056 | tf_op jit(solution)/shard_map/all_gather | solution.py:371
  293.3 1.0 join_pieces.1
  (1 shorter events, 0.0 us)
Async XLA Ops:
  6.5 63.1 %copy-start.1 = (bf16[256,1024]{1,0:T(8,128)(2,1)S(1)}, bf16[256,1024]{1,0:T(8,128)(2,1)}, u32[]{:S(2)}) copy-start(bf16[256,1024]{1,0:T(8,128)(2,1)} %student_ref.3) | copy-start | bytes 1572868
  6.5 63.1 %copy-start = (bf16[256,1024]{1,0:T(8,128)(2,1)S(1)}, bf16[256,1024]{1,0:T(8,128)(2,1)}, u32[]{:S(2)}) copy-start(bf16[256,1024]{1,0:T(8,128)(2,1)} %teacher_ref.3) | copy-start | bytes 1572868
  6.5 63.1 %all-gather.7.cloned.1.call-start = ((), (), s32[]{:S(2)}) async-start(), calls=%async_computation.8 | async-start | bytes 2359296 | tf_op jit(solution)/shard_map/all_gather | solution.py:356
  6.5 1.0 copy-start.2
  7.5 0.9 copy-start.3
  8.4 0.7 copy-start.4
  21.3 170.2 %all-gather.5.cloned.1.call-start = ((), (), s32[]{:S(2)}) async-start(), calls=%async_computation.7 | async-start | bytes 2359296 | tf_op jit(solution)/shard_map/all_gather | solution.py:358
  70.2 0.8 copy-start.7
  71.0 1.6 copy-start.6
  186.3 14.5 %all-to-all-start.4 = ((f32[16,8,128]{2,1,0:T(8,128)}), f32[16,8,128]{2,1,0:T(8,128)S(1)}, u32[]{:S(2)}, u32[]{:S(2)}) async-start(f32[16,8,128]{2,1,0:T(8,128)} %col_pass.3), calls=%async_computation.4 | async-start | bytes 131072 | tf_op jit(solution)/shard_map/all_to_all | solution.py:349
  191.6 1.6 copy-start.5
  193.2 1.0 copy-start.8
  250.9 26.3 %all-to-all-start.6 = ((bf16[16,128,128]{2,1,0:T(8,128)(2,1)}), bf16[16,128,128]{2,1,0:T(8,128)(2,1)S(1)}, u32[]{:S(2)}, u32[]{:S(2)}) async-start(bf16[16,128,128]{2,1,0:T(8,128)(2,1)} %grad_pieces.1), calls=%async_computation.6 | async-start | bytes 1048576 | tf_op jit(solution)/shard_map/all_to_all | solution.py:349
Sparse Core Ops, SparseCore 0:
  21.5 48.1 all-gather.6
  71.7 42.7 all-gather.4

commit v2 on v1

v2 whole, which is shorter than its diff:
```python
import functools
import math

import jax
import jax.numpy as jnp
from jax import lax
from jax.experimental import pallas as pl
from jax.experimental.pallas import tpu as pltpu
from jax.sharding import Mesh
from jax.sharding import PartitionSpec as P

GROUP = ("y", "core")
MEMBER = ("z", "x")
LANES = 128
CHUNK = 1024
VMEM_LIMIT = 28 * 1024 * 1024
LOG2E = math.log2(math.e)
IN_VMEM = pl.BlockSpec(memory_space=pltpu.VMEM)
IN_HBM = pl.BlockSpec(memory_space=pltpu.HBM)

epsilon = 1e-06
teacher_scale = 1.0 / 0.07
student_scale = 1.0 / 0.1
grad_factor = 256.0 / 0.1
NT = (((1,), (1,)), ((), ()))
TN = (((0,), (0,)), ((), ()))
f32 = jnp.float32
bf16 = jnp.bfloat16


def params():
    return pltpu.CompilerParams(vmem_limit_bytes=VMEM_LIMIT)


def cost(flops, transcendentals, nbytes):
    return pl.CostEstimate(flops=flops, transcendentals=transcendentals, bytes_accessed=nbytes)


def lane_row(block, start, count):
    return jnp.concatenate([block[start + j : start + j + 1, :] for j in range(count)], axis=1)


def rows_kernel(teacher_ref, student_ref, mask_ref, out_ref):
    patches = teacher_ref.shape[0]
    count = mask_ref.shape[1]
    chosen = lax.broadcasted_iota(jnp.int32, (patches, count), 0) == mask_ref[...]
    chosen = chosen.astype(f32).astype(bf16)
    for part, ref in enumerate((teacher_ref, student_ref)):
        rows = lax.dot_general(chosen, ref[...], TN, preferred_element_type=f32)
        square = jnp.sum(rows * rows, axis=1, keepdims=True)
        out_ref[part] = (rows * lax.rsqrt(square + epsilon)).astype(bf16)


def masked_rows(teacher, student, mask):
    count = mask.shape[1]
    return pl.pallas_call(
        rows_kernel,
        out_shape=jax.ShapeDtypeStruct((2, count, teacher.shape[1]), bf16),
        compiler_params=params(),
        name="masked_rows",
    )(teacher, student, mask)


def pack_piece(block, piece, pieces):
    rows, columns = block.shape
    width = columns // pieces
    part = block[:, piece * width : (piece + 1) * width]
    return jnp.concatenate([part[: rows // 2], part[rows // 2 :]], axis=1)


def protos_kernel(pieces, teacher_ref, student_ref, teach_ref, stud_ref, pack_ref):
    for source, out in ((teacher_ref, teach_ref), (student_ref, stud_ref)):
        values = source[...].astype(f32)
        square = jnp.sum(values * values, axis=0, keepdims=True)
        out[...] = (values * lax.rsqrt(square + epsilon)).astype(bf16)
    weight = student_ref[...].astype(f32)
    for piece in range(pieces):
        pack_ref[piece] = pack_piece(weight, piece, pieces)


def prototypes(teacher, student, pieces):
    rows, columns = teacher.shape
    like = jax.ShapeDtypeStruct(teacher.shape, bf16)
    return pl.pallas_call(
        functools.partial(protos_kernel, pieces),
        out_shape=(like, like, jax.ShapeDtypeStruct((pieces, rows // 2, 2 * columns // pieces), f32)),
        compiler_params=params(),
        name="prototypes",
    )(teacher, student)


def spread_cols(total, cols_ref):
    for j in range(cols_ref.shape[1]):
        part = total[:, j * LANES : (j + 1) * LANES]
        cols_ref[:, j, :] = jnp.broadcast_to(part, (cols_ref.shape[0], LANES))


def fetch(source, target, sem):
    copy = pltpu.make_async_copy(source, target, sem)
    copy.start()
    copy.wait()


def codes_kernel(rows_ref, protos_ref, codes_ref, cols_ref, held_ref, sem):
    fetch(rows_ref, held_ref, sem)
    scores = jnp.dot(held_ref[...], protos_ref[...], preferred_element_type=f32)
    codes = jnp.exp2(scores * (teacher_scale * LOG2E))
    codes_ref[...] = codes.astype(bf16)
    spread_cols(jnp.sum(codes, axis=0, keepdims=True), cols_ref)


def first_codes(rows, protos, groups):
    count, width = rows.shape
    columns = protos.shape[1]
    return pl.pallas_call(
        codes_kernel,
        in_specs=[IN_HBM, IN_VMEM],
        out_specs=(IN_VMEM, IN_VMEM),
        out_shape=(
            pltpu.VMEM((count, columns), bf16),
            jax.ShapeDtypeStruct((groups, columns // LANES, LANES), f32),
        ),
        scratch_shapes=[pltpu.VMEM((count, width), bf16), pltpu.SemaphoreType.DMA],
        compiler_params=params(),
        cost_estimate=cost(2 * count * width * columns, count * columns, 2 * count * columns),
        name="first_codes",
    )(rows, protos)


def sum_lanes(block):
    ones = jnp.ones((16, LANES), bf16)
    sums = lax.dot_general(ones, block.astype(bf16), NT, preferred_element_type=f32)[0:1]
    lines = block.shape[0] // LANES
    return jnp.concatenate([sums[:, j * LANES : (j + 1) * LANES] for j in range(lines)], axis=0)


def row_pass_kernel(extra, *refs):
    recv_ref, codes_ref, out_ref = refs[0], refs[1], refs[-1]
    tiles = recv_ref.shape[1]
    lines = CHUNK // LANES
    scale = lane_row(1.0 / jnp.sum(recv_ref[...], axis=0), 0, tiles)
    for i in range(codes_ref.shape[0] // CHUNK):
        part = None
        for j in range(tiles):
            columns = slice(j * LANES, (j + 1) * LANES)
            term = codes_ref[i * CHUNK : (i + 1) * CHUNK, columns].astype(f32) * scale[:, columns]
            part = term if part is None else part + term
        block = jnp.broadcast_to(sum_lanes(part)[None], (out_ref.shape[0], lines, LANES))
        out_ref[:, 0, i * lines : (i + 1) * lines, :] = block.astype(out_ref.dtype)
    if extra:
        norm = refs[2][...]
        out_ref[:, 1, :, :] = jnp.broadcast_to(norm[None], out_ref.shape[:1] + norm.shape).astype(out_ref.dtype)


def row_pass(recv, codes, members, norm=None):
    count, columns = codes.shape
    extra = () if norm is None else (norm,)
    shape = (members, 1 + len(extra), count // LANES, LANES)
    return pl.pallas_call(
        functools.partial(row_pass_kernel, bool(extra)),
        in_specs=[IN_VMEM] * (2 + len(extra)),
        out_specs=IN_VMEM,
        out_shape=jax.ShapeDtypeStruct(shape, bf16),
        compiler_params=params(),
        cost_estimate=cost(2 * count * columns, 0, 2 * count * columns),
        name="row_pass",
    )(recv, codes, *extra)


def col_pass_kernel(recv_ref, codes_ref, cols_ref):
    count, columns = codes_ref.shape
    lines = CHUNK // LANES
    scale = 1.0 / jnp.sum(recv_ref[:, 0].astype(f32), axis=0)
    ones = jnp.ones((16, LANES), bf16)
    first = lax.broadcasted_iota(jnp.int32, (16, CHUNK), 0) == 0
    total = jnp.zeros((16, columns), f32)
    for i in range(count // CHUNK):
        row = jnp.where(first, lane_row(scale, i * lines, lines), 0.0).astype(bf16)
        spread = lax.dot_general(row, ones, TN, preferred_element_type=f32).astype(bf16)
        for g in range(lines):
            parts = []
            for j in range(columns // LANES):
                part = None
                for q in range(LANES // 16):
                    at = g * LANES + q * 16
                    term = codes_ref[i * CHUNK + at : i * CHUNK + at + 16, j * LANES : (j + 1) * LANES]
                    term = term * spread[at : at + 16]
                    part = term if part is None else part + term
                parts.append(part.astype(f32))
            total = total + jnp.concatenate(parts, axis=1)
    spread_cols(jnp.sum(total, axis=0, keepdims=True), cols_ref)


def col_pass(recv, codes, groups):
    count, columns = codes.shape
    return pl.pallas_call(
        col_pass_kernel,
        in_specs=[IN_VMEM, IN_VMEM],
        out_specs=IN_VMEM,
        out_shape=jax.ShapeDtypeStruct((groups, columns // LANES, LANES), f32),
        compiler_params=params(),
        cost_estimate=cost(2 * count * columns, 0, 2 * count * columns),
        name="col_pass",
    )(recv, codes)


def student_kernel(rows_ref, protos_ref, expo_ref, norm_ref, turned_ref, held_ref, sem):
    fetch(rows_ref, held_ref, sem)
    count, columns = expo_ref.shape
    lines = CHUNK // LANES
    for i in range(count // CHUNK):
        span = slice(i * CHUNK, (i + 1) * CHUNK)
        rows = held_ref[span, :]
        scores = jnp.dot(rows, protos_ref[...], preferred_element_type=f32)
        expo = jnp.exp2(scores * (student_scale * LOG2E))
        expo_ref[span, :] = expo.astype(bf16)
        part = expo[:, :LANES]
        for j in range(1, columns // LANES):
            part = part + expo[:, j * LANES : (j + 1) * LANES]
        norm_ref[i * lines : (i + 1) * lines, :] = sum_lanes(part)
        turned_ref[:, span] = rows.T


def student_expo(rows, protos):
    count, width = rows.shape
    columns = protos.shape[1]
    return pl.pallas_call(
        student_kernel,
        in_specs=[IN_HBM, IN_VMEM],
        out_specs=(IN_VMEM, IN_VMEM, IN_VMEM),
        out_shape=(
            pltpu.VMEM((count, columns), bf16),
            jax.ShapeDtypeStruct((count // LANES, LANES), f32),
            pltpu.VMEM((width, count), bf16),
        ),
        scratch_shapes=[pltpu.VMEM((count, width), bf16), pltpu.SemaphoreType.DMA],
        compiler_params=params(),
        cost_estimate=cost(2 * count * width * columns, count * columns, 2 * count * columns),
        name="student_expo",
    )(rows, protos)


def scaled_product(recv_ref, part, turned_ref, codes_ref):
    scale = 1.0 / jnp.sum(recv_ref[:, part].astype(f32), axis=0)
    turned = (turned_ref[...].astype(f32) * lane_row(scale, 0, scale.shape[0])).astype(bf16)
    return jnp.dot(turned, codes_ref[...], preferred_element_type=f32)


def student_grad_kernel(recv_ref, turned_ref, expo_ref, out_ref):
    out_ref[...] = scaled_product(recv_ref, 1, turned_ref, expo_ref)


def student_grad(recv, turned, expo):
    count, columns = expo.shape
    width = turned.shape[0]
    return pl.pallas_call(
        student_grad_kernel,
        in_specs=[IN_VMEM] * 3,
        out_specs=IN_VMEM,
        out_shape=pltpu.VMEM((width, columns), f32),
        compiler_params=params(),
        cost_estimate=cost(2 * count * width * columns, 0, 2 * count * columns),
        name="student_grad",
    )(recv, turned, expo)


def grad_kernel(recv_ref, cols_ref, turned_ref, codes_ref, stud_ref, out_ref):
    teach = scaled_product(recv_ref, 0, turned_ref, codes_ref)
    mass = jnp.sum(cols_ref[...], axis=0)
    col_scale = lane_row(1.0 / mass, 0, cols_ref.shape[1])
    grad = grad_factor * (stud_ref[...] - teach * col_scale)
    for piece in range(out_ref.shape[0]):
        out_ref[piece] = pack_piece(grad, piece, out_ref.shape[0]).astype(bf16)


def grad_pieces(recv, cols, turned, codes, stud):
    count, columns = codes.shape
    width = turned.shape[0]
    pieces = cols.shape[0]
    return pl.pallas_call(
        grad_kernel,
        in_specs=[IN_VMEM] * 5,
        out_specs=IN_VMEM,
        out_shape=jax.ShapeDtypeStruct((pieces, width // 2, 2 * columns // pieces), bf16),
        compiler_params=params(),
        cost_estimate=cost(2 * count * width * columns, 0, 2 * count * columns),
        name="grad_pieces",
    )(recv, cols, turned, codes, stud)


def back_kernel(recv_ref, weight_ref, out_ref):
    grad = jnp.sum(recv_ref[...].astype(f32), axis=0)
    weight = weight_ref[...]
    half = weight.shape[1] // 2

    def column_sum(values):
        total = jnp.sum(values, axis=0, keepdims=True)
        return total + jnp.concatenate([total[:, half:], total[:, :half]], axis=1)

    inverse = lax.rsqrt(column_sum(weight * weight) + epsilon)
    along = column_sum(grad * weight)
    out_ref[...] = (grad * inverse - weight * (inverse * inverse * inverse * along)).astype(bf16)


def weight_back(recv, weight):
    return pl.pallas_call(
        back_kernel,
        out_shape=jax.ShapeDtypeStruct(weight.shape, bf16),
        compiler_params=params(),
        name="weight_back",
    )(recv, weight)


def join_kernel(pieces_ref, out_ref):
    pieces, rows, lanes = pieces_ref.shape
    half = lanes // 2
    for pair in range(pieces // 2):
        left, right = pieces_ref[2 * pair], pieces_ref[2 * pair + 1]
        columns = pl.ds(pair * lanes, lanes)
        out_ref[:rows, columns] = jnp.concatenate([left[:, :half], right[:, :half]], axis=1)
        out_ref[rows:, columns] = jnp.concatenate([left[:, half:], right[:, half:]], axis=1)


def join_pieces(pieces):
    count, rows, lanes = pieces.shape
    return pl.pallas_call(
        join_kernel,
        out_shape=jax.ShapeDtypeStruct((2 * rows, count * lanes // 2), pieces.dtype),
        compiler_params=params(),
        name="join_pieces",
    )(pieces)


def exchange(values, axes):
    return lax.all_to_all(values, axes, 0, 0, tiled=True)


def shards(groups, members, teacher_patches, student_patches, mask_index, teacher_weight, student_weight):
    local = masked_rows(teacher_patches, student_patches, mask_index.reshape(1, -1))
    count, width = local.shape[1:]
    along_x = lax.all_gather(local, "x", axis=1, tiled=True)
    teach_rows = lax.all_gather(along_x[0], "z", axis=0, tiled=True)
    stud_x, teach_rows = lax.optimization_barrier((along_x[1], teach_rows))
    stud_rows = lax.all_gather(stud_x, "z", axis=0, tiled=True)
    teach_protos, stud_protos, packed = prototypes(teacher_weight, student_weight, groups)
    own_weight = lax.dynamic_index_in_dim(packed, lax.axis_index(GROUP), 0, keepdims=False)

    codes, cols = first_codes(teach_rows, teach_protos, groups)
    cols = exchange(cols, GROUP)
    rows = exchange(row_pass(cols, codes, members), MEMBER)
    cols = exchange(col_pass(rows, codes, groups), GROUP)
    expo, norm, turned = student_expo(stud_rows, stud_protos)
    both = exchange(row_pass(cols, codes, members, norm), MEMBER)
    cols = exchange(col_pass(both, codes, groups), GROUP)
    stud = student_grad(both, turned, expo)
    rows = exchange(row_pass(cols, codes, members), MEMBER)
    pieces = exchange(grad_pieces(rows, cols, turned, codes, stud), GROUP)
    return join_pieces(lax.all_gather(weight_back(pieces, own_weight), GROUP, axis=0))


def solution(mesh):
    groups, members = mesh.devices.shape
    split = Mesh(mesh.devices.reshape(8, 2, 8, 4), GROUP + MEMBER)
    rows = P(GROUP + MEMBER, None)
    columns = P(None, MEMBER)
    return jax.shard_map(
        functools.partial(shards, groups, members),
        mesh=split,
        in_specs=(rows, rows, P(GROUP + MEMBER), columns, columns),
        out_specs=columns,
        check_vma=False,
    )
```

time: 302 us -> 250 us (0.83)
  Pallas kernels: 62.4 us -> 23.3 us
  blocking collectives: 137 us -> 103 us
  local copies, waits for them, and re-layouts: 8.4 us -> 24 us
  waiting for transfers between devices: 65.6 us -> 69.6 us
    pallas_call x8 -> x9, Pallas kernels: 60.4 us -> 21.3 us  [the longest x3 5.94 us: row_pass(): pl.pallas_call(functools.partial(row_pass_kernel, bool(extra)), in_specs=...]
    all_to_all x5 -> x4, blocking collectives: 110 us -> 76 us  [exchange(): return lax.all_to_all(values, axes, 0, 0, tiled=True)]
    unnamed x18 -> x30, local copies, waits for them, and re-layouts: 7.56 us -> 22.3 us
    all_to_all x2 -> x3, waiting for transfers between devices: 17.3 us -> 21.3 us  [exchange(): return lax.all_to_all(values, axes, 0, 0, tiled=True)]
    all_to_all x2 -> x3, starting transfers between devices: 14.2 us -> 15.9 us  [exchange(): return lax.all_to_all(values, axes, 0, 0, tiled=True)]
  transfers between devices with their start and end apart: 4 -> 5, of which waited for: 2 -> 3; matrix products, arithmetic and copies ran while one was open for 0% -> 0% of each run, Pallas kernels for 14% -> 5%
where the time goes in v2:
time: 250 us
  blocking collectives  103 us (41%)
  waiting for transfers between devices  69.6 us (28%)
  local copies, waits for them, and re-layouts  24 us (10%)
  Pallas kernels  23.3 us (9%)
  starting transfers between devices  16 us (6%)
  between operations  13.6 us (5%)
    all_to_all x4, blocking collectives, exchange(): return lax.all_to_all(values, axes, 0, 0, tiled=True)  76 us
    all_gather x1, waiting for transfers between devices, shards(): teach_rows = lax.all_gather(along_x[0], 'z', axis=0, tiled=True)  48.2 us
    unnamed x30, local copies, waits for them, and re-layouts  22.3 us
    all_to_all x3, waiting for transfers between devices, exchange(): return lax.all_to_all(values, axes, 0, 0, tiled=True)  21.3 us
    all_to_all x3, starting transfers between devices, exchange(): return lax.all_to_all(values, axes, 0, 0, tiled=True)  15.9 us
    all_gather x1, blocking collectives, shards(): lax.all_gather(weight_back(pieces, own_weight), GROUP, axis=0)  15.9 us
    all_gather x1, blocking collectives, shards(): along_x = lax.all_gather(local, 'x', axis=1, tiled=True)  11.1 us
    pallas_call x3, Pallas kernels, row_pass(): pl.pallas_call(functools.partial(row_pass_kernel, bool(extra)), in_specs=...  5.94 us
  transfers between devices with their start and end apart: 5, of which 3 were waited for; matrix products, arithmetic and copies ran while one was open for 0% of the time, Pallas kernels for 5%

profile of v2, /device:TPU:1, one launch (start us, length us, event | category | flops | bytes accessed | tf_op | source)
XLA Modules:
  0.0 249.5 jit_solution(13614170901056931178)
XLA Ops:
  6.5 0.0 copy-start.8
  6.5 0.0 copy-start.7
  6.5 0.0 all-gather.7.cloned.1.call-start
  6.5 0.0 copy-start.9
  6.5 1.0 copy-done.9
  7.5 0.0 copy-start.10
  7.5 0.9 copy-done.10
  8.4 0.0 copy-start.12
  8.4 0.7 copy-done.12
  9.1 0.3 masked_rows.1
  9.4 11.1 %all_gather.15 = bf16[2,512,256]{2,1,0:T(8,128)(2,1)S(1)} all-gather(bf16[2,128,256]{2,1,0:T(8,128)(2,1)S(1)} %masked_rows.1), channel_id=1, replica_groups=mesh['y'=8,'core'=2,'z'=8,'x'=4] {'x'}, dimensions={1}, use_global_device_ids=true | all-gather | bytes 655360 | tf_op jit(solution)/shard_map/all_gather | solution.py:341
  20.5 0.8 fusion
  21.3 0.0 all-gather.7.cloned.1.call-update
  21.3 0.0 all-gather.5.cloned.1.call-start
  21.4 48.2 %all-gather.7.cloned.1.call-done = bf16[1,4096,256]{2,1,0:T(8,128)(2,1)} async-done(((bf16[1,512,256]{2,1,0:T(8,128)(2,1)}), bf16[1,4096,256]{2,1,0:T(8,128)(2,1)}) %all-gather.7.cloned.1.call-update) | async-done | bytes 2097168 | tf_op jit(solution)/shard_map/all_gather | solution.py:342
  69.6 0.0 all-gather.5.cloned.1.call-update
  69.7 0.0 copy-done.8
  69.7 0.0 copy-done.7
  69.7 0.5 prototypes.1
  70.2 0.0 copy-start.11
  70.2 1.0 copy-done.11
  71.2 0.0 copy-start.14
  71.2 1.6 copy-done.14
  72.8 2.5 %first_codes.1 = (bf16[4096,1024]{1,0:T(8,128)(2,1)S(1)}, f32[16,8,128]{2,1,0:T(8,128)S(1)}) custom-call(bf16[4096,256]{1,0:T(8,128)(2,1)S(1)} %bitcast.9, bf16[256,1024]{1,0:T(8,128)(2,1)S(1)} %get-tuple-element.16.protos_ref), custom_call_target="tpu_custom_call" | custom-call | flops 2147483648 | bytes 8388608 | tf_op jit(solution)/shard_map/first_codes/pallas_call | solution.py:115
  75.4 0.0 copy-start
  75.4 19.1 %all_to_all.35.refs_0_ = f32[16,8,128]{2,1,0:T(8,128)S(1)} all-to-all(f32[16,8,128]{2,1,0:T(8,128)S(1)} %get-tuple-element.17), channel_id=1, replica_groups=mesh['y'=8,'core'=2,'z'=8,'x'=4] {'y','core'}, dimensions={0} | all-to-all | bytes 131072 | tf_op jit(solution)/shard_map/all_to_all | solution.py:335
  94.4 1.7 row_pass.3
  96.2 20.4 %all_to_all.36.recv_ref = bf16[32,1,32,128]{3,2,1,0:T(8,128)(2,1)S(1)} all-to-all(bf16[32,1,32,128]{3,2,1,0:T(8,128)(2,1)S(1)} %row_pass.3), channel_id=1, replica_groups=mesh['y'=8,'core'=2,'z'=8,'x'=4] {'z','x'}, dimensions={0} | all-to-all | bytes 524288 | tf_op jit(solution)/shard_map/all_to_all | solution.py:335
  116.6 0.0 copy-done
  116.6 2.3 col_pass.2
  118.9 5.9 %all-to-all-start.2 = ((f32[16,8,128]{2,1,0:T(8,128)}), f32[16,8,128]{2,1,0:T(8,128)S(1)}, u32[]{:S(2)}, u32[]{:S(2)}) async-start(f32[16,8,128]{2,1,0:T(8,128)} %col_pass.2), calls=%async_computation.2 | async-start | bytes 131072 | tf_op jit(solution)/shard_map/all_to_all | solution.py:335
  124.8 0.0 all-gather.5.cloned.1.call-done.rows_ref
  124.8 0.0 copy-start.13
  124.9 1.6 copy-done.13
  126.4 3.3 %student_expo.1 = (bf16[4096,1024]{1,0:T(8,128)(2,1)S(1)}, f32[32,128]{1,0:T(8,128)S(1)}, bf16[256,4096]{1,0:T(8,128)(2,1)S(1)}) custom-call(bf16[4096,256]{1,0:T(8,128)(2,1)S(1)} %copy-done.13, bf16[256,1024]{1,0:T(8,128)(2,1)S(1)} %get-tuple-element.20.protos_ref), custom_call_target="tpu_custom_call" | custom-call | flops 2147483648 | bytes 8388608 | tf_op jit(solution)/shard_map/student_expo/pallas_call | solution.py:227
  129.7 0.0 copy-start.3
  129.7 3.2 %copy-done.3 = bf16[4096,1024]{1,0:T(8,128)(2,1)} copy-done((bf16[4096,1024]{1,0:T(8,128)(2,1)}, bf16[4096,1024]{1,0:T(8,128)(2,1)S(1)}, u32[]{:S(2)}) %copy-start.3) | copy-done | bytes 8388632
  132.9 0.0 all-to-all-done.2.refs_0_
  132.9 0.0 copy-start.1
  132.9 3.4 %copy-done.1 = bf16[4096,1024]{1,0:T(8,128)(2,1)S(1)} copy-done((bf16[4096,1024]{1,0:T(8,128)(2,1)S(1)}, bf16[4096,1024]{1,0:T(8,128)(2,1)}, u32[]{:S(2)}) %copy-start.1) | copy-done | bytes 8388632
  136.3 1.8 row_pass.4
  138.1 17.1 %all_to_all.37.recv_ref = bf16[32,2,32,128]{3,2,1,0:T(8,128)(2,1)S(1)} all-to-all(bf16[32,2,32,128]{3,2,1,0:T(8,128)(2,1)S(1)} %row_pass.4), channel_id=1, replica_groups=mesh['y'=8,'core'=2,'z'=8,'x'=4] {'z','x'}, dimensions={0} | all-to-all | bytes 1048576 | tf_op jit(solution)/shard_map/all_to_all | solution.py:335
  155.2 1.7 col_pass.3
  156.9 19.5 %all_to_all.38.refs_0_.cols_ref = f32[16,8,128]{2,1,0:T(8,128)S(1)} all-to-all(f32[16,8,128]{2,1,0:T(8,128)S(1)} %col_pass.3), channel_id=1, replica_groups=mesh['y'=8,'core'=2,'z'=8,'x'=4] {'y','core'}, dimensions={0} | all-to-all | bytes 131072 | tf_op jit(solution)/shard_map/all_to_all | solution.py:335
  176.4 2.4 row_pass.5
  178.8 4.5 %all-to-all-start.5 = ((bf16[32,1,32,128]{3,2,1,0:T(8,128)(2,1)}), bf16[32,1,32,128]{3,2,1,0:T(8,128)(2,1)S(1)}, u32[]{:S(2)}, u32[]{:S(2)}) async-start(bf16[32,1,32,128]{3,2,1,0:T(8,128)(2,1)} %row_pass.5), calls=%async_computation.5 | async-start | bytes 524288 | tf_op jit(solution)/shard_map/all_to_all | solution.py:335
  183.3 0.0 copy-start.4
  183.3 3.4 %copy-done.4 = bf16[4096,1024]{1,0:T(8,128)(2,1)S(1)} copy-done((bf16[4096,1024]{1,0:T(8,128)(2,1)S(1)}, bf16[4096,1024]{1,0:T(8,128)(2,1)}, u32[]{:S(2)}) %copy-start.4) | copy-done | bytes 8388632
  186.7 2.3 student_grad.1.stud_ref
  189.0 0.0 copy-start.5
  189.0 1.0 copy-done.5
  190.1 4.8 %all-to-all-done.5.recv_ref = bf16[32,1,32,128]{3,2,1,0:T(8,128)(2,1)S(1)} async-done(((bf16[32,1,32,128]{3,2,1,0:T(8,128)(2,1)}), bf16[32,1,32,128]{3,2,1,0:T(8,128)(2,1)S(1)}, u32[]{:S(2)}, u32[]{:S(2)}) %all-to-all-start.5) | async-done | bytes 262176 | tf_op jit(solution)/shard_map/all_to_all | solution.py:335
  194.9 0.0 copy-start.2
  194.9 3.4 %copy-done.2 = bf16[4096,1024]{1,0:T(8,128)(2,1)S(1)} copy-done((bf16[4096,1024]{1,0:T(8,128)(2,1)S(1)}, bf16[4096,1024]{1,0:T(8,128)(2,1)}, u32[]{:S(2)}) %copy-start.2) | copy-done | bytes 8388632
  198.3 0.0 copy-start.6
  198.3 1.2 copy-done.6
  199.5 3.2 %grad_pieces.1 = bf16[16,128,128]{2,1,0:T(8,128)(2,1)} custom-call(bf16[32,1,32,128]{3,2,1,0:T(8,128)(2,1)S(1)} %all-to-all-done.5.recv_ref, f32[16,8,128]{2,1,0:T(8,128)S(1)} %all_to_all.38.refs_0_.cols_ref, bf16[256,4096]{1,0:T(8,128)(2,1)S(1)} %get-tuple-element.22.turned_ref, bf16[4096,1024]{1,0:T(8,128)(2,1)S(1)} %copy-done.2, f32[256,1024]{1,0:T(8,128)S(1)} %copy-done.6), custom_call_target="tpu_custom_call" | custom-call | flops 2147483648 | bytes 8388608 | tf_op jit(solution)/shard_map/grad_pieces/pallas_call | solution.py:280
  202.7 5.5 %all-to-all-start.6 = ((bf16[16,128,128]{2,1,0:T(8,128)(2,1)}), bf16[16,128,128]{2,1,0:T(8,128)(2,1)S(1)}, u32[]{:S(2)}, u32[]{:S(2)}) async-start(bf16[16,128,128]{2,1,0:T(8,128)(2,1)} %grad_pieces.1), calls=%async_computation.6 | async-start | bytes 1048576 | tf_op jit(solution)/shard_map/all_to_all | solution.py:335
  208.3 0.8 dynamic-slice_bitcast_fusion.weight_ref
  209.1 16.5 %all-to-all-done.6.recv_ref = bf16[16,128,128]{2,1,0:T(8,128)(2,1)S(1)} async-done(((bf16[16,128,128]{2,1,0:T(8,128)(2,1)}), bf16[16,128,128]{2,1,0:T(8,128)(2,1)S(1)}, u32[]{:S(2)}, u32[]{:S(2)}) %all-to-all-start.6) | async-done | bytes 524320 | tf_op jit(solution)/shard_map/all_to_all | solution.py:335
  225.6 0.2 weight_back.1
  225.8 15.9 %all-gather.1 = bf16[2048,128]{1,0:T(8,128)(2,1)S(1)} all-gather(bf16[128,128]{1,0:T(8,128)(2,1)S(1)} %weight_back.1), channel_id=3, replica_groups=mesh['y'=8,'core'=2,'z'=8,'x'=4] {'y','core'}, dimensions={0}, use_global_device_ids=true | all-gather | bytes 557056 | tf_op jit(solution)/shard_map/all_gather | solution.py:358
  241.7 1.0 join_pieces.1
Async XLA Ops:
  6.5 63.1 %copy-start.8 = (bf16[256,1024]{1,0:T(8,128)(2,1)S(1)}, bf16[256,1024]{1,0:T(8,128)(2,1)}, u32[]{:S(2)}) copy-start(bf16[256,1024]{1,0:T(8,128)(2,1)} %student_ref.3) | copy-start | bytes 1572868
  6.5 63.1 %copy-start.7 = (bf16[256,1024]{1,0:T(8,128)(2,1)S(1)}, bf16[256,1024]{1,0:T(8,128)(2,1)}, u32[]{:S(2)}) copy-start(bf16[256,1024]{1,0:T(8,128)(2,1)} %teacher_ref.3) | copy-start | bytes 1572868
  6.5 63.1 %all-gather.7.cloned.1.call-start = ((), (), s32[]{:S(2)}) async-start(), calls=%async_computation.8 | async-start | bytes 2359296 | tf_op jit(solution)/shard_map/all_gather | solution.py:342
  6.5 1.0 copy-start.9
  7.5 0.9 copy-start.10
  8.4 0.7 copy-start.12
  21.3 103.5 %all-gather.5.cloned.1.call-start = ((), (), s32[]{:S(2)}) async-start(), calls=%async_computation.7 | async-start | bytes 2359296 | tf_op jit(solution)/shard_map/all_gather | solution.py:344
  70.2 1.0 copy-start.11
  71.2 1.6 copy-start.14
  75.4 41.2 %copy-start = (bf16[4096,1024]{1,0:T(8,128)(2,1)}, bf16[4096,1024]{1,0:T(8,128)(2,1)S(1)}, u32[]{:S(2)}) copy-start(bf16[4096,1024]{1,0:T(8,128)(2,1)S(1)} %get-tuple-element.18.refs_1_.codes_ref) | copy-start | bytes 25165828
  118.9 14.1 %all-to-all-start.2 = ((f32[16,8,128]{2,1,0:T(8,128)}), f32[16,8,128]{2,1,0:T(8,128)S(1)}, u32[]{:S(2)}, u32[]{:S(2)}) async-start(f32[16,8,128]{2,1,0:T(8,128)} %col_pass.2), calls=%async_computation.2 | async-start | bytes 131072 | tf_op jit(solution)/shard_map/all_to_all | solution.py:335
  124.8 1.6 copy-start.13
  129.7 3.2 %copy-start.3 = (bf16[4096,1024]{1,0:T(8,128)(2,1)}, bf16[4096,1024]{1,0:T(8,128)(2,1)S(1)}, u32[]{:S(2)}) copy-start(bf16[4096,1024]{1,0:T(8,128)(2,1)S(1)} %get-tuple-element.23.expo_ref) | copy-start | bytes 25165828
  132.9 3.4 %copy-start.1 = (bf16[4096,1024]{1,0:T(8,128)(2,1)S(1)}, bf16[4096,1024]{1,0:T(8,128)(2,1)}, u32[]{:S(2)}) copy-start(bf16[4096,1024]{1,0:T(8,128)(2,1)} %copy-done) | copy-start | bytes 25165828
  178.8 16.1 %all-to-all-start.5 = ((bf16[32,1,32,128]{3,2,1,0:T(8,128)(2,1)}), bf16[32,1,32,128]{3,2,1,0:T(8,128)(2,1)S(1)}, u32[]{:S(2)}, u32[]{:S(2)}) async-start(bf16[32,1,32,128]{3,2,1,0:T(8,128)(2,1)} %row_pass.5), calls=%async_computation.5 | async-start | bytes 524288 | tf_op jit(solution)/shard_map/all_to_all | solution.py:335
  183.3 3.4 %copy-start.4 = (bf16[4096,1024]{1,0:T(8,128)(2,1)S(1)}, bf16[4096,1024]{1,0:T(8,128)(2,1)}, u32[]{:S(2)}) copy-start(bf16[4096,1024]{1,0:T(8,128)(2,1)} %copy-done.3) | copy-start | bytes 25165828
  189.0 1.1 copy-start.5
  194.9 3.4 %copy-start.2 = (bf16[4096,1024]{1,0:T(8,128)(2,1)S(1)}, bf16[4096,1024]{1,0:T(8,128)(2,1)}, u32[]{:S(2)}) copy-start(bf16[4096,1024]{1,0:T(8,128)(2,1)} %copy-done) | copy-start | bytes 25165828
  198.3 1.2 copy-start.6
  202.7 22.9 %all-to-all-start.6 = ((bf16[16,128,128]{2,1,0:T(8,128)(2,1)}), bf16[16,128,128]{2,1,0:T(8,128)(2,1)S(1)}, u32[]{:S(2)}, u32[]{:S(2)}) async-start(bf16[16,128,128]{2,1,0:T(8,128)(2,1)} %grad_pieces.1), calls=%async_computation.6 | async-start | bytes 1048576 | tf_op jit(solution)/shard_map/all_to_all | solution.py:335
Sparse Core Ops, SparseCore 0:
  21.5 48.1 all-gather.6
  71.7 47.8 all-gather.4

commit v3 on v2

v3 whole, which is shorter than its diff:
```python
import functools
import math

import jax
import jax.numpy as jnp
from jax import lax
from jax.experimental import pallas as pl
from jax.experimental.pallas import tpu as pltpu
from jax.sharding import Mesh
from jax.sharding import PartitionSpec as P

GROUP = ("y", "core")
MEMBER = ("z", "x")
LANES = 128
CHUNK = 1024
EXTRA = 8
VMEM_LIMIT = 16 * 1024 * 1024
LOG2E = math.log2(math.e)
IN_VMEM = pl.BlockSpec(memory_space=pltpu.VMEM)
IN_HBM = pl.BlockSpec(memory_space=pltpu.HBM)

epsilon = 1e-06
teacher_scale = 1.0 / 0.07
student_scale = 1.0 / 0.1
grad_factor = 256.0 / 0.1
NT = (((1,), (1,)), ((), ()))
TN = (((0,), (0,)), ((), ()))
f32 = jnp.float32
bf16 = jnp.bfloat16


def params():
    return pltpu.CompilerParams(vmem_limit_bytes=VMEM_LIMIT)


def cost(flops, transcendentals, nbytes):
    return pl.CostEstimate(flops=flops, transcendentals=transcendentals, bytes_accessed=nbytes)


def lane_row(block, start, count):
    return jnp.concatenate([block[start + j : start + j + 1, :] for j in range(count)], axis=1)


def in_hbm(values):
    return pltpu.with_memory_space_constraint(values, pltpu.HBM)


def prepare_kernel(*refs):
    sources, (teach_ref, stud_ref, teach_protos_ref, stud_protos_ref), held, sems = refs[:5], refs[5:9], refs[9:14], refs[14]
    copies = [pltpu.make_async_copy(source, to, sems.at[i]) for i, (source, to) in enumerate(zip(sources, held))]
    for copy in copies:
        copy.start()
    copies[0].wait()
    count = held[0].shape[1]
    patches = held[1].shape[0]
    chosen = lax.broadcasted_iota(jnp.int32, (patches, count), 0) == held[0][...]
    chosen = chosen.astype(f32).astype(bf16)
    for part, out in ((1, teach_ref), (2, stud_ref)):
        copies[part].wait()
        rows = lax.dot_general(chosen, held[part][...], TN, preferred_element_type=f32)
        square = jnp.sum(rows * rows, axis=1, keepdims=True)
        rows = (rows * lax.rsqrt(square + epsilon)).astype(bf16)
        out[...] = jnp.broadcast_to(rows[None], out.shape) if part == 1 else rows
    for part, out in ((3, teach_protos_ref), (4, stud_protos_ref)):
        copies[part].wait()
        values = held[part][...].astype(f32)
        square = jnp.sum(values * values, axis=0, keepdims=True)
        out[...] = (values * lax.rsqrt(square + epsilon)).astype(bf16)


def prepare(mask, teacher, student, teacher_weight, student_weight, copies):
    sources = (mask, teacher, student, teacher_weight, student_weight)
    count, width = mask.shape[1], teacher.shape[1]
    return pl.pallas_call(
        prepare_kernel,
        in_specs=[IN_HBM] * 5,
        out_specs=(IN_VMEM,) * 4,
        out_shape=(
            jax.ShapeDtypeStruct((copies, count, width), bf16),
            jax.ShapeDtypeStruct((count, width), bf16),
            jax.ShapeDtypeStruct(teacher_weight.shape, bf16),
            jax.ShapeDtypeStruct(student_weight.shape, bf16),
        ),
        scratch_shapes=[pltpu.VMEM(source.shape, source.dtype) for source in sources] + [pltpu.SemaphoreType.DMA((5,))],
        compiler_params=params(),
        name="prepare",
    )(*map(in_hbm, sources))


def pack_piece(block, piece, pieces):
    rows, columns = block.shape
    width = columns // pieces
    part = block[:, piece * width : (piece + 1) * width]
    return jnp.concatenate([part[: rows // 2], part[rows // 2 :]], axis=1)


def spread_cols(total, cols_ref):
    for j in range(cols_ref.shape[1]):
        part = total[:, j * LANES : (j + 1) * LANES]
        cols_ref[:, j, :] = jnp.broadcast_to(part, (cols_ref.shape[0], LANES))


def fetch(source, target, sem):
    copy = pltpu.make_async_copy(source, target, sem)
    copy.start()
    copy.wait()


class Blocks:
    def __init__(self, source, held=None, sems=None):
        self.count = source.shape[0] // CHUNK
        self.block = source if held is None else held
        self.copies = []
        if held is not None:
            for i in range(self.count):
                span = pl.ds(i * CHUNK, CHUNK)
                self.copies.append(pltpu.make_async_copy(source.at[span, :], held.at[span, :], sems.at[i]))
            for copy in self.copies:
                copy.start()

    def ready(self, i):
        if self.copies:
            self.copies[i].wait()


def held_blocks(shape):
    return [pltpu.VMEM(shape, bf16), pltpu.SemaphoreType.DMA((shape[0] // CHUNK,))]


def codes_kernel(rows_ref, protos_ref, codes_ref, cols_ref):
    scores = jnp.dot(rows_ref[...], protos_ref[...], preferred_element_type=f32)
    codes = jnp.exp2(scores * (teacher_scale * LOG2E))
    codes_ref[...] = codes.astype(bf16)
    spread_cols(jnp.sum(codes, axis=0, keepdims=True), cols_ref)


def first_codes(rows, protos, groups):
    count, width = rows.shape
    columns = protos.shape[1]
    return pl.pallas_call(
        codes_kernel,
        in_specs=[IN_VMEM, IN_VMEM],
        out_specs=(IN_VMEM, IN_VMEM),
        out_shape=(
            pltpu.VMEM((count, columns), bf16),
            jax.ShapeDtypeStruct((groups, columns // LANES, LANES), f32),
        ),
        compiler_params=params(),
        cost_estimate=cost(2 * count * width * columns, count * columns, 2 * count * columns),
        name="first_codes",
    )(rows, protos)


def sum_lanes(block):
    ones = jnp.ones((16, LANES), bf16)
    sums = lax.dot_general(ones, block.astype(bf16), NT, preferred_element_type=f32)[0:1]
    lines = block.shape[0] // LANES
    return jnp.concatenate([sums[:, j * LANES : (j + 1) * LANES] for j in range(lines)], axis=0)


def row_pass_kernel(stage, *refs):
    recv_ref, codes_ref = refs[:2]
    norm_ref, refs = (refs[2], refs[3:]) if stage else (None, refs[2:])
    out_ref, held = refs[0], refs[1:]
    blocks = Blocks(codes_ref, *held)
    tiles = recv_ref.shape[1]
    lines = CHUNK // LANES
    scale = lane_row(1.0 / jnp.sum(recv_ref[...], axis=0), 0, tiles)
    for i in range(blocks.count):
        blocks.ready(i)
        part = None
        for j in range(tiles):
            columns = slice(j * LANES, (j + 1) * LANES)
            term = blocks.block[i * CHUNK : (i + 1) * CHUNK, columns].astype(f32) * scale[:, columns]
            part = term if part is None else part + term
        block = jnp.broadcast_to(sum_lanes(part)[None], (out_ref.shape[0], lines, LANES))
        out_ref[:, i * lines : (i + 1) * lines, :] = block.astype(bf16)
    first = blocks.count * lines
    if stage == 1:
        for member in range(out_ref.shape[0]):
            line = norm_ref[member : member + 1, :]
            out_ref[member, first:, :] = jnp.broadcast_to(line, (EXTRA, LANES)).astype(bf16)
    if stage == 2:
        total = jnp.sum(norm_ref[:, first : first + 1, :].astype(f32), axis=0)
        high = total.astype(bf16).astype(f32)
        index = lax.broadcasted_iota(jnp.int32, (EXTRA, LANES), 0)
        extra = jnp.where(index == 0, high, jnp.where(index == 1, total - high, 0.0)).astype(bf16)
        out_ref[:, first:, :] = jnp.broadcast_to(extra[None], (out_ref.shape[0], EXTRA, LANES))


def row_pass(recv, codes, members, stream, norm=None, stage=0):
    count, columns = codes.shape
    lines = count // LANES + (EXTRA if stage else 0)
    return pl.pallas_call(
        functools.partial(row_pass_kernel, stage),
        in_specs=[IN_VMEM, IN_HBM if stream else IN_VMEM] + ([IN_VMEM] if stage else []),
        out_specs=IN_VMEM,
        out_shape=jax.ShapeDtypeStruct((members, lines, LANES), bf16),
        scratch_shapes=held_blocks(codes.shape) if stream else [],
        compiler_params=params(),
        cost_estimate=cost(2 * count * columns, 0, 2 * count * columns),
        name="row_pass",
    )(recv, in_hbm(codes) if stream else codes, *((norm,) if stage else ()))


def col_pass_kernel(recv_ref, codes_ref, cols_ref):
    count, columns = codes_ref.shape
    lines = CHUNK // LANES
    scale = 1.0 / jnp.sum(recv_ref[:, : count // LANES, :].astype(f32), axis=0)
    ones = jnp.ones((16, LANES), bf16)
    first = lax.broadcasted_iota(jnp.int32, (16, CHUNK), 0) == 0
    total = jnp.zeros((16, columns), f32)
    for i in range(count // CHUNK):
        row = jnp.where(first, lane_row(scale, i * lines, lines), 0.0).astype(bf16)
        spread = lax.dot_general(row, ones, TN, preferred_element_type=f32).astype(bf16)
        for g in range(lines):
            parts = []
            for j in range(columns // LANES):
                part = None
                for q in range(LANES // 16):
                    at = g * LANES + q * 16
                    term = codes_ref[i * CHUNK + at : i * CHUNK + at + 16, j * LANES : (j + 1) * LANES]
                    term = term * spread[at : at + 16]
                    part = term if part is None else part + term
                parts.append(part.astype(f32))
            total = total + jnp.concatenate(parts, axis=1)
    spread_cols(jnp.sum(total, axis=0, keepdims=True), cols_ref)


def col_pass(recv, codes, groups):
    count, columns = codes.shape
    return pl.pallas_call(
        col_pass_kernel,
        in_specs=[IN_VMEM, IN_VMEM],
        out_specs=IN_VMEM,
        out_shape=jax.ShapeDtypeStruct((groups, columns // LANES, LANES), f32),
        compiler_params=params(),
        cost_estimate=cost(2 * count * columns, 0, 2 * count * columns),
        name="col_pass",
    )(recv, codes)


def student_kernel(rows_ref, protos_ref, expo_ref, norm_ref, turned_ref, held_ref, sem):
    fetch(rows_ref, held_ref, sem)
    count, columns = expo_ref.shape
    lines = CHUNK // LANES
    for i in range(count // CHUNK):
        span = slice(i * CHUNK, (i + 1) * CHUNK)
        rows = held_ref[span, :]
        scores = jnp.dot(rows, protos_ref[...], preferred_element_type=f32)
        expo = jnp.exp2(scores * (student_scale * LOG2E))
        expo_ref[span, :] = expo.astype(bf16)
        part = expo[:, :LANES]
        for j in range(1, columns // LANES):
            part = part + expo[:, j * LANES : (j + 1) * LANES]
        norm_ref[i * lines : (i + 1) * lines, :] = sum_lanes(part)
        turned_ref[:, span] = rows.T


def student_expo(rows, protos):
    count, width = rows.shape
    columns = protos.shape[1]
    return pl.pallas_call(
        student_kernel,
        in_specs=[IN_HBM, IN_VMEM],
        out_specs=(IN_VMEM, IN_VMEM, IN_VMEM),
        out_shape=(
            jax.ShapeDtypeStruct((count, columns), bf16),
            jax.ShapeDtypeStruct((count // LANES, LANES), f32),
            jax.ShapeDtypeStruct((width, count), bf16),
        ),
        scratch_shapes=[pltpu.VMEM((count, width), bf16), pltpu.SemaphoreType.DMA],
        compiler_params=params(),
        cost_estimate=cost(2 * count * width * columns, count * columns, 2 * count * columns),
        name="student_expo",
    )(in_hbm(rows), protos)


def scaled_product(scale, turned_ref, blocks):
    lines = CHUNK // LANES
    total = None
    for i in range(blocks.count):
        span = slice(i * CHUNK, (i + 1) * CHUNK)
        turned = (turned_ref[:, span].astype(f32) * lane_row(scale, i * lines, lines)).astype(bf16)
        blocks.ready(i)
        term = jnp.dot(turned, blocks.block[span, :], preferred_element_type=f32)
        total = term if total is None else total + term
    return total


def grad_kernel(recv_ref, cols_ref, turned_ref, codes_ref, expo_ref, out_ref, *held):
    stud_blocks = Blocks(expo_ref, *held)
    members = recv_ref.shape[0]
    lines = codes_ref.shape[0] // LANES
    row_scale = 1.0 / jnp.sum(recv_ref[:, :lines, :].astype(f32), axis=0)
    norm = jnp.concatenate(
        [recv_ref[m, lines : lines + 1, :].astype(f32) + recv_ref[m, lines + 1 : lines + 2, :].astype(f32) for m in range(members)],
        axis=0,
    )
    teach = scaled_product(row_scale, turned_ref, Blocks(codes_ref))
    mass = jnp.sum(cols_ref[...], axis=0)
    teach = teach * lane_row(1.0 / mass, 0, cols_ref.shape[1])
    grad = grad_factor * (scaled_product(1.0 / norm, turned_ref, stud_blocks) - teach)
    for piece in range(out_ref.shape[0]):
        out_ref[piece] = pack_piece(grad, piece, out_ref.shape[0]).astype(bf16)


def grad_pieces(recv, cols, turned, codes, expo):
    count, columns = codes.shape
    width = turned.shape[0]
    pieces = cols.shape[0]
    return pl.pallas_call(
        grad_kernel,
        in_specs=[IN_VMEM, IN_VMEM, IN_VMEM, IN_VMEM, IN_HBM],
        out_specs=IN_VMEM,
        out_shape=jax.ShapeDtypeStruct((pieces, width // 2, 2 * columns // pieces), bf16),
        scratch_shapes=held_blocks(expo.shape),
        compiler_params=params(),
        cost_estimate=cost(4 * count * width * columns, 0, 4 * count * columns),
        name="grad_pieces",
    )(recv, cols, turned, codes, in_hbm(expo))


def back_kernel(index_ref, recv_ref, weight_ref, out_ref):
    half = out_ref.shape[1] // 2
    index = index_ref[0]
    block = weight_ref[:, pl.ds(pl.multiple_of(index // 2 * LANES, LANES), LANES)].astype(f32)
    block = jnp.where(index % 2 == 0, block[:, :half], block[:, half:])
    rows = block.shape[0] // 2
    weight = jnp.concatenate([block[:rows], block[rows:]], axis=1)
    grad = jnp.sum(recv_ref[...].astype(f32), axis=0)

    def column_sum(values):
        total = jnp.sum(values, axis=0, keepdims=True)
        return total + jnp.concatenate([total[:, half:], total[:, :half]], axis=1)

    inverse = lax.rsqrt(column_sum(weight * weight) + epsilon)
    along = column_sum(grad * weight)
    out_ref[...] = (grad * inverse - weight * (inverse * inverse * inverse * along)).astype(bf16)


def weight_back(index, recv, weight):
    return pl.pallas_call(
        back_kernel,
        in_specs=[pl.BlockSpec(memory_space=pltpu.SMEM), IN_VMEM, IN_VMEM],
        out_specs=IN_VMEM,
        out_shape=jax.ShapeDtypeStruct(recv.shape[1:], bf16),
        compiler_params=params(),
        name="weight_back",
    )(index, recv, weight)


def join_kernel(pieces_ref, out_ref):
    pieces, rows, lanes = pieces_ref.shape
    half = lanes // 2
    for pair in range(pieces // 2):
        left, right = pieces_ref[2 * pair], pieces_ref[2 * pair + 1]
        columns = pl.ds(pair * lanes, lanes)
        out_ref[:rows, columns] = jnp.concatenate([left[:, :half], right[:, :half]], axis=1)
        out_ref[rows:, columns] = jnp.concatenate([left[:, half:], right[:, half:]], axis=1)


def join_pieces(pieces):
    count, rows, lanes = pieces.shape
    return pl.pallas_call(
        join_kernel,
        out_shape=jax.ShapeDtypeStruct((2 * rows, count * lanes // 2), pieces.dtype),
        compiler_params=params(),
        name="join_pieces",
    )(pieces)


def exchange(values, axes):
    return lax.all_to_all(values, axes, 0, 0, tiled=True)


def shards(groups, members, teacher_patches, student_patches, mask_index, teacher_weight, student_weight):
    along_z, along_x = lax.axis_size("z"), lax.axis_size("x")
    own, stud_own, teach_protos, stud_protos = prepare(
        mask_index.reshape(1, -1), teacher_patches, student_patches, teacher_weight, student_weight, along_z
    )
    width = own.shape[2]
    stud_rows = lax.all_gather(stud_own, ("x", "z"), axis=0, tiled=True)
    line = exchange(own, "z")
    line = jnp.broadcast_to(line.reshape(1, -1, width), (along_x, line.shape[0] * line.shape[1], width))
    teach_rows = exchange(line, "x").reshape(-1, width)

    codes, cols = first_codes(teach_rows, teach_protos, groups)
    cols = exchange(cols, GROUP)
    rows = exchange(row_pass(cols, codes, members, False), MEMBER)
    cols = exchange(col_pass(rows, codes, groups), GROUP)
    expo, norm, turned = student_expo(stud_rows, stud_protos)
    rows = exchange(row_pass(cols, codes, members, True, norm, 1), MEMBER)
    cols = exchange(col_pass(rows, codes, groups), GROUP)
    rows = exchange(row_pass(cols, codes, members, False, rows, 2), MEMBER)
    pieces = exchange(grad_pieces(rows, cols, turned, codes, expo), GROUP)
    index = lax.axis_index(GROUP).reshape(1)
    back = weight_back(index, pieces, student_weight)
    return join_pieces(lax.all_gather(back, GROUP, axis=0))


def solution(mesh):
    groups, members = mesh.devices.shape
    split = Mesh(mesh.devices.reshape(8, 2, 8, 4), GROUP + MEMBER)
    rows = P(GROUP + MEMBER, None)
    columns = P(None, MEMBER)
    return jax.shard_map(
        functools.partial(shards, groups, members),
        mesh=split,
        in_specs=(rows, rows, P(GROUP + MEMBER), columns, columns),
        out_specs=columns,
        check_vma=False,
    )
```

time: 250 us -> 231 us (0.924)
  waiting for transfers between devices: 69.6 us -> 17.4 us
  blocking collectives: 103 us -> 154 us
  local copies, waits for them, and re-layouts: 24 us -> 3.37 us
  Pallas kernels: 23.3 us -> 30.4 us
  starting transfers between devices: 16 us -> 11.3 us
    all_to_all x4 -> x7, blocking collectives: 76 us -> 139 us  [exchange(): return lax.all_to_all(values, axes, 0, 0, tiled=True)]
    all_gather x2 -> x1, waiting for transfers between devices: 48.3 us -> 0.02 us  [shards(): stud_rows = lax.all_gather(stud_own, ('x', 'z'), axis=0, tiled=True)]
    unnamed x30 -> x8, local copies, waits for them, and re-layouts: 22.3 us -> 3.23 us
    all_gather x2 -> x1, blocking collectives: 27 us -> 15.9 us  [shards(): return join_pieces(lax.all_gather(back, GROUP, axis=0))]
    pallas_call x9 -> x7, Pallas kernels: 15 us -> 20.7 us  [the longest x1 8.04 us: grad_pieces(): pl.pallas_call(grad_kernel, in_specs=[IN_VMEM, IN_VMEM, IN_VMEM, IN_VMEM,...]
    all_to_all x3 -> x2, starting transfers between devices: 15.9 us -> 11.3 us  [exchange(): return lax.all_to_all(values, axes, 0, 0, tiled=True)]
    all_to_all x3 -> x2, waiting for transfers between devices: 21.3 us -> 17.4 us  [exchange(): return lax.all_to_all(values, axes, 0, 0, tiled=True)]
  transfers between devices with their start and end apart: 5 -> 3, of which waited for: 3 -> 1; matrix products, arithmetic and copies ran while one was open for 0% -> 0% of each run, Pallas kernels for 5% -> 5%
where the time goes in v3:
time: 231 us; the launch traced here: 230 us
  blocking collectives  154 us (67%)
  Pallas kernels  30.4 us (13%)
  waiting for transfers between devices  17.4 us (8%)
  between operations  13.5 us (6%)
  starting transfers between devices  11.3 us (5%)
  local copies, waits for them, and re-layouts  3.37 us (1%)
    all_to_all x7, blocking collectives, exchange(): return lax.all_to_all(values, axes, 0, 0, tiled=True)  139 us
    all_to_all x2, waiting for transfers between devices, exchange(): return lax.all_to_all(values, axes, 0, 0, tiled=True)  17.4 us
    all_gather x1, blocking collectives, shards(): return join_pieces(lax.all_gather(back, GROUP, axis=0))  15.9 us
    all_to_all x2, starting transfers between devices, exchange(): return lax.all_to_all(values, axes, 0, 0, tiled=True)  11.3 us
    pallas_call x1, Pallas kernels, grad_pieces(): pl.pallas_call(grad_kernel, in_specs=[IN_VMEM, IN_VMEM, IN_VMEM, IN_VMEM,...  8.04 us
    pallas_call x3, Pallas kernels, row_pass(): pl.pallas_call(functools.partial(row_pass_kernel, stage), in_specs=[IN_VM...  7.67 us
    pallas_call x1, Pallas kernels, student_expo(): pl.pallas_call(student_kernel, in_specs=[IN_HBM, IN_VMEM], out_specs=(IN_...  4.72 us
  transfers between devices with their start and end apart: 3, of which 1 were waited for; matrix products, arithmetic and copies ran while one was open for 0% of the time, Pallas kernels for 5%

profile of v3, /device:TPU:1, one launch (start us, length us, event | category | flops | bytes accessed | tf_op | source)
XLA Modules:
  0.0 230.4 jit_solution(8552353857449982472)
XLA Ops:
  6.5 0.0 all-gather.3.cloned.1.call-start
  6.5 2.3 %prepare.1 = (bf16[8,128,256]{2,1,0:T(8,128)(2,1)S(1)}, bf16[128,256]{1,0:T(8,128)(2,1)}, bf16[256,1024]{1,0:T(8,128)(2,1)S(1)}, bf16[256,1024]{1,0:T(8,128)(2,1)S(1)}) custom-call(s32[1,128]{1,0:T(1,128)} %bitcast.8, bf16[256,256]{1,0:T(8,128)(2,1)} %refs_1_.1, bf16[256,256]{1,0:T(8,128)(2,1)} %refs_2_.1, bf16[256,1024]{1,0:T(8,128)(2,1)} %refs_3_.1, ...), custom_call_target="tpu_custom_call" | custom-call | tf_op jit(solution)/shard_map/prepare/pallas_call | solution.py:74
  8.9 0.0 all-gather.3.cloned.1.call-update
  8.9 26.7 %all_to_all.45 = bf16[8,128,256]{2,1,0:T(8,128)(2,1)S(1)} all-to-all(bf16[8,128,256]{2,1,0:T(8,128)(2,1)S(1)} %get-tuple-element.14), channel_id=1, replica_groups=mesh['y'=8,'core'=2,'z'=8,'x'=4] {'z'}, dimensions={0} | all-to-all | bytes 1048576 | tf_op jit(solution)/shard_map/all_to_all | solution.py:374
  35.6 0.1 broadcast_in_dim.8
  35.7 27.9 %all_to_all.46 = bf16[4,1024,256]{2,1,0:T(8,128)(2,1)S(1)} all-to-all(bf16[4,1024,256]{2,1,0:T(8,128)(2,1)S(1)} %broadcast_in_dim.8), channel_id=1, replica_groups=mesh['y'=8,'core'=2,'z'=8,'x'=4] {'x'}, dimensions={0} | all-to-all | bytes 4194304 | tf_op jit(solution)/shard_map/all_to_all | solution.py:374
  63.6 2.4 %first_codes.1 = (bf16[4096,1024]{1,0:T(8,128)(2,1)S(1)}, f32[16,8,128]{2,1,0:T(8,128)S(1)}) custom-call(bf16[4096,256]{1,0:T(8,128)(2,1)S(1)} %bitcast.5, bf16[256,1024]{1,0:T(8,128)(2,1)S(1)} %get-tuple-element.15.protos_ref), custom_call_target="tpu_custom_call" | custom-call | flops 2147483648 | bytes 8388608 | tf_op jit(solution)/shard_map/first_codes/pallas_call | solution.py:140
  66.0 0.0 copy-start
  66.0 18.2 %all_to_all.47.refs_0_ = f32[16,8,128]{2,1,0:T(8,128)S(1)} all-to-all(f32[16,8,128]{2,1,0:T(8,128)S(1)} %get-tuple-element.16), channel_id=1, replica_groups=mesh['y'=8,'core'=2,'z'=8,'x'=4] {'y','core'}, dimensions={0} | all-to-all | bytes 131072 | tf_op jit(solution)/shard_map/all_to_all | solution.py:374
  84.2 1.7 row_pass.3
  86.0 16.6 %all_to_all.48.recv_ref = bf16[32,32,128]{2,1,0:T(8,128)(2,1)S(1)} all-to-all(bf16[32,32,128]{2,1,0:T(8,128)(2,1)S(1)} %row_pass.3), channel_id=1, replica_groups=mesh['y'=8,'core'=2,'z'=8,'x'=4] {'z','x'}, dimensions={0} | all-to-all | bytes 524288 | tf_op jit(solution)/shard_map/all_to_all | solution.py:374
  102.6 0.0 copy-done
  102.6 2.3 col_pass.2
  104.9 5.6 %all-to-all-start.4 = ((f32[16,8,128]{2,1,0:T(8,128)}), f32[16,8,128]{2,1,0:T(8,128)S(1)}, u32[]{:S(2)}, u32[]{:S(2)}) async-start(f32[16,8,128]{2,1,0:T(8,128)} %col_pass.2), calls=%async_computation.4 | async-start | bytes 131072 | tf_op jit(solution)/shard_map/all_to_all | solution.py:374
  110.5 0.0 all-gather.3.cloned.1.call-done.rows_ref
  110.5 4.7 %student_expo.1 = (bf16[4096,1024]{1,0:T(8,128)(2,1)S(1)}, f32[32,128]{1,0:T(8,128)S(1)}, bf16[256,4096]{1,0:T(8,128)(2,1)S(1)}) custom-call(bf16[4096,256]{1,0:T(8,128)(2,1)} %all-gather.3.cloned.1.call-done.rows_ref, bf16[256,1024]{1,0:T(8,128)(2,1)S(1)} %get-tuple-element.19.protos_ref), custom_call_target="tpu_custom_call" | custom-call | flops 2147483648 | bytes 8388608 | tf_op jit(solution)/shard_map/student_expo/pallas_call | solution.py:263
  115.3 0.0 copy-start.2
  115.3 3.2 %copy-done.2 = bf16[4096,1024]{1,0:T(8,128)(2,1)} copy-done((bf16[4096,1024]{1,0:T(8,128)(2,1)}, bf16[4096,1024]{1,0:T(8,128)(2,1)S(1)}, u32[]{:S(2)}) %copy-start.2) | copy-done | bytes 8388632
  118.5 0.0 all-to-all-done.4.refs_0_
  118.5 0.0 copy-start.1
  118.5 4.2 %row_pass.4 = bf16[32,40,128]{2,1,0:T(8,128)(2,1)S(1)} custom-call(f32[16,8,128]{2,1,0:T(8,128)S(1)} %all-to-all-done.4.refs_0_, bf16[4096,1024]{1,0:T(8,128)(2,1)} %copy-done, f32[32,128]{1,0:T(8,128)S(1)} %get-tuple-element.20.refs_2_), custom_call_target="tpu_custom_call" | custom-call | flops 8388608 | bytes 8388608 | tf_op jit(solution)/shard_map/row_pass/pallas_call | solution.py:194
  122.7 16.0 %all_to_all.49.recv_ref.refs_2_ = bf16[32,40,128]{2,1,0:T(8,128)(2,1)S(1)} all-to-all(bf16[32,40,128]{2,1,0:T(8,128)(2,1)S(1)} %row_pass.4), channel_id=1, replica_groups=mesh['y'=8,'core'=2,'z'=8,'x'=4] {'z','x'}, dimensions={0} | all-to-all | bytes 655360 | tf_op jit(solution)/shard_map/all_to_all | solution.py:374
  138.6 0.0 copy-done.1
  138.7 1.7 col_pass.3
  140.3 16.8 %all_to_all.50.refs_0_.cols_ref = f32[16,8,128]{2,1,0:T(8,128)S(1)} all-to-all(f32[16,8,128]{2,1,0:T(8,128)S(1)} %col_pass.3), channel_id=1, replica_groups=mesh['y'=8,'core'=2,'z'=8,'x'=4] {'y','core'}, dimensions={0} | all-to-all | bytes 131072 | tf_op jit(solution)/shard_map/all_to_all | solution.py:374
  157.1 1.8 row_pass.5
  158.9 16.5 %all_to_all.51.recv_ref = bf16[32,40,128]{2,1,0:T(8,128)(2,1)S(1)} all-to-all(bf16[32,40,128]{2,1,0:T(8,128)(2,1)S(1)} %row_pass.5), channel_id=1, replica_groups=mesh['y'=8,'core'=2,'z'=8,'x'=4] {'z','x'}, dimensions={0} | all-to-all | bytes 655360 | tf_op jit(solution)/shard_map/all_to_all | solution.py:374
  175.3 0.0 copy-start.3
  175.3 8.0 %grad_pieces.1 = bf16[16,128,128]{2,1,0:T(8,128)(2,1)} custom-call(bf16[32,40,128]{2,1,0:T(8,128)(2,1)S(1)} %all_to_all.51.recv_ref, f32[16,8,128]{2,1,0:T(8,128)S(1)} %all_to_all.50.refs_0_.cols_ref, bf16[256,4096]{1,0:T(8,128)(2,1)S(1)} %get-tuple-element.21.turned_ref, bf16[4096,1024]{1,0:T(8,128)(2,1)S(1)} %copy-done.1, bf16[4096,1024]{1,0:T(8,128)(2,1)} %copy-done.2), custom_call_target="tpu_custom_call" | custom-call | flops 4294967296 | bytes 16777216 | tf_op jit(solution)/shard_map/grad_pieces/pallas_call | solution.py:312
  183.4 5.7 %all-to-all-start.8 = ((bf16[16,128,128]{2,1,0:T(8,128)(2,1)}), bf16[16,128,128]{2,1,0:T(8,128)(2,1)S(1)}, u32[]{:S(2)}, u32[]{:S(2)}) async-start(bf16[16,128,128]{2,1,0:T(8,128)(2,1)} %grad_pieces.1), calls=%async_computation.8 | async-start | bytes 1048576 | tf_op jit(solution)/shard_map/all_to_all | solution.py:374
  189.0 17.3 %all-to-all-done.8.recv_ref = bf16[16,128,128]{2,1,0:T(8,128)(2,1)S(1)} async-done(((bf16[16,128,128]{2,1,0:T(8,128)(2,1)}), bf16[16,128,128]{2,1,0:T(8,128)(2,1)S(1)}, u32[]{:S(2)}, u32[]{:S(2)}) %all-to-all-start.8) | async-done | bytes 524320 | tf_op jit(solution)/shard_map/all_to_all | solution.py:374
  206.4 0.0 copy-done.3
  206.4 0.3 weight_back.1
  206.7 15.9 %all-gather = bf16[2048,128]{1,0:T(8,128)(2,1)S(1)} all-gather(bf16[128,128]{1,0:T(8,128)(2,1)S(1)} %weight_back.1), channel_id=2, replica_groups=mesh['y'=8,'core'=2,'z'=8,'x'=4] {'y','core'}, dimensions={0}, use_global_device_ids=true | all-gather | bytes 557056 | tf_op jit(solution)/shard_map/all_gather | solution.py:399
  222.6 1.0 join_pieces.1
Async XLA Ops:
  6.5 104.0 %all-gather.3.cloned.1.call-start = ((), (), s32[]{:S(2)}) async-start(), calls=%async_computation.9 | async-start | bytes 2162688 | tf_op jit(solution)/shard_map/all_gather | solution.py:383
  66.0 36.6 %copy-start = (bf16[4096,1024]{1,0:T(8,128)(2,1)}, bf16[4096,1024]{1,0:T(8,128)(2,1)S(1)}, u32[]{:S(2)}) copy-start(bf16[4096,1024]{1,0:T(8,128)(2,1)S(1)} %get-tuple-element.17.refs_1_.codes_ref) | copy-start | bytes 25165828
  104.9 13.6 %all-to-all-start.4 = ((f32[16,8,128]{2,1,0:T(8,128)}), f32[16,8,128]{2,1,0:T(8,128)S(1)}, u32[]{:S(2)}, u32[]{:S(2)}) async-start(f32[16,8,128]{2,1,0:T(8,128)} %col_pass.2), calls=%async_computation.4 | async-start | bytes 131072 | tf_op jit(solution)/shard_map/all_to_all | solution.py:374
  115.3 3.2 %copy-start.2 = (bf16[4096,1024]{1,0:T(8,128)(2,1)}, bf16[4096,1024]{1,0:T(8,128)(2,1)S(1)}, u32[]{:S(2)}) copy-start(bf16[4096,1024]{1,0:T(8,128)(2,1)S(1)} %get-tuple-element.22.expo_ref) | copy-start | bytes 25165828
  118.5 20.2 %copy-start.1 = (bf16[4096,1024]{1,0:T(8,128)(2,1)S(1)}, bf16[4096,1024]{1,0:T(8,128)(2,1)}, u32[]{:S(2)}) copy-start(bf16[4096,1024]{1,0:T(8,128)(2,1)} %copy-done) | copy-start | bytes 25165828
  175.3 31.1 %copy-start.3 = (bf16[256,1024]{1,0:T(8,128)(2,1)S(1)}, bf16[256,1024]{1,0:T(8,128)(2,1)}, u32[]{:S(2)}) copy-start(bf16[256,1024]{1,0:T(8,128)(2,1)} %weight_ref.1) | copy-start | bytes 1572868
  183.4 23.0 %all-to-all-start.8 = ((bf16[16,128,128]{2,1,0:T(8,128)(2,1)}), bf16[16,128,128]{2,1,0:T(8,128)(2,1)S(1)}, u32[]{:S(2)}, u32[]{:S(2)}) async-start(bf16[16,128,128]{2,1,0:T(8,128)(2,1)} %grad_pieces.1), calls=%async_computation.8 | async-start | bytes 1048576 | tf_op jit(solution)/shard_map/all_to_all | solution.py:374
Sparse Core Ops, SparseCore 0:
  10.5 87.2 all-gather.2

commit v4 on v3

--- a/solution.py
+++ b/solution.py
@@ -14,7 +14,7 @@
 LANES = 128
 CHUNK = 1024
 EXTRA = 8
-VMEM_LIMIT = 16 * 1024 * 1024
+VMEM_LIMIT = 28 * 1024 * 1024
 LOG2E = math.log2(math.e)
 IN_VMEM = pl.BlockSpec(memory_space=pltpu.VMEM)
 IN_HBM = pl.BlockSpec(memory_space=pltpu.HBM)
@@ -97,13 +97,7 @@
 def spread_cols(total, cols_ref):
     for j in range(cols_ref.shape[1]):
         part = total[:, j * LANES : (j + 1) * LANES]
-        cols_ref[:, j, :] = jnp.broadcast_to(part, (cols_ref.shape[0], LANES))
-
-
-def fetch(source, target, sem):
-    copy = pltpu.make_async_copy(source, target, sem)
-    copy.start()
-    copy.wait()
+        cols_ref[:, j, :] = jnp.broadcast_to(part, (cols_ref.shape[0], LANES)).astype(bf16)
 
 
 class Blocks:
@@ -143,7 +137,7 @@
         out_specs=(IN_VMEM, IN_VMEM),
         out_shape=(
             pltpu.VMEM((count, columns), bf16),
-            jax.ShapeDtypeStruct((groups, columns // LANES, LANES), f32),
+            jax.ShapeDtypeStruct((groups, columns // LANES, LANES), bf16),
         ),
         compiler_params=params(),
         cost_estimate=cost(2 * count * width * columns, count * columns, 2 * count * columns),
@@ -165,7 +159,7 @@
     blocks = Blocks(codes_ref, *held)
     tiles = recv_ref.shape[1]
     lines = CHUNK // LANES
-    scale = lane_row(1.0 / jnp.sum(recv_ref[...], axis=0), 0, tiles)
+    scale = lane_row(1.0 / jnp.sum(recv_ref[...].astype(f32), axis=0), 0, tiles)
     for i in range(blocks.count):
         blocks.ready(i)
         part = None
@@ -233,28 +227,38 @@
         col_pass_kernel,
         in_specs=[IN_VMEM, IN_VMEM],
         out_specs=IN_VMEM,
-        out_shape=jax.ShapeDtypeStruct((groups, columns // LANES, LANES), f32),
+        out_shape=jax.ShapeDtypeStruct((groups, columns // LANES, LANES), bf16),
         compiler_params=params(),
         cost_estimate=cost(2 * count * columns, 0, 2 * count * columns),
         name="col_pass",
     )(recv, codes)
 
 
-def student_kernel(rows_ref, protos_ref, expo_ref, norm_ref, turned_ref, held_ref, sem):
-    fetch(rows_ref, held_ref, sem)
+def student_kernel(rows_ref, protos_ref, expo_ref, norm_ref, turned_ref, held, made, turned, in_sems, out_sems):
     count, columns = expo_ref.shape
     lines = CHUNK // LANES
-    for i in range(count // CHUNK):
-        span = slice(i * CHUNK, (i + 1) * CHUNK)
-        rows = held_ref[span, :]
+    spans = [pl.ds(i * CHUNK, CHUNK) for i in range(count // CHUNK)]
+    fetches = [pltpu.make_async_copy(rows_ref.at[span, :], held.at[span, :], in_sems.at[i]) for i, span in enumerate(spans)]
+    for fetch in fetches:
+        fetch.start()
+    sends = []
+    for i, span in enumerate(spans):
+        fetches[i].wait()
+        rows = held[span, :]
         scores = jnp.dot(rows, protos_ref[...], preferred_element_type=f32)
         expo = jnp.exp2(scores * (student_scale * LOG2E))
-        expo_ref[span, :] = expo.astype(bf16)
+        made[span, :] = expo.astype(bf16)
+        sends.append(pltpu.make_async_copy(made.at[span, :], expo_ref.at[span, :], out_sems.at[2 * i]))
+        sends[-1].start()
         part = expo[:, :LANES]
         for j in range(1, columns // LANES):
             part = part + expo[:, j * LANES : (j + 1) * LANES]
         norm_ref[i * lines : (i + 1) * lines, :] = sum_lanes(part)
-        turned_ref[:, span] = rows.T
+        turned[:, span] = rows.T
+        sends.append(pltpu.make_async_copy(turned.at[:, span], turned_ref.at[:, span], out_sems.at[2 * i + 1]))
+        sends[-1].start()
+    for send in sends:
+        send.wait()
 
 
 def student_expo(rows, protos):
@@ -263,33 +267,31 @@
     return pl.pallas_call(
         student_kernel,
         in_specs=[IN_HBM, IN_VMEM],
-        out_specs=(IN_VMEM, IN_VMEM, IN_VMEM),
+        out_specs=(IN_HBM, IN_VMEM, IN_HBM),
         out_shape=(
-            jax.ShapeDtypeStruct((count, columns), bf16),
+            pltpu.HBM((count, columns), bf16),
             jax.ShapeDtypeStruct((count // LANES, LANES), f32),
-            jax.ShapeDtypeStruct((width, count), bf16),
+            pltpu.HBM((width, count), bf16),
         ),
-        scratch_shapes=[pltpu.VMEM((count, width), bf16), pltpu.SemaphoreType.DMA],
+        scratch_shapes=[
+            pltpu.VMEM((count, width), bf16),
+            pltpu.VMEM((count, columns), bf16),
+            pltpu.VMEM((width, count), bf16),
+            pltpu.SemaphoreType.DMA((count // CHUNK,)),
+            pltpu.SemaphoreType.DMA((2 * count // CHUNK,)),
+        ],
         compiler_params=params(),
         cost_estimate=cost(2 * count * width * columns, count * columns, 2 * count * columns),
         name="student_expo",
     )(in_hbm(rows), protos)
 
 
-def scaled_product(scale, turned_ref, blocks):
-    lines = CHUNK // LANES
-    total = None
-    for i in range(blocks.count):
-        span = slice(i * CHUNK, (i + 1) * CHUNK)
-        turned = (turned_ref[:, span].astype(f32) * lane_row(scale, i * lines, lines)).astype(bf16)
-        blocks.ready(i)
-        term = jnp.dot(turned, blocks.block[span, :], preferred_element_type=f32)
-        total = term if total is None else total + term
-    return total
-
-
-def grad_kernel(recv_ref, cols_ref, turned_ref, codes_ref, expo_ref, out_ref, *held):
-    stud_blocks = Blocks(expo_ref, *held)
+def scaled_product(scale, turned_ref, codes_ref):
+    turned = (turned_ref[...].astype(f32) * lane_row(scale, 0, scale.shape[0])).astype(bf16)
+    return jnp.dot(turned, codes_ref[...], preferred_element_type=f32)
+
+
+def grad_kernel(recv_ref, cols_ref, turned_ref, codes_ref, expo_ref, out_ref):
     members = recv_ref.shape[0]
     lines = codes_ref.shape[0] // LANES
     row_scale = 1.0 / jnp.sum(recv_ref[:, :lines, :].astype(f32), axis=0)
@@ -297,10 +299,9 @@
         [recv_ref[m, lines : lines + 1, :].astype(f32) + recv_ref[m, lines + 1 : lines + 2, :].astype(f32) for m in range(members)],
         axis=0,
     )
-    teach = scaled_product(row_scale, turned_ref, Blocks(codes_ref))
-    mass = jnp.sum(cols_ref[...], axis=0)
-    teach = teach * lane_row(1.0 / mass, 0, cols_ref.shape[1])
-    grad = grad_factor * (scaled_product(1.0 / norm, turned_ref, stud_blocks) - teach)
+    mass = jnp.sum(cols_ref[...].astype(f32), axis=0)
+    teach = scaled_product(row_scale, turned_ref, codes_ref) * lane_row(1.0 / mass, 0, cols_ref.shape[1])
+    grad = grad_factor * (scaled_product(1.0 / norm, turned_ref, expo_ref) - teach)
     for piece in range(out_ref.shape[0]):
         out_ref[piece] = pack_piece(grad, piece, out_ref.shape[0]).astype(bf16)
 
@@ -311,14 +312,13 @@
     pieces = cols.shape[0]
     return pl.pallas_call(
         grad_kernel,
-        in_specs=[IN_VMEM, IN_VMEM, IN_VMEM, IN_VMEM, IN_HBM],
+        in_specs=[IN_VMEM] * 5,
         out_specs=IN_VMEM,
         out_shape=jax.ShapeDtypeStruct((pieces, width // 2, 2 * columns // pieces), bf16),
-        scratch_shapes=held_blocks(expo.shape),
         compiler_params=params(),
         cost_estimate=cost(4 * count * width * columns, 0, 4 * count * columns),
         name="grad_pieces",
-    )(recv, cols, turned, codes, in_hbm(expo))
+    )(recv, cols, turned, codes, expo)
 
 
 def back_kernel(index_ref, recv_ref, weight_ref, out_ref):

time: 231 us -> 226 us (0.978)
  local copies, waits for them, and re-layouts: 3.37 us -> 0.16 us
    unnamed x8 -> x12, local copies, waits for them, and re-layouts: 3.23 us -> 0.03 us
    pallas_call x1, Pallas kernels: 8.04 us -> 5.39 us  [grad_pieces(): pl.pallas_call(grad_kernel, in_specs=[IN_VMEM] * 5, out_specs=IN_VMEM, ou...]
  transfers between devices with their start and end apart: 3 -> 3, of which waited for: 1 -> 2; matrix products, arithmetic and copies ran while one was open for 0% -> 0% of each run, Pallas kernels for 5% -> 6%
where the time goes in v4:
time: 226 us; the launch traced here: 225 us
  blocking collectives  153 us (68%)
  Pallas kernels  29.1 us (13%)
  waiting for transfers between devices  18.7 us (8%)
  between operations  13.5 us (6%)
  starting transfers between devices  11.2 us (5%)
    all_to_all x7, blocking collectives, exchange(): return lax.all_to_all(values, axes, 0, 0, tiled=True)  137 us
    all_to_all x2, waiting for transfers between devices, exchange(): return lax.all_to_all(values, axes, 0, 0, tiled=True)  18.7 us
    all_gather x1, blocking collectives, shards(): return join_pieces(lax.all_gather(back, GROUP, axis=0))  15.9 us
    all_to_all x2, starting transfers between devices, exchange(): return lax.all_to_all(values, axes, 0, 0, tiled=True)  11.2 us
    pallas_call x3, Pallas kernels, row_pass(): pl.pallas_call(functools.partial(row_pass_kernel, stage), in_specs=[IN_VM...  7.68 us
    pallas_call x1, Pallas kernels, student_expo(): pl.pallas_call(student_kernel, in_specs=[IN_HBM, IN_VMEM], out_specs=(IN_...  6.02 us
    pallas_call x1, Pallas kernels, grad_pieces(): pl.pallas_call(grad_kernel, in_specs=[IN_VMEM] * 5, out_specs=IN_VMEM, ou...  5.39 us
  transfers between devices with their start and end apart: 3, of which 2 were waited for; matrix products, arithmetic and copies ran while one was open for 0% of the time, Pallas kernels for 6%

profile of v4, /device:TPU:1, one launch (start us, length us, event | category | flops | bytes accessed | tf_op | source)
XLA Modules:
  0.0 225.4 jit_solution(4054613983167848660)
XLA Ops:
  6.5 0.0 all-gather.3.cloned.1.call-start
  6.5 2.3 %prepare.1 = (bf16[8,128,256]{2,1,0:T(8,128)(2,1)S(1)}, bf16[128,256]{1,0:T(8,128)(2,1)}, bf16[256,1024]{1,0:T(8,128)(2,1)S(1)}, bf16[256,1024]{1,0:T(8,128)(2,1)S(1)}) custom-call(s32[1,128]{1,0:T(1,128)} %bitcast.10, bf16[256,256]{1,0:T(8,128)(2,1)} %refs_1_.1, bf16[256,256]{1,0:T(8,128)(2,1)} %refs_2_.1, bf16[256,1024]{1,0:T(8,128)(2,1)} %refs_3_.1, ...), custom_call_target="tpu_custom_call" | custom-call | tf_op jit(solution)/shard_map/prepare/pallas_call | solution.py:74
  8.9 0.0 all-gather.3.cloned.1.call-update
  8.9 26.7 %all_to_all.45 = bf16[8,128,256]{2,1,0:T(8,128)(2,1)S(1)} all-to-all(bf16[8,128,256]{2,1,0:T(8,128)(2,1)S(1)} %get-tuple-element.14), channel_id=1, replica_groups=mesh['y'=8,'core'=2,'z'=8,'x'=4] {'z'}, dimensions={0} | all-to-all | bytes 1048576 | tf_op jit(solution)/shard_map/all_to_all | solution.py:374
  35.6 0.1 broadcast_in_dim.8
  35.7 27.9 %all_to_all.46 = bf16[4,1024,256]{2,1,0:T(8,128)(2,1)S(1)} all-to-all(bf16[4,1024,256]{2,1,0:T(8,128)(2,1)S(1)} %broadcast_in_dim.8), channel_id=1, replica_groups=mesh['y'=8,'core'=2,'z'=8,'x'=4] {'x'}, dimensions={0} | all-to-all | bytes 4194304 | tf_op jit(solution)/shard_map/all_to_all | solution.py:374
  63.6 2.4 %first_codes.1 = (bf16[4096,1024]{1,0:T(8,128)(2,1)S(1)}, bf16[16,8,128]{2,1,0:T(8,128)(2,1)S(1)}) custom-call(bf16[4096,256]{1,0:T(8,128)(2,1)S(1)} %bitcast.7, bf16[256,1024]{1,0:T(8,128)(2,1)S(1)} %get-tuple-element.15.protos_ref), custom_call_target="tpu_custom_call" | custom-call | flops 2147483648 | bytes 8388608 | tf_op jit(solution)/shard_map/first_codes/pallas_call | solution.py:134
  66.0 0.0 copy-start
  66.0 17.8 %all_to_all.47.refs_0_ = bf16[16,8,128]{2,1,0:T(8,128)(2,1)S(1)} all-to-all(bf16[16,8,128]{2,1,0:T(8,128)(2,1)S(1)} %get-tuple-element.16), channel_id=1, replica_groups=mesh['y'=8,'core'=2,'z'=8,'x'=4] {'y','core'}, dimensions={0} | all-to-all | bytes 65536 | tf_op jit(solution)/shard_map/all_to_all | solution.py:374
  83.8 1.7 row_pass.3
  85.6 17.0 %all_to_all.48.recv_ref = bf16[32,32,128]{2,1,0:T(8,128)(2,1)S(1)} all-to-all(bf16[32,32,128]{2,1,0:T(8,128)(2,1)S(1)} %row_pass.3), channel_id=1, replica_groups=mesh['y'=8,'core'=2,'z'=8,'x'=4] {'z','x'}, dimensions={0} | all-to-all | bytes 524288 | tf_op jit(solution)/shard_map/all_to_all | solution.py:374
  102.6 0.0 copy-done
  102.6 2.3 %col_pass.2 = bf16[16,8,128]{2,1,0:T(8,128)(2,1)} custom-call(bf16[32,32,128]{2,1,0:T(8,128)(2,1)S(1)} %all_to_all.48.recv_ref, bf16[4096,1024]{1,0:T(8,128)(2,1)S(1)} %get-tuple-element.17.refs_1_.codes_ref), custom_call_target="tpu_custom_call" | custom-call | flops 8388608 | bytes 8388608 | tf_op jit(solution)/shard_map/col_pass/pallas_call | solution.py:226
  104.9 5.4 %all-to-all-start.4 = ((bf16[16,8,128]{2,1,0:T(8,128)(2,1)}), bf16[16,8,128]{2,1,0:T(8,128)(2,1)S(1)}, u32[]{:S(2)}, u32[]{:S(2)}) async-start(bf16[16,8,128]{2,1,0:T(8,128)(2,1)} %col_pass.2), calls=%async_computation.4 | async-start | bytes 65536 | tf_op jit(solution)/shard_map/all_to_all | solution.py:374
  110.3 0.0 all-gather.3.cloned.1.call-done.rows_ref
  110.3 6.0 %student_expo.1 = (bf16[4096,1024]{1,0:T(8,128)(2,1)}, f32[32,128]{1,0:T(8,128)S(1)}, bf16[256,4096]{1,0:T(8,128)(2,1)}) custom-call(bf16[4096,256]{1,0:T(8,128)(2,1)} %all-gather.3.cloned.1.call-done.rows_ref, bf16[256,1024]{1,0:T(8,128)(2,1)S(1)} %get-tuple-element.19.protos_ref), custom_call_target="tpu_custom_call" | custom-call | flops 2147483648 | bytes 8388608 | tf_op jit(solution)/shard_map/student_expo/pallas_call | solution.py:267
  116.4 1.3 all-to-all-done.4.refs_0_
  117.7 0.0 copy-start.1
  117.7 4.2 %row_pass.4 = bf16[32,40,128]{2,1,0:T(8,128)(2,1)S(1)} custom-call(bf16[16,8,128]{2,1,0:T(8,128)(2,1)S(1)} %all-to-all-done.4.refs_0_, bf16[4096,1024]{1,0:T(8,128)(2,1)} %copy-done, f32[32,128]{1,0:T(8,128)S(1)} %get-tuple-element.20.refs_2_), custom_call_target="tpu_custom_call" | custom-call | flops 8388608 | bytes 8388608 | tf_op jit(solution)/shard_map/row_pass/pallas_call | solution.py:188
  121.9 15.9 %all_to_all.49.recv_ref.refs_2_ = bf16[32,40,128]{2,1,0:T(8,128)(2,1)S(1)} all-to-all(bf16[32,40,128]{2,1,0:T(8,128)(2,1)S(1)} %row_pass.4), channel_id=1, replica_groups=mesh['y'=8,'core'=2,'z'=8,'x'=4] {'z','x'}, dimensions={0} | all-to-all | bytes 655360 | tf_op jit(solution)/shard_map/all_to_all | solution.py:374
  137.8 0.0 copy-done.1
  137.8 0.0 slice-start
  137.8 1.7 col_pass.3
  139.5 15.1 %all_to_all.50.refs_0_.cols_ref = bf16[16,8,128]{2,1,0:T(8,128)(2,1)S(1)} all-to-all(bf16[16,8,128]{2,1,0:T(8,128)(2,1)S(1)} %col_pass.3), channel_id=1, replica_groups=mesh['y'=8,'core'=2,'z'=8,'x'=4] {'y','core'}, dimensions={0} | all-to-all | bytes 65536 | tf_op jit(solution)/shard_map/all_to_all | solution.py:374
  154.6 0.0 slice-start.1
  154.6 0.0 copy-start.2
  154.6 1.8 row_pass.5
  156.4 16.4 %all_to_all.51.recv_ref = bf16[32,40,128]{2,1,0:T(8,128)(2,1)S(1)} all-to-all(bf16[32,40,128]{2,1,0:T(8,128)(2,1)S(1)} %row_pass.5), channel_id=1, replica_groups=mesh['y'=8,'core'=2,'z'=8,'x'=4] {'z','x'}, dimensions={0} | all-to-all | bytes 655360 | tf_op jit(solution)/shard_map/all_to_all | solution.py:374
  172.8 0.0 slice-done
  172.8 0.0 slice-done.1
  172.8 0.0 copy-done.2
  172.8 0.0 copy-start.3
  172.8 5.4 %grad_pieces.1 = bf16[16,128,128]{2,1,0:T(8,128)(2,1)} custom-call(bf16[32,40,128]{2,1,0:T(8,128)(2,1)S(1)} %all_to_all.51.recv_ref, bf16[16,8,128]{2,1,0:T(8,128)(2,1)S(1)} %all_to_all.50.refs_0_.cols_ref, bf16[256,4096]{1,0:T(8,128)(2,1)S(1)} %copy-done.2, bf16[4096,1024]{1,0:T(8,128)(2,1)S(1)} %copy-done.1, bf16[4096,1024]{1,0:T(8,128)(2,1)S(1)} %bitcast.6), custom_call_target="tpu_custom_call" | custom-call | flops 4294967296 | bytes 16777216 | tf_op jit(solution)/shard_map/grad_pieces/pallas_call | solution.py:313
  178.2 5.8 %all-to-all-start.8 = ((bf16[16,128,128]{2,1,0:T(8,128)(2,1)}), bf16[16,128,128]{2,1,0:T(8,128)(2,1)S(1)}, u32[]{:S(2)}, u32[]{:S(2)}) async-start(bf16[16,128,128]{2,1,0:T(8,128)(2,1)} %grad_pieces.1), calls=%async_computation.8 | async-start | bytes 1048576 | tf_op jit(solution)/shard_map/all_to_all | solution.py:374
  184.0 17.3 %all-to-all-done.8.recv_ref = bf16[16,128,128]{2,1,0:T(8,128)(2,1)S(1)} async-done(((bf16[16,128,128]{2,1,0:T(8,128)(2,1)}), bf16[16,128,128]{2,1,0:T(8,128)(2,1)S(1)}, u32[]{:S(2)}, u32[]{:S(2)}) %all-to-all-start.8) | async-done | bytes 524320 | tf_op jit(solution)/shard_map/all_to_all | solution.py:374
  201.4 0.0 copy-done.3
  201.4 0.3 weight_back.1
  201.6 15.9 %all-gather = bf16[2048,128]{1,0:T(8,128)(2,1)S(1)} all-gather(bf16[128,128]{1,0:T(8,128)(2,1)S(1)} %weight_back.1), channel_id=2, replica_groups=mesh['y'=8,'core'=2,'z'=8,'x'=4] {'y','core'}, dimensions={0}, use_global_device_ids=true | all-gather | bytes 557056 | tf_op jit(solution)/shard_map/all_gather | solution.py:399
  217.5 1.0 join_pieces.1
  (1 shorter events, 0.0 us)
Async XLA Ops:
  6.5 103.8 %all-gather.3.cloned.1.call-start = ((), (), s32[]{:S(2)}) async-start(), calls=%async_computation.9 | async-start | bytes 2162688 | tf_op jit(solution)/shard_map/all_gather | solution.py:383
  66.0 36.5 %copy-start = (bf16[4096,1024]{1,0:T(8,128)(2,1)}, bf16[4096,1024]{1,0:T(8,128)(2,1)S(1)}, u32[]{:S(2)}) copy-start(bf16[4096,1024]{1,0:T(8,128)(2,1)S(1)} %get-tuple-element.17.refs_1_.codes_ref) | copy-start | bytes 25165828
  104.9 12.8 %all-to-all-start.4 = ((bf16[16,8,128]{2,1,0:T(8,128)(2,1)}), bf16[16,8,128]{2,1,0:T(8,128)(2,1)S(1)}, u32[]{:S(2)}, u32[]{:S(2)}) async-start(bf16[16,8,128]{2,1,0:T(8,128)(2,1)} %col_pass.2), calls=%async_computation.4 | async-start | bytes 65536 | tf_op jit(solution)/shard_map/all_to_all | solution.py:374
  117.7 20.1 %copy-start.1 = (bf16[4096,1024]{1,0:T(8,128)(2,1)S(1)}, bf16[4096,1024]{1,0:T(8,128)(2,1)}, u32[]{:S(2)}) copy-start(bf16[4096,1024]{1,0:T(8,128)(2,1)} %copy-done) | copy-start | bytes 25165828
  137.8 35.0 %slice-start = ((s8[8388608]{0:T(1024)(128)(4,1)}), s8[4194304]{0:T(1024)(128)(4,1)S(1)}, s32[]{:S(2)}) async-start(s8[8388608]{0:T(1024)(128)(4,1)} %bitcast.5), calls=%async_computation.10 | async-start | bytes 8388608
  154.6 18.2 %slice-start.1 = ((s8[8388608]{0:T(1024)(128)(4,1)}), s8[4194304]{0:T(1024)(128)(4,1)S(1)}, s32[]{:S(2)}) async-start(s8[8388608]{0:T(1024)(128)(4,1)} %bitcast.5), calls=%async_computation.11 | async-start | bytes 8388608
  154.6 18.2 %copy-start.2 = (bf16[256,4096]{1,0:T(8,128)(2,1)S(1)}, bf16[256,4096]{1,0:T(8,128)(2,1)}, u32[]{:S(2)}) copy-start(bf16[256,4096]{1,0:T(8,128)(2,1)} %get-tuple-element.21.turned_ref) | copy-start | bytes 6291460
  172.8 28.6 %copy-start.3 = (bf16[256,1024]{1,0:T(8,128)(2,1)S(1)}, bf16[256,1024]{1,0:T(8,128)(2,1)}, u32[]{:S(2)}) copy-start(bf16[256,1024]{1,0:T(8,128)(2,1)} %weight_ref.1) | copy-start | bytes 1572868
  178.2 23.2 %all-to-all-start.8 = ((bf16[16,128,128]{2,1,0:T(8,128)(2,1)}), bf16[16,128,128]{2,1,0:T(8,128)(2,1)S(1)}, u32[]{:S(2)}, u32[]{:S(2)}) async-start(bf16[16,128,128]{2,1,0:T(8,128)(2,1)} %grad_pieces.1), calls=%async_computation.8 | async-start | bytes 1048576 | tf_op jit(solution)/shard_map/all_to_all | solution.py:374
Sparse Core Ops, SparseCore 0:
  10.5 87.5 all-gather.2

commit v5 on v4

v5 whole, which is shorter than its diff:
```python
import functools
import math

import jax
import jax.numpy as jnp
from jax import lax
from jax.experimental import pallas as pl
from jax.experimental.pallas import tpu as pltpu
from jax.sharding import Mesh
from jax.sharding import PartitionSpec as P

ALL = ("y", "core", "z", "xhi", "xlo")
SHARD = ("z", "xhi", "xlo")
COLUMN_PEERS = ("y", "xhi", "xlo")
ROW_PEERS = ("core", "z")
PIECE_PEERS = ("xlo", "xhi", "y")
SHARD_PEERS = ("xhi", "y")
LANES = 128
CHUNK = 1024
EXTRA = 8
VMEM_LIMIT = 20 * 1024 * 1024
LOG2E = math.log2(math.e)
IN_VMEM = pl.BlockSpec(memory_space=pltpu.VMEM)
IN_HBM = pl.BlockSpec(memory_space=pltpu.HBM)
IN_SMEM = pl.BlockSpec(memory_space=pltpu.SMEM)

epsilon = 1e-06
teacher_scale = 1.0 / 0.07
student_scale = 1.0 / 0.1
grad_factor = 256.0 / 0.1
NT = (((1,), (1,)), ((), ()))
TN = (((0,), (0,)), ((), ()))
f32 = jnp.float32
bf16 = jnp.bfloat16


def params():
    return pltpu.CompilerParams(vmem_limit_bytes=VMEM_LIMIT)


def cost(flops, transcendentals, nbytes):
    return pl.CostEstimate(flops=flops, transcendentals=transcendentals, bytes_accessed=nbytes)


def lane_row(block, start, count):
    return jnp.concatenate([block[start + j : start + j + 1, :] for j in range(count)], axis=1)


def in_hbm(values):
    return pltpu.with_memory_space_constraint(values, pltpu.HBM)


def rows_kernel(mask_ref, teacher_ref, student_ref, out_ref, index_ref, held_ref, sems):
    copies = [
        pltpu.make_async_copy(mask_ref, index_ref, sems.at[0]),
        pltpu.make_async_copy(teacher_ref, held_ref.at[0], sems.at[1]),
        pltpu.make_async_copy(student_ref, held_ref.at[1], sems.at[2]),
    ]
    for copy in copies:
        copy.start()
    copies[0].wait()
    patches = teacher_ref.shape[0]
    count = mask_ref.shape[1]
    chosen = lax.broadcasted_iota(jnp.int32, (patches, count), 0) == index_ref[...]
    chosen = chosen.astype(f32).astype(bf16)
    for part in range(2):
        copies[1 + part].wait()
        rows = lax.dot_general(chosen, held_ref[part], TN, preferred_element_type=f32)
        square = jnp.sum(rows * rows, axis=1, keepdims=True)
        rows = (rows * lax.rsqrt(square + epsilon)).astype(bf16)
        out_ref[:, part * count : (part + 1) * count, :] = jnp.broadcast_to(rows[None], (out_ref.shape[0],) + rows.shape)


def masked_rows(mask, teacher, student, copies):
    count, width = mask.shape[1], teacher.shape[1]
    return pl.pallas_call(
        rows_kernel,
        in_specs=[IN_HBM] * 3,
        out_specs=IN_VMEM,
        out_shape=jax.ShapeDtypeStruct((copies, 2 * count, width), bf16),
        scratch_shapes=[
            pltpu.VMEM(mask.shape, jnp.int32),
            pltpu.VMEM((2,) + teacher.shape, bf16),
            pltpu.SemaphoreType.DMA((3,)),
        ],
        compiler_params=params(),
        name="masked_rows",
    )(in_hbm(mask), in_hbm(teacher), in_hbm(student))


def two_shards(flags_ref, own_ref, near_ref, far_ref, act):
    @pl.when(flags_ref[2] == 1)
    def _():
        act(own_ref, near_ref)

    @pl.when(flags_ref[2] == 0)
    def _():
        act(near_ref, far_ref)


def protos_kernel(flags_ref, own_ref, near_ref, far_ref, teach_ref, stud_ref, held_ref, sems):
    def bring(first, second):
        copies = [
            pltpu.make_async_copy(first, held_ref.at[0], sems.at[0]),
            pltpu.make_async_copy(second, held_ref.at[1], sems.at[1]),
        ]
        for copy in copies:
            copy.start()
        for copy in copies:
            copy.wait()

    two_shards(flags_ref, own_ref, near_ref, far_ref, bring)
    columns = own_ref.shape[2]
    xlo = flags_ref[1]
    for net, out_ref in enumerate((teach_ref, stud_ref)):
        for part, place in ((0, xlo), (1, 1 - xlo)):
            values = held_ref[part, net].astype(f32)
            square = jnp.sum(values * values, axis=0, keepdims=True)
            at = pl.multiple_of(place * columns, columns)
            out_ref[:, pl.ds(at, columns)] = (values * lax.rsqrt(square + epsilon)).astype(bf16)


def prototypes(flags, own, near, far):
    nets, rows, columns = own.shape
    like = jax.ShapeDtypeStruct((rows, 2 * columns), bf16)
    return pl.pallas_call(
        protos_kernel,
        in_specs=[IN_SMEM] + [IN_HBM] * 3,
        out_specs=(IN_VMEM, IN_VMEM),
        out_shape=(like, like),
        scratch_shapes=[pltpu.VMEM((2,) + own.shape, bf16), pltpu.SemaphoreType.DMA((2,))],
        compiler_params=params(),
        name="prototypes",
    )(flags, in_hbm(own), in_hbm(near), in_hbm(far))


def pack_piece(block, piece, pieces):
    rows, columns = block.shape
    width = columns // pieces
    part = block[:, piece * width : (piece + 1) * width]
    return jnp.concatenate([part[: rows // 2], part[rows // 2 :]], axis=1)


def own_piece_kernel(pieces, flags_ref, own_ref, near_ref, out_ref, held_ref, sem):
    index = flags_ref[3]
    columns = pl.ds(pl.multiple_of(index // 2 * LANES, LANES), LANES)

    def bring(first, _):
        copy = pltpu.make_async_copy(first.at[1, :, columns], held_ref, sem)
        copy.start()
        copy.wait()

    two_shards(flags_ref, own_ref, near_ref, near_ref, bring)
    half = own_ref.shape[2] // pieces
    block = held_ref[...].astype(f32)
    block = jnp.where(index % 2 == 0, block[:, :half], block[:, half:])
    rows = block.shape[0] // 2
    out_ref[...] = jnp.concatenate([block[:rows], block[rows:]], axis=1)


def own_piece(flags, own, near, pieces):
    _, rows, columns = own.shape
    return pl.pallas_call(
        functools.partial(own_piece_kernel, pieces),
        in_specs=[IN_SMEM, IN_HBM, IN_HBM],
        out_specs=IN_VMEM,
        out_shape=jax.ShapeDtypeStruct((rows // 2, 2 * columns // pieces), f32),
        scratch_shapes=[pltpu.VMEM((rows, LANES), bf16), pltpu.SemaphoreType.DMA],
        compiler_params=params(),
        name="own_piece",
    )(flags, in_hbm(own), in_hbm(near))


def spread_cols(total, cols_ref):
    for j in range(cols_ref.shape[1]):
        part = total[:, j * LANES : (j + 1) * LANES]
        cols_ref[:, j, :] = jnp.broadcast_to(part, (cols_ref.shape[0], LANES)).astype(bf16)


def net_rows(ref, net):
    blocks, both, width = ref.shape
    count = both // 2
    return ref[:, net * count : (net + 1) * count, :].reshape(blocks * count, width)


def codes_kernel(flags_ref, own_ref, other_ref, protos_ref, codes_ref, cols_ref):
    core = flags_ref[0]
    count = codes_ref.shape[0] // 2
    total = None
    for ref, place in ((own_ref, core), (other_ref, 1 - core)):
        scores = jnp.dot(net_rows(ref, 0), protos_ref[...], preferred_element_type=f32)
        codes = jnp.exp2(scores * (teacher_scale * LOG2E))
        codes_ref[pl.ds(pl.multiple_of(place * count, count), count), :] = codes.astype(bf16)
        sums = jnp.sum(codes, axis=0, keepdims=True)
        total = sums if total is None else total + sums
    spread_cols(total, cols_ref)


def first_codes(flags, own, other, protos, groups):
    blocks, both, width = own.shape
    count = blocks * both
    columns = protos.shape[1]
    return pl.pallas_call(
        codes_kernel,
        in_specs=[IN_SMEM] + [IN_VMEM] * 3,
        out_specs=(IN_VMEM, IN_VMEM),
        out_shape=(
            pltpu.VMEM((count, columns), bf16),
            jax.ShapeDtypeStruct((groups, columns // LANES, LANES), bf16),
        ),
        compiler_params=params(),
        cost_estimate=cost(2 * count * width * columns, count * columns, 2 * count * columns),
        name="first_codes",
    )(flags, own, other, protos)


def sum_lanes(block):
    ones = jnp.ones((16, LANES), bf16)
    sums = lax.dot_general(ones, block.astype(bf16), NT, preferred_element_type=f32)[0:1]
    lines = block.shape[0] // LANES
    return jnp.concatenate([sums[:, j * LANES : (j + 1) * LANES] for j in range(lines)], axis=0)


def row_pass_kernel(stage, *refs):
    recv_ref, codes_ref = refs[:2]
    norm_ref, out_ref = refs[2] if stage else None, refs[-1]
    count = codes_ref.shape[0]
    tiles = recv_ref.shape[1]
    lines = CHUNK // LANES
    scale = lane_row(1.0 / jnp.sum(recv_ref[...].astype(f32), axis=0), 0, tiles)
    for i in range(count // CHUNK):
        part = None
        for j in range(tiles):
            columns = slice(j * LANES, (j + 1) * LANES)
            term = codes_ref[i * CHUNK : (i + 1) * CHUNK, columns].astype(f32) * scale[:, columns]
            part = term if part is None else part + term
        block = jnp.broadcast_to(sum_lanes(part)[None], (out_ref.shape[0], lines, LANES))
        out_ref[:, i * lines : (i + 1) * lines, :] = block.astype(bf16)
    first = count // LANES
    if stage == 1:
        for member in range(out_ref.shape[0]):
            line = norm_ref[member : member + 1, :]
            out_ref[member, first:, :] = jnp.broadcast_to(line, (EXTRA, LANES)).astype(bf16)
    if stage == 2:
        total = jnp.sum(norm_ref[:, first : first + 1, :].astype(f32), axis=0)
        high = total.astype(bf16).astype(f32)
        index = lax.broadcasted_iota(jnp.int32, (EXTRA, LANES), 0)
        extra = jnp.where(index == 0, high, jnp.where(index == 1, total - high, 0.0)).astype(bf16)
        out_ref[:, first:, :] = jnp.broadcast_to(extra[None], (out_ref.shape[0], EXTRA, LANES))


def row_pass(recv, codes, members, norm=None, stage=0):
    count, columns = codes.shape
    lines = count // LANES + (EXTRA if stage else 0)
    return pl.pallas_call(
        functools.partial(row_pass_kernel, stage),
        in_specs=[IN_VMEM] * (3 if stage else 2),
        out_specs=IN_VMEM,
        out_shape=jax.ShapeDtypeStruct((members, lines, LANES), bf16),
        compiler_params=params(),
        cost_estimate=cost(2 * count * columns, 0, 2 * count * columns),
        name="row_pass",
    )(recv, codes, *((norm,) if stage else ()))


def col_pass_kernel(recv_ref, codes_ref, cols_ref):
    count, columns = codes_ref.shape
    lines = CHUNK // LANES
    scale = 1.0 / jnp.sum(recv_ref[:, : count // LANES, :].astype(f32), axis=0)
    ones = jnp.ones((16, LANES), bf16)
    first = lax.broadcasted_iota(jnp.int32, (16, CHUNK), 0) == 0
    spreads = []
    for i in range(count // CHUNK):
        row = jnp.where(first, lane_row(scale, i * lines, lines), 0.0).astype(bf16)
        spreads.append(lax.dot_general(row, ones, TN, preferred_element_type=f32).astype(bf16))
    width = 8 * LANES
    for h in range(columns // width):
        total = jnp.zeros((16, width), f32)
        for i, spread in enumerate(spreads):
            for g in range(lines):
                parts = []
                for j in range(width // LANES):
                    part = None
                    for q in range(LANES // 16):
                        at = g * LANES + q * 16
                        lane = h * width + j * LANES
                        term = codes_ref[i * CHUNK + at : i * CHUNK + at + 16, lane : lane + LANES]
                        term = term * spread[at : at + 16]
                        part = term if part is None else part + term
                    parts.append(part.astype(f32))
                total = total + jnp.concatenate(parts, axis=1)
        total = jnp.sum(total, axis=0, keepdims=True)
        for j in range(width // LANES):
            part = jnp.broadcast_to(total[:, j * LANES : (j + 1) * LANES], (cols_ref.shape[0], LANES))
            cols_ref[:, h * (width // LANES) + j, :] = part.astype(bf16)


def col_pass(recv, codes, groups):
    count, columns = codes.shape
    return pl.pallas_call(
        col_pass_kernel,
        in_specs=[IN_VMEM, IN_VMEM],
        out_specs=IN_VMEM,
        out_shape=jax.ShapeDtypeStruct((groups, columns // LANES, LANES), bf16),
        compiler_params=params(),
        cost_estimate=cost(2 * count * columns, 0, 2 * count * columns),
        name="col_pass",
    )(recv, codes)


def student_kernel(flags_ref, own_ref, other_ref, protos_ref, expo_ref, norm_ref, turned_ref):
    core = flags_ref[0]
    columns = protos_ref.shape[1]
    count = expo_ref.shape[0] // 2
    lines = count // LANES
    for half in range(2):
        rows = jnp.where(core == half, net_rows(own_ref, 1), net_rows(other_ref, 1))
        span = slice(half * count, (half + 1) * count)
        scores = jnp.dot(rows, protos_ref[...], preferred_element_type=f32)
        expo = jnp.exp2(scores * (student_scale * LOG2E))
        expo_ref[span, :] = expo.astype(bf16)
        part = expo[:, :LANES]
        for j in range(1, columns // LANES):
            part = part + expo[:, j * LANES : (j + 1) * LANES]
        norm_ref[half * lines : (half + 1) * lines, :] = sum_lanes(part)
        turned_ref[:, span] = rows.T


def student_expo(flags, own, other, protos):
    blocks, both, width = own.shape
    count = blocks * both
    columns = protos.shape[1]
    return pl.pallas_call(
        student_kernel,
        in_specs=[IN_SMEM] + [IN_VMEM] * 3,
        out_specs=(IN_VMEM,) * 3,
        out_shape=(
            pltpu.VMEM((count, columns), bf16),
            jax.ShapeDtypeStruct((count // LANES, LANES), f32),
            pltpu.VMEM((width, count), bf16),
        ),
        compiler_params=params(),
        cost_estimate=cost(2 * count * width * columns, count * columns, 2 * count * columns),
        name="student_expo",
    )(flags, own, other, protos)


def scaled_product(scale, turned_ref, codes_ref):
    turned = (turned_ref[...].astype(f32) * lane_row(scale, 0, scale.shape[0])).astype(bf16)
    return jnp.dot(turned, codes_ref[...], preferred_element_type=f32)


def grad_kernel(recv_ref, norm_ref, cols_ref, turned_ref, codes_ref, expo_ref, out_ref):
    members = recv_ref.shape[0]
    lines = codes_ref.shape[0] // LANES
    row_scale = 1.0 / jnp.sum(recv_ref[:, :lines, :].astype(f32), axis=0)
    norm = jnp.concatenate(
        [norm_ref[m, lines : lines + 1, :].astype(f32) + norm_ref[m, lines + 1 : lines + 2, :].astype(f32) for m in range(members)],
        axis=0,
    )
    mass = jnp.sum(cols_ref[...].astype(f32), axis=0)
    teach = scaled_product(row_scale, turned_ref, codes_ref) * lane_row(1.0 / mass, 0, cols_ref.shape[1])
    grad = grad_factor * (scaled_product(1.0 / norm, turned_ref, expo_ref) - teach)
    for piece in range(out_ref.shape[0]):
        out_ref[piece] = pack_piece(grad, piece, out_ref.shape[0]).astype(bf16)


def grad_pieces(recv, norm, cols, turned, codes, expo, pieces):
    count, columns = codes.shape
    width = turned.shape[0]
    return pl.pallas_call(
        grad_kernel,
        in_specs=[IN_VMEM] * 6,
        out_specs=IN_VMEM,
        out_shape=jax.ShapeDtypeStruct((pieces, width // 2, 2 * columns // pieces), bf16),
        compiler_params=params(),
        cost_estimate=cost(4 * count * width * columns, 0, 4 * count * columns),
        name="grad_pieces",
    )(recv, norm, cols, turned, codes, expo)


def back_kernel(recv_ref, weight_ref, out_ref):
    grad = jnp.sum(recv_ref[...].astype(f32), axis=0)
    weight = weight_ref[...]
    half = weight.shape[1] // 2

    def column_sum(values):
        total = jnp.sum(values, axis=0, keepdims=True)
        return total + jnp.concatenate([total[:, half:], total[:, :half]], axis=1)

    inverse = lax.rsqrt(column_sum(weight * weight) + epsilon)
    along = column_sum(grad * weight)
    back = (grad * inverse - weight * (inverse * inverse * inverse * along)).astype(bf16)
    out_ref[...] = jnp.broadcast_to(back[None], out_ref.shape)


def weight_back(recv, weight, copies):
    return pl.pallas_call(
        back_kernel,
        in_specs=[IN_VMEM, IN_VMEM],
        out_specs=IN_VMEM,
        out_shape=jax.ShapeDtypeStruct((copies,) + weight.shape, bf16),
        compiler_params=params(),
        name="weight_back",
    )(recv, weight)


def join_kernel(flags_ref, mine_ref, other_ref, out_ref):
    pieces, rows, lanes = mine_ref.shape
    half = lanes // 2

    def join(ref):
        for pair in range(pieces // 2):
            left, right = ref[2 * pair], ref[2 * pair + 1]
            columns = pl.ds(pair * lanes, lanes)
            out_ref[:rows, columns] = jnp.concatenate([left[:, :half], right[:, :half]], axis=1)
            out_ref[rows:, columns] = jnp.concatenate([left[:, half:], right[:, half:]], axis=1)

    @pl.when(flags_ref[2] == 1)
    def _():
        join(mine_ref)

    @pl.when(flags_ref[2] == 0)
    def _():
        join(other_ref)


def join_pieces(flags, mine, other):
    count, rows, lanes = mine.shape
    return pl.pallas_call(
        join_kernel,
        in_specs=[IN_SMEM, IN_VMEM, IN_VMEM],
        out_specs=IN_VMEM,
        out_shape=jax.ShapeDtypeStruct((2 * rows, count * lanes // 2), mine.dtype),
        compiler_params=params(),
        name="join_pieces",
    )(flags, mine, other)


def exchange(values, axes):
    return lax.all_to_all(values, axes, 0, 0, tiled=True)


def shard_permutes(weight):
    axes = ("core", "xhi", "xlo")
    near, far = [], []
    for core in range(2):
        for xhi in range(2):
            for xlo in range(2):
                here = core * 4 + xhi * 2 + xlo
                if xhi == core:
                    near.append((core * 4 + xhi * 2 + 1 - xlo, here))
                else:
                    near.append(((1 - core) * 4 + core * 2 + xlo, here))
                    far.append((core * 4 + core * 2 + 1 - xlo, here))
    return lax.ppermute(weight, axes, near), lax.ppermute(weight, axes, far)


def shards(teacher_patches, student_patches, mask_index, teacher_weight, student_weight):
    size = lax.axis_size
    column_peers, row_peers = size(COLUMN_PEERS), size(ROW_PEERS)
    shard_pieces = size(SHARD_PEERS)
    core, xhi, xlo = lax.axis_index("core"), lax.axis_index("xhi"), lax.axis_index("xlo")
    matched = (core == xhi).astype(jnp.int32)
    flags = jnp.stack([core, xlo, matched, lax.axis_index(SHARD_PEERS)]).astype(jnp.int32)

    weights = jnp.stack([teacher_weight, student_weight])
    near, far = shard_permutes(weights)
    teach_protos, stud_protos = prototypes(flags, weights, near, far)
    line = masked_rows(mask_index.reshape(1, -1), teacher_patches, student_patches, size("z"))
    line = exchange(line, "z")
    line, teach_protos, stud_protos = lax.optimization_barrier((line, teach_protos, stud_protos))
    other = lax.ppermute(line, "core", [(0, 1), (1, 0)])

    codes, cols = first_codes(flags, line, other, teach_protos, column_peers)
    expo, norm, turned = student_expo(flags, line, other, stud_protos)
    cols, expo, norm, turned = lax.optimization_barrier((cols, expo, norm, turned))
    cols = exchange(cols, COLUMN_PEERS)
    rows = exchange(row_pass(cols, codes, row_peers, norm, 1), ROW_PEERS)
    cols = exchange(col_pass(rows, codes, column_peers), COLUMN_PEERS)
    rows = exchange(row_pass(cols, codes, row_peers, rows, 2), ROW_PEERS)
    norm = rows
    cols = exchange(col_pass(rows, codes, column_peers), COLUMN_PEERS)
    rows = exchange(row_pass(cols, codes, row_peers), ROW_PEERS)
    pieces = exchange(grad_pieces(rows, norm, cols, turned, codes, expo, 2 * shard_pieces), PIECE_PEERS)
    weight = own_piece(flags, weights, near, shard_pieces)
    mine = exchange(weight_back(pieces, weight, shard_pieces), SHARD_PEERS)
    other = lax.ppermute(mine, ("core", "xhi"), [(0, 2), (3, 1)])
    return join_pieces(flags, mine, other)


def solution(mesh):
    split = Mesh(mesh.devices.reshape(8, 2, 8, 2, 2), ALL)
    rows = P(ALL, None)
    columns = P(None, SHARD)
    return jax.shard_map(
        shards,
        mesh=split,
        in_specs=(rows, rows, P(ALL), columns, columns),
        out_specs=columns,
        check_vma=False,
    )
```

time: 226 us -> 227 us (level)
  blocking collectives: 153 us -> 106 us
  waiting for transfers between devices: 18.7 us -> 52.5 us
  starting transfers between devices: 11.2 us -> 26.1 us
  between operations: 13.5 us -> 0.13 us
  Pallas kernels: 29.1 us -> 39 us
    all_to_all x7, blocking collectives: 137 us -> 106 us  [exchange(): return lax.all_to_all(values, axes, 0, 0, tiled=True)]
    ppermute x0 -> x4, waiting for transfers between devices: none -> 29.4 us  [the longest x2 22.1 us: shard_permutes(): return (lax.ppermute(weight, axes, near), lax.ppermute(weight, axes, far))]
    all_gather x1 -> x0, blocking collectives: 15.9 us -> none  [shards(): return join_pieces(lax.all_gather(back, GROUP, axis=0))]
    ppermute x0 -> x4, starting transfers between devices: none -> 11.3 us  [the longest x2 6.78 us: shard_permutes(): return (lax.ppermute(weight, axes, near), lax.ppermute(weight, axes, far))]
    pallas_call x3, Pallas kernels: 7.68 us -> 14.4 us  [row_pass(): pl.pallas_call(functools.partial(row_pass_kernel, stage), in_specs=[IN_VM...]
    all_to_all x2, waiting for transfers between devices: 18.7 us -> 23.1 us  [exchange(): return lax.all_to_all(values, axes, 0, 0, tiled=True)]
    all_to_all x2, starting transfers between devices: 11.2 us -> 14.8 us  [exchange(): return lax.all_to_all(values, axes, 0, 0, tiled=True)]
    pallas_call x6 -> x8, Pallas kernels: 17.4 us -> 20.8 us  [the longest x1 5.57 us: grad_pieces(): pl.pallas_call(grad_kernel, in_specs=[IN_VMEM] * 6, out_specs=IN_VMEM, ou...]
  transfers between devices with their start and end apart: 3 -> 6, of which waited for: 2 -> 5; matrix products, arithmetic and copies ran while one was open for 0% -> 1% of each run, Pallas kernels for 6% -> 2%
where the time goes in v5:
time: 227 us; the launch traced here: 226 us
  blocking collectives  106 us (47%)
  waiting for transfers between devices  52.5 us (23%)
  Pallas kernels  39 us (17%)
  starting transfers between devices  26.1 us (11%)
    all_to_all x7, blocking collectives, exchange(): return lax.all_to_all(values, axes, 0, 0, tiled=True)  106 us
    all_to_all x2, waiting for transfers between devices, exchange(): return lax.all_to_all(values, axes, 0, 0, tiled=True)  23.1 us
    ppermute x2, waiting for transfers between devices, shard_permutes(): return (lax.ppermute(weight, axes, near), lax.ppermute(weight, axes, far))  22.1 us
    all_to_all x2, starting transfers between devices, exchange(): return lax.all_to_all(values, axes, 0, 0, tiled=True)  14.8 us
    pallas_call x3, Pallas kernels, row_pass(): pl.pallas_call(functools.partial(row_pass_kernel, stage), in_specs=[IN_VM...  14.4 us
    ppermute x2, starting transfers between devices, shard_permutes(): return (lax.ppermute(weight, axes, near), lax.ppermute(weight, axes, far))  6.78 us
    pallas_call x1, Pallas kernels, grad_pieces(): pl.pallas_call(grad_kernel, in_specs=[IN_VMEM] * 6, out_specs=IN_VMEM, ou...  5.57 us
    ppermute x1, waiting for transfers between devices, shards(): other = lax.ppermute(mine, ('core', 'xhi'), [(0, 2), (3, 1)])  4.98 us
  transfers between devices with their start and end apart: 6, of which 5 were waited for; matrix products, arithmetic and copies ran while one was open for 1% of the time, Pallas kernels for 2%

profile of v5, /device:TPU:1, one launch (start us, length us, event | category | flops | bytes accessed | tf_op | source)
XLA Modules:
  0.0 226.4 jit_solution(7236802809895693359)
XLA Ops:
  0.0 2.5 %masked_rows.1 = bf16[8,256,256]{2,1,0:T(8,128)(2,1)} custom-call(s32[1,128]{1,0:T(1,128)} %bitcast.9, bf16[256,256]{1,0:T(8,128)(2,1)} %teacher_ref.1, bf16[256,256]{1,0:T(8,128)(2,1)} %student_ref.1), custom_call_target="tpu_custom_call" | custom-call | tf_op jit(solution)/shard_map/masked_rows/pallas_call | solution.py:76
  2.5 10.9 %all-to-all-start = ((bf16[8,256,256]{2,1,0:T(8,128)(2,1)}), bf16[8,256,256]{2,1,0:T(8,128)(2,1)S(1)}, u32[]{:S(2)}, u32[]{:S(2)}) async-start(bf16[8,256,256]{2,1,0:T(8,128)(2,1)} %masked_rows.1), calls=%async_computation | async-start | bytes 2097152 | tf_op jit(solution)/shard_map/all_to_all | solution.py:441
  13.4 1.3 pad_maximum_fusion.own_ref
  14.7 0.0 copy-start
  14.7 1.3 collective-permute-start.1
  16.0 5.5 %collective-permute-start = (bf16[2,256,1024]{2,1,0:T(8,128)(2,1)S(1)}, bf16[2,256,1024]{2,1,0:T(8,128)(2,1)}, u32[]{:S(2)}, u32[]{:S(2)}) collective-permute-start(bf16[2,256,1024]{2,1,0:T(8,128)(2,1)S(1)} %pad_maximum_fusion.own_ref), channel_id=1, source_target_pairs={{1,0},{0,1},{32,2},{33,3},{2,32},{3,33},{35,34},{34,35},{5,4},{4,5... | collective-permute-start | bytes 3145736 | tf_op jit(solution)/shard_map/ppermute | solution.py:456
  21.5 0.1 pad_add_fusion.flags_ref
  21.6 19.5 %collective-permute-done.1.far_ref = bf16[2,256,1024]{2,1,0:T(8,128)(2,1)S(1)} collective-permute-done((bf16[2,256,1024]{2,1,0:T(8,128)(2,1)S(1)}, bf16[2,256,1024]{2,1,0:T(8,128)(2,1)S(1)}, u32[]{:S(2)}, u32[]{:S(2)}) %collective-permute-start.1) | collective-permute-done | bytes 1048608 | tf_op jit(solution)/shard_map/ppermute | solution.py:456
  41.0 0.0 copy-done
  41.0 0.0 copy-start.1
  41.0 1.0 copy-done.1
  42.0 2.6 %collective-permute-done.near_ref = bf16[2,256,1024]{2,1,0:T(8,128)(2,1)} collective-permute-done((bf16[2,256,1024]{2,1,0:T(8,128)(2,1)S(1)}, bf16[2,256,1024]{2,1,0:T(8,128)(2,1)}, u32[]{:S(2)}, u32[]{:S(2)}) %collective-permute-start) | collective-permute-done | bytes 1048608 | tf_op jit(solution)/shard_map/ppermute | solution.py:456
  44.7 2.8 %prototypes.1 = (bf16[256,2048]{1,0:T(8,128)(2,1)S(1)}, bf16[256,2048]{1,0:T(8,128)(2,1)S(1)}) custom-call(s32[4]{0:T(128)S(1)} %pad_add_fusion.flags_ref, bf16[2,256,1024]{2,1,0:T(8,128)(2,1)} %copy-done, bf16[2,256,1024]{2,1,0:T(8,128)(2,1)} %collective-permute-done.near_ref, bf16[2,256,1024]{2,1,0:T(8,128)(2,1)} %copy-done.1), custom_call_target="tpu_custom_call" | custom-call | tf_op jit(solution)/shard_map/prototypes/pallas_call | solution.py:126
  47.5 0.0 all-to-all-done.own_ref
  47.5 3.2 %collective-permute-start.2 = (bf16[8,256,256]{2,1,0:T(8,128)(2,1)S(1)}, bf16[8,256,256]{2,1,0:T(8,128)(2,1)S(1)}, u32[]{:S(2)}, u32[]{:S(2)}) collective-permute-start(bf16[8,256,256]{2,1,0:T(8,128)(2,1)S(1)} %all-to-all-done.own_ref), channel_id=1, source_target_pairs={{0,32},{32,0},{1,33},{33,1},{2,34},{34,2},{3,35},{35,3},{4,36},{36... | collective-permute-start | bytes 3145736 | tf_op jit(solution)/shard_map/ppermute | solution.py:473
  50.8 2.3 %collective-permute-done.2.other_ref = bf16[8,256,256]{2,1,0:T(8,128)(2,1)S(1)} collective-permute-done((bf16[8,256,256]{2,1,0:T(8,128)(2,1)S(1)}, bf16[8,256,256]{2,1,0:T(8,128)(2,1)S(1)}, u32[]{:S(2)}, u32[]{:S(2)}) %collective-permute-start.2) | collective-permute-done | bytes 1048608 | tf_op jit(solution)/shard_map/ppermute | solution.py:473
  53.1 3.2 %first_codes.1 = (bf16[2048,2048]{1,0:T(8,128)(2,1)S(1)}, bf16[32,16,128]{2,1,0:T(8,128)(2,1)S(1)}) custom-call(s32[4]{0:T(128)S(1)} %pad_add_fusion.flags_ref, bf16[8,256,256]{2,1,0:T(8,128)(2,1)S(1)} %all-to-all-done.own_ref, bf16[8,256,256]{2,1,0:T(8,128)(2,1)S(1)} %collective-permute-done.2.other_ref, bf16[256,2048]{1,0:T(8,128)(2,1)S(1)} %get-tuple-element.22.protos_ref), custom_call_target="tpu_custom_call" | custom-call | flops 2147483648 | bytes 8388608 | tf_op jit(solution)/shard_map/first_codes/pallas_call | solution.py:203
  56.3 3.3 %student_expo.1 = (bf16[2048,2048]{1,0:T(8,128)(2,1)S(1)}, f32[16,128]{1,0:T(8,128)S(1)}, bf16[256,2048]{1,0:T(8,128)(2,1)S(1)}) custom-call(s32[4]{0:T(128)S(1)} %pad_add_fusion.flags_ref, bf16[8,256,256]{2,1,0:T(8,128)(2,1)S(1)} %all-to-all-done.own_ref, bf16[8,256,256]{2,1,0:T(8,128)(2,1)S(1)} %collective-permute-done.2.other_ref, ...), custom_call_target="tpu_custom_call" | custom-call | flops 2147483648 | bytes 8388608 | tf_op jit(solution)/shard_map/student_expo/pallas_call | solution.py:333
  59.6 18.3 %all_to_all.45.refs_0_ = bf16[32,16,128]{2,1,0:T(8,128)(2,1)S(1)} all-to-all(bf16[32,16,128]{2,1,0:T(8,128)(2,1)S(1)} %get-tuple-element.28), channel_id=1, replica_groups=mesh['y'=8,'core'=2,'z'=8,'xhi'=2,'xlo'=2] {'y','xhi','xlo'}, dimensions={0} | all-to-all | bytes 262144 | tf_op jit(solution)/shard_map/all_to_all | solution.py:441
  77.9 4.8 %row_pass.3 = bf16[16,24,128]{2,1,0:T(8,128)(2,1)S(1)} custom-call(bf16[32,16,128]{2,1,0:T(8,128)(2,1)S(1)} %all_to_all.45.refs_0_, bf16[2048,2048]{1,0:T(8,128)(2,1)S(1)} %get-tuple-element.29.refs_1_.codes_ref, f32[16,128]{1,0:T(8,128)S(1)} %get-tuple-element.30.refs_2_), custom_call_target="tpu_custom_call" | custom-call | flops 8388608 | bytes 8388608 | tf_op jit(solution)/shard_map/row_pass/pallas_call | solution.py:255
  82.7 16.5 %all_to_all.46.recv_ref.refs_2_ = bf16[16,24,128]{2,1,0:T(8,128)(2,1)S(1)} all-to-all(bf16[16,24,128]{2,1,0:T(8,128)(2,1)S(1)} %row_pass.3), channel_id=1, replica_groups=mesh['y'=8,'core'=2,'z'=8,'xhi'=2,'xlo'=2] {'core','z'}, dimensions={0} | all-to-all | bytes 196608 | tf_op jit(solution)/shard_map/all_to_all | solution.py:441
  99.1 1.9 col_pass.2
  101.1 12.5 %all_to_all.47.refs_0_ = bf16[32,16,128]{2,1,0:T(8,128)(2,1)S(1)} all-to-all(bf16[32,16,128]{2,1,0:T(8,128)(2,1)S(1)} %col_pass.2), channel_id=1, replica_groups=mesh['y'=8,'core'=2,'z'=8,'xhi'=2,'xlo'=2] {'y','xhi','xlo'}, dimensions={0} | all-to-all | bytes 262144 | tf_op jit(solution)/shard_map/all_to_all | solution.py:441
  113.5 4.8 %row_pass.4 = bf16[16,24,128]{2,1,0:T(8,128)(2,1)S(1)} custom-call(bf16[32,16,128]{2,1,0:T(8,128)(2,1)S(1)} %all_to_all.47.refs_0_, bf16[2048,2048]{1,0:T(8,128)(2,1)S(1)} %get-tuple-element.29.refs_1_.codes_ref, bf16[16,24,128]{2,1,0:T(8,128)(2,1)S(1)} %all_to_all.46.recv_ref.refs_2_), custom_call_target="tpu_custom_call" | custom-call | flops 8388608 | bytes 8388608 | tf_op jit(solution)/shard_map/row_pass/pallas_call | solution.py:255
  118.3 12.2 %all_to_all.48.recv_ref.norm_ref = bf16[16,24,128]{2,1,0:T(8,128)(2,1)S(1)} all-to-all(bf16[16,24,128]{2,1,0:T(8,128)(2,1)S(1)} %row_pass.4), channel_id=1, replica_groups=mesh['y'=8,'core'=2,'z'=8,'xhi'=2,'xlo'=2] {'core','z'}, dimensions={0} | all-to-all | bytes 196608 | tf_op jit(solution)/shard_map/all_to_all | solution.py:441
  130.5 1.9 col_pass.3
  132.5 12.5 %all_to_all.49.refs_0_.cols_ref = bf16[32,16,128]{2,1,0:T(8,128)(2,1)S(1)} all-to-all(bf16[32,16,128]{2,1,0:T(8,128)(2,1)S(1)} %col_pass.3), channel_id=1, replica_groups=mesh['y'=8,'core'=2,'z'=8,'xhi'=2,'xlo'=2] {'y','xhi','xlo'}, dimensions={0} | all-to-all | bytes 262144 | tf_op jit(solution)/shard_map/all_to_all | solution.py:441
  145.0 4.8 %row_pass.5 = bf16[16,16,128]{2,1,0:T(8,128)(2,1)S(1)} custom-call(bf16[32,16,128]{2,1,0:T(8,128)(2,1)S(1)} %all_to_all.49.refs_0_.cols_ref, bf16[2048,2048]{1,0:T(8,128)(2,1)S(1)} %get-tuple-element.29.refs_1_.codes_ref), custom_call_target="tpu_custom_call" | custom-call | flops 8388608 | bytes 8388608 | tf_op jit(solution)/shard_map/row_pass/pallas_call | solution.py:255
  149.7 12.1 %all_to_all.50.recv_ref = bf16[16,16,128]{2,1,0:T(8,128)(2,1)S(1)} all-to-all(bf16[16,16,128]{2,1,0:T(8,128)(2,1)S(1)} %row_pass.5), channel_id=1, replica_groups=mesh['y'=8,'core'=2,'z'=8,'xhi'=2,'xlo'=2] {'core','z'}, dimensions={0} | all-to-all | bytes 131072 | tf_op jit(solution)/shard_map/all_to_all | solution.py:441
  161.8 5.6 %grad_pieces.1 = bf16[32,128,128]{2,1,0:T(8,128)(2,1)} custom-call(bf16[16,16,128]{2,1,0:T(8,128)(2,1)S(1)} %all_to_all.50.recv_ref, bf16[16,24,128]{2,1,0:T(8,128)(2,1)S(1)} %all_to_all.48.recv_ref.norm_ref, bf16[32,16,128]{2,1,0:T(8,128)(2,1)S(1)} %all_to_all.49.refs_0_.cols_ref, bf16[256,2048]{1,0:T(8,128)(2,1)S(1)} %get-tuple-element.31.turned_ref, ...), custom_call_target="tpu_custom_call" | custom-call | flops 4294967296 | bytes 16777216 | tf_op jit(solution)/shard_map/grad_pieces/pallas_call | solution.py:371
  167.4 3.9 %all-to-all-start.7 = ((bf16[32,128,128]{2,1,0:T(8,128)(2,1)}), bf16[32,128,128]{2,1,0:T(8,128)(2,1)S(1)}, u32[]{:S(2)}, u32[]{:S(2)}) async-start(bf16[32,128,128]{2,1,0:T(8,128)(2,1)} %grad_pieces.1), calls=%async_computation.7 | async-start | bytes 2097152 | tf_op jit(solution)/shard_map/all_to_all | solution.py:441
  171.3 1.6 own_piece.1.weight_ref
  172.9 23.1 %all-to-all-done.7.recv_ref = bf16[32,128,128]{2,1,0:T(8,128)(2,1)S(1)} async-done(((bf16[32,128,128]{2,1,0:T(8,128)(2,1)}), bf16[32,128,128]{2,1,0:T(8,128)(2,1)S(1)}, u32[]{:S(2)}, u32[]{:S(2)}) %all-to-all-start.7) | async-done | bytes 1048608 | tf_op jit(solution)/shard_map/all_to_all | solution.py:441
  196.0 0.3 weight_back.1
  196.3 22.3 %all_to_all.51.mine_ref = bf16[16,128,128]{2,1,0:T(8,128)(2,1)S(1)} all-to-all(bf16[16,128,128]{2,1,0:T(8,128)(2,1)S(1)} %weight_back.1), channel_id=1, replica_groups=mesh['y'=8,'core'=2,'z'=8,'xhi'=2,'xlo'=2] {'xhi','y'}, dimensions={0} | all-to-all | bytes 1048576 | tf_op jit(solution)/shard_map/all_to_all | solution.py:441
  218.6 1.3 collective-permute-start.3
  219.9 5.0 %collective-permute-done.3.other_ref = bf16[16,128,128]{2,1,0:T(8,128)(2,1)S(1)} collective-permute-done((bf16[16,128,128]{2,1,0:T(8,128)(2,1)S(1)}, bf16[16,128,128]{2,1,0:T(8,128)(2,1)S(1)}, u32[]{:S(2)}, u32[]{:S(2)}) %collective-permute-start.3) | collective-permute-done | bytes 524320 | tf_op jit(solution)/shard_map/ppermute | solution.py:488
  224.9 1.6 join_pieces.1
Async XLA Ops:
  2.5 45.0 %all-to-all-start = ((bf16[8,256,256]{2,1,0:T(8,128)(2,1)}), bf16[8,256,256]{2,1,0:T(8,128)(2,1)S(1)}, u32[]{:S(2)}, u32[]{:S(2)}) async-start(bf16[8,256,256]{2,1,0:T(8,128)(2,1)} %masked_rows.1), calls=%async_computation | async-start | bytes 2097152 | tf_op jit(solution)/shard_map/all_to_all | solution.py:441
  14.7 26.4 %copy-start = (bf16[2,256,1024]{2,1,0:T(8,128)(2,1)}, bf16[2,256,1024]{2,1,0:T(8,128)(2,1)S(1)}, u32[]{:S(2)}) copy-start(bf16[2,256,1024]{2,1,0:T(8,128)(2,1)S(1)} %pad_maximum_fusion.own_ref) | copy-start | bytes 3145732
  14.7 26.4 %collective-permute-start.1 = (bf16[2,256,1024]{2,1,0:T(8,128)(2,1)S(1)}, bf16[2,256,1024]{2,1,0:T(8,128)(2,1)S(1)}, u32[]{:S(2)}, u32[]{:S(2)}) collective-permute-start(bf16[2,256,1024]{2,1,0:T(8,128)(2,1)S(1)} %pad_maximum_fusion.own_ref), channel_id=1, source_target_pairs={{1,2},{0,3},{35,32},{34,33},{5,6},{4,7},{39,36},{38,37},{9,10},{8,... | collective-permute-start | bytes 3145736 | tf_op jit(solution)/shard_map/ppermute | solution.py:456
  16.0 28.7 %collective-permute-start = (bf16[2,256,1024]{2,1,0:T(8,128)(2,1)S(1)}, bf16[2,256,1024]{2,1,0:T(8,128)(2,1)}, u32[]{:S(2)}, u32[]{:S(2)}) collective-permute-start(bf16[2,256,1024]{2,1,0:T(8,128)(2,1)S(1)} %pad_maximum_fusion.own_ref), channel_id=1, source_target_pairs={{1,0},{0,1},{32,2},{33,3},{2,32},{3,33},{35,34},{34,35},{5,4},{4,5... | collective-permute-start | bytes 3145736 | tf_op jit(solution)/shard_map/ppermute | solution.py:456
  41.0 1.0 copy-start.1
  47.5 5.5 %collective-permute-start.2 = (bf16[8,256,256]{2,1,0:T(8,128)(2,1)S(1)}, bf16[8,256,256]{2,1,0:T(8,128)(2,1)S(1)}, u32[]{:S(2)}, u32[]{:S(2)}) collective-permute-start(bf16[8,256,256]{2,1,0:T(8,128)(2,1)S(1)} %all-to-all-done.own_ref), channel_id=1, source_target_pairs={{0,32},{32,0},{1,33},{33,1},{2,34},{34,2},{3,35},{35,3},{4,36},{36... | collective-permute-start | bytes 3145736 | tf_op jit(solution)/shard_map/ppermute | solution.py:473
  167.4 28.6 %all-to-all-start.7 = ((bf16[32,128,128]{2,1,0:T(8,128)(2,1)}), bf16[32,128,128]{2,1,0:T(8,128)(2,1)S(1)}, u32[]{:S(2)}, u32[]{:S(2)}) async-start(bf16[32,128,128]{2,1,0:T(8,128)(2,1)} %grad_pieces.1), calls=%async_computation.7 | async-start | bytes 2097152 | tf_op jit(solution)/shard_map/all_to_all | solution.py:441
  218.6 6.3 %collective-permute-start.3 = (bf16[16,128,128]{2,1,0:T(8,128)(2,1)S(1)}, bf16[16,128,128]{2,1,0:T(8,128)(2,1)S(1)}, u32[]{:S(2)}, u32[]{:S(2)}) collective-permute-start(bf16[16,128,128]{2,1,0:T(8,128)(2,1)S(1)} %all_to_all.51.mine_ref), channel_id=1, source_target_pairs={{0,32},{34,2},{1,33},{35,3},{4,36},{38,6},{5,37},{39,7},{8,40},{42... | collective-permute-start | bytes 1572872 | tf_op jit(solution)/shard_map/ppermute | solution.py:488

commit v6 on v5

--- a/solution.py
+++ b/solution.py
@@ -98,40 +98,41 @@
         act(near_ref, far_ref)
 
 
-def protos_kernel(flags_ref, own_ref, near_ref, far_ref, teach_ref, stud_ref, held_ref, sems):
-    def bring(first, second):
-        copies = [
-            pltpu.make_async_copy(first, held_ref.at[0], sems.at[0]),
-            pltpu.make_async_copy(second, held_ref.at[1], sems.at[1]),
-        ]
-        for copy in copies:
-            copy.start()
-        for copy in copies:
-            copy.wait()
-
-    two_shards(flags_ref, own_ref, near_ref, far_ref, bring)
-    columns = own_ref.shape[2]
+def protos_kernel(pieces, flags_ref, own_ref, near_ref, far_ref, out_ref, *piece_ref):
+    columns = own_ref.shape[1]
     xlo = flags_ref[1]
-    for net, out_ref in enumerate((teach_ref, stud_ref)):
-        for part, place in ((0, xlo), (1, 1 - xlo)):
-            values = held_ref[part, net].astype(f32)
+
+    def scaled(first, second):
+        for ref, place in ((first, xlo), (second, 1 - xlo)):
+            values = ref[...].astype(f32)
             square = jnp.sum(values * values, axis=0, keepdims=True)
             at = pl.multiple_of(place * columns, columns)
             out_ref[:, pl.ds(at, columns)] = (values * lax.rsqrt(square + epsilon)).astype(bf16)
-
-
-def prototypes(flags, own, near, far):
-    nets, rows, columns = own.shape
-    like = jax.ShapeDtypeStruct((rows, 2 * columns), bf16)
-    return pl.pallas_call(
-        protos_kernel,
-        in_specs=[IN_SMEM] + [IN_HBM] * 3,
-        out_specs=(IN_VMEM, IN_VMEM),
-        out_shape=(like, like),
-        scratch_shapes=[pltpu.VMEM((2,) + own.shape, bf16), pltpu.SemaphoreType.DMA((2,))],
-        compiler_params=params(),
+        if pieces:
+            index = flags_ref[3]
+            half = columns // pieces
+            block = first[:, pl.ds(pl.multiple_of(index // 2 * LANES, LANES), LANES)].astype(f32)
+            block = jnp.where(index % 2 == 0, block[:, :half], block[:, half:])
+            rows = block.shape[0] // 2
+            piece_ref[0][...] = jnp.concatenate([block[:rows], block[rows:]], axis=1)
+
+    two_shards(flags_ref, own_ref, near_ref, far_ref, scaled)
+
+
+def prototypes(flags, own, near, far, pieces=0):
+    rows, columns = own.shape
+    shapes = [jax.ShapeDtypeStruct((rows, 2 * columns), bf16)]
+    if pieces:
+        shapes.append(jax.ShapeDtypeStruct((rows // 2, 2 * columns // pieces), f32))
+    return pl.pallas_call(
+        functools.partial(protos_kernel, pieces),
+        in_specs=[IN_SMEM] + [IN_VMEM] * 3,
+        out_specs=[IN_VMEM] * len(shapes),
+        out_shape=shapes,
+        compiler_params=params(),
+        cost_estimate=cost(4 * rows * columns, 0, 8 * rows * columns),
         name="prototypes",
-    )(flags, in_hbm(own), in_hbm(near), in_hbm(far))
+    )(flags, own, near, far)
 
 
 def pack_piece(block, piece, pieces):
@@ -139,36 +140,6 @@
     width = columns // pieces
     part = block[:, piece * width : (piece + 1) * width]
     return jnp.concatenate([part[: rows // 2], part[rows // 2 :]], axis=1)
-
-
-def own_piece_kernel(pieces, flags_ref, own_ref, near_ref, out_ref, held_ref, sem):
-    index = flags_ref[3]
-    columns = pl.ds(pl.multiple_of(index // 2 * LANES, LANES), LANES)
-
-    def bring(first, _):
-        copy = pltpu.make_async_copy(first.at[1, :, columns], held_ref, sem)
-        copy.start()
-        copy.wait()
-
-    two_shards(flags_ref, own_ref, near_ref, near_ref, bring)
-    half = own_ref.shape[2] // pieces
-    block = held_ref[...].astype(f32)
-    block = jnp.where(index % 2 == 0, block[:, :half], block[:, half:])
-    rows = block.shape[0] // 2
-    out_ref[...] = jnp.concatenate([block[:rows], block[rows:]], axis=1)
-
-
-def own_piece(flags, own, near, pieces):
-    _, rows, columns = own.shape
-    return pl.pallas_call(
-        functools.partial(own_piece_kernel, pieces),
-        in_specs=[IN_SMEM, IN_HBM, IN_HBM],
-        out_specs=IN_VMEM,
-        out_shape=jax.ShapeDtypeStruct((rows // 2, 2 * columns // pieces), f32),
-        scratch_shapes=[pltpu.VMEM((rows, LANES), bf16), pltpu.SemaphoreType.DMA],
-        compiler_params=params(),
-        name="own_piece",
-    )(flags, in_hbm(own), in_hbm(near))
 
 
 def spread_cols(total, cols_ref):
@@ -229,12 +200,16 @@
     lines = CHUNK // LANES
     scale = lane_row(1.0 / jnp.sum(recv_ref[...].astype(f32), axis=0), 0, tiles)
     for i in range(count // CHUNK):
-        part = None
-        for j in range(tiles):
-            columns = slice(j * LANES, (j + 1) * LANES)
-            term = codes_ref[i * CHUNK : (i + 1) * CHUNK, columns].astype(f32) * scale[:, columns]
-            part = term if part is None else part + term
-        block = jnp.broadcast_to(sum_lanes(part)[None], (out_ref.shape[0], lines, LANES))
+        blocks = []
+        for k in range(lines):
+            at = i * CHUNK + k * LANES
+            part = None
+            for j in range(tiles):
+                columns = slice(j * LANES, (j + 1) * LANES)
+                term = codes_ref[at : at + LANES, columns].astype(f32) * scale[:, columns]
+                part = term if part is None else part + term
+            blocks.append(part.astype(bf16))
+        block = jnp.broadcast_to(sum_lanes(jnp.concatenate(blocks, axis=0))[None], (out_ref.shape[0], lines, LANES))
         out_ref[:, i * lines : (i + 1) * lines, :] = block.astype(bf16)
     first = count // LANES
     if stage == 1:
@@ -464,13 +439,15 @@
     matched = (core == xhi).astype(jnp.int32)
     flags = jnp.stack([core, xlo, matched, lax.axis_index(SHARD_PEERS)]).astype(jnp.int32)
 
-    weights = jnp.stack([teacher_weight, student_weight])
-    near, far = shard_permutes(weights)
-    teach_protos, stud_protos = prototypes(flags, weights, near, far)
+    teach_near, teach_far = shard_permutes(teacher_weight)
+    stud_near, stud_far = shard_permutes(student_weight)
+    (teach_protos,) = prototypes(flags, teacher_weight, teach_near, teach_far)
     line = masked_rows(mask_index.reshape(1, -1), teacher_patches, student_patches, size("z"))
     line = exchange(line, "z")
-    line, teach_protos, stud_protos = lax.optimization_barrier((line, teach_protos, stud_protos))
+    line, teach_protos, stud_near, stud_far = lax.optimization_barrier((line, teach_protos, stud_near, stud_far))
     other = lax.ppermute(line, "core", [(0, 1), (1, 0)])
+    stud_protos, weight = prototypes(flags, student_weight, stud_near, stud_far, shard_pieces)
+    other, stud_protos, weight = lax.optimization_barrier((other, stud_protos, weight))
 
     codes, cols = first_codes(flags, line, other, teach_protos, column_peers)
     expo, norm, turned = student_expo(flags, line, other, stud_protos)
@@ -483,7 +460,6 @@
     cols = exchange(col_pass(rows, codes, column_peers), COLUMN_PEERS)
     rows = exchange(row_pass(cols, codes, row_peers), ROW_PEERS)
     pieces = exchange(grad_pieces(rows, norm, cols, turned, codes, expo, 2 * shard_pieces), PIECE_PEERS)
-    weight = own_piece(flags, weights, near, shard_pieces)
     mine = exchange(weight_back(pieces, weight, shard_pieces), SHARD_PEERS)
     other = lax.ppermute(mine, ("core", "xhi"), [(0, 2), (3, 1)])
     return join_pieces(flags, mine, other)

time: 227 us -> 213 us (0.938)
  waiting for transfers between devices: 52.5 us -> 21.4 us
  blocking collectives: 106 us -> 134 us
  Pallas kernels: 39 us -> 26.8 us
  local copies, waits for them, and re-layouts: 1 us -> 5.78 us
    all_to_all x7 -> x8, blocking collectives: 106 us -> 134 us  [exchange(): return lax.all_to_all(values, axes, 0, 0, tiled=True)]
    all_to_all x2 -> x1, waiting for transfers between devices: 23.1 us -> 0.01 us  [exchange(): return lax.all_to_all(values, axes, 0, 0, tiled=True)]
    pallas_call x3, Pallas kernels: 14.4 us -> 5.65 us  [row_pass(): pl.pallas_call(functools.partial(row_pass_kernel, stage), in_specs=[IN_VM...]
    ppermute x2 -> x4, waiting for transfers between devices: 22.1 us -> 15.8 us  [shard_permutes(): return (lax.ppermute(weight, axes, near), lax.ppermute(weight, axes, far))]
    unnamed x4 -> x12, local copies, waits for them, and re-layouts: 1 us -> 5.78 us
    all_to_all x2 -> x1, starting transfers between devices: 14.8 us -> 10.9 us  [exchange(): return lax.all_to_all(values, axes, 0, 0, tiled=True)]
    ppermute x2 -> x4, starting transfers between devices: 6.78 us -> 9.99 us  [shard_permutes(): return (lax.ppermute(weight, axes, near), lax.ppermute(weight, axes, far))]
    pallas_call x2, Pallas kernels: 4.4 us -> 1.84 us  [prototypes(): pl.pallas_call(functools.partial(protos_kernel, pieces), in_specs=[IN_SME...]
  transfers between devices with their start and end apart: 6 -> 7, of which waited for: 5 -> 6; matrix products, arithmetic and copies ran while one was open for 1% -> 0% of each run, Pallas kernels for 2% -> 1%
where the time goes in v6:
time: 213 us; the launch traced here: 212 us
  blocking collectives  134 us (63%)
  Pallas kernels  26.8 us (13%)
  starting transfers between devices  24.1 us (11%)
  waiting for transfers between devices  21.4 us (10%)
  local copies, waits for them, and re-layouts  5.78 us (3%)
    all_to_all x8, blocking collectives, exchange(): return lax.all_to_all(values, axes, 0, 0, tiled=True)  134 us
    ppermute x4, waiting for transfers between devices, shard_permutes(): return (lax.ppermute(weight, axes, near), lax.ppermute(weight, axes, far))  15.8 us
    all_to_all x1, starting transfers between devices, exchange(): return lax.all_to_all(values, axes, 0, 0, tiled=True)  10.9 us
    ppermute x4, starting transfers between devices, shard_permutes(): return (lax.ppermute(weight, axes, near), lax.ppermute(weight, axes, far))  9.99 us
    unnamed x12, local copies, waits for them, and re-layouts  5.78 us
    pallas_call x3, Pallas kernels, row_pass(): pl.pallas_call(functools.partial(row_pass_kernel, stage), in_specs=[IN_VM...  5.65 us
    ppermute x1, waiting for transfers between devices, shards(): other = lax.ppermute(mine, ('core', 'xhi'), [(0, 2), (3, 1)])  4.97 us
    pallas_call x1, Pallas kernels, grad_pieces(): pl.pallas_call(grad_kernel, in_specs=[IN_VMEM] * 6, out_specs=IN_VMEM, ou...  4.59 us
  transfers between devices with their start and end apart: 7, of which 6 were waited for; matrix products, arithmetic and copies ran while one was open for 0% of the time, Pallas kernels for 1%

profile of v6, /device:TPU:1, one launch (start us, length us, event | category | flops | bytes accessed | tf_op | source)
XLA Modules:
  0.0 211.9 jit_solution(7823142049102736654)
XLA Ops:
  0.0 2.5 %masked_rows.1 = bf16[8,256,256]{2,1,0:T(8,128)(2,1)} custom-call(s32[1,128]{1,0:T(1,128)} %bitcast.5, bf16[256,256]{1,0:T(8,128)(2,1)} %teacher_ref.1, bf16[256,256]{1,0:T(8,128)(2,1)} %student_ref.1), custom_call_target="tpu_custom_call" | custom-call | tf_op jit(solution)/shard_map/masked_rows/pallas_call | solution.py:76
  2.5 10.9 %all-to-all-start = ((bf16[8,256,256]{2,1,0:T(8,128)(2,1)}), bf16[8,256,256]{2,1,0:T(8,128)(2,1)S(1)}, u32[]{:S(2)}, u32[]{:S(2)}) async-start(bf16[8,256,256]{2,1,0:T(8,128)(2,1)} %masked_rows.1), calls=%async_computation | async-start | bytes 2097152 | tf_op jit(solution)/shard_map/all_to_all | solution.py:416
  13.4 5.5 %collective-permute-start = (bf16[256,1024]{1,0:T(8,128)(2,1)}, bf16[256,1024]{1,0:T(8,128)(2,1)S(1)}, u32[]{:S(2)}, u32[]{:S(2)}) collective-permute-start(bf16[256,1024]{1,0:T(8,128)(2,1)} %own_ref.2), channel_id=1, source_target_pairs={{1,0},{0,1},{32,2},{33,3},{2,32},{3,33},{35,34},{34,35},{5,4},{4,5... | collective-permute-start | bytes 1572872 | tf_op jit(solution)/shard_map/ppermute | solution.py:431
  18.9 1.3 collective-permute-start.1
  20.2 1.9 collective-permute-start.2
  22.1 1.3 collective-permute-start.3
  23.4 0.1 pad_add_fusion.flags_ref
  23.5 8.4 %collective-permute-done.near_ref = bf16[256,1024]{1,0:T(8,128)(2,1)S(1)} collective-permute-done((bf16[256,1024]{1,0:T(8,128)(2,1)}, bf16[256,1024]{1,0:T(8,128)(2,1)S(1)}, u32[]{:S(2)}, u32[]{:S(2)}) %collective-permute-start) | collective-permute-done | bytes 524320 | tf_op jit(solution)/shard_map/ppermute | solution.py:431
  31.8 0.0 copy-start.2
  31.8 0.8 copy-done.2
  32.6 3.2 %collective-permute-done.1.far_ref = bf16[256,1024]{1,0:T(8,128)(2,1)S(1)} collective-permute-done((bf16[256,1024]{1,0:T(8,128)(2,1)}, bf16[256,1024]{1,0:T(8,128)(2,1)S(1)}, u32[]{:S(2)}, u32[]{:S(2)}) %collective-permute-start.1) | collective-permute-done | bytes 524320 | tf_op jit(solution)/shard_map/ppermute | solution.py:431
  35.8 0.0 copy-start.4
  35.8 0.8 copy-done.4
  36.6 0.0 copy-start.1
  36.6 1.0 copy-done.1
  37.7 0.0 copy-start.3
  37.7 1.0 copy-done.3
  38.7 0.0 copy-start.5
  38.7 1.0 copy-done.5
  39.8 0.9 prototypes.2.protos_ref
  40.7 2.0 collective-permute-done.2.near_ref
  42.7 2.3 %collective-permute-done.3.far_ref = bf16[256,1024]{1,0:T(8,128)(2,1)S(1)} collective-permute-done((bf16[256,1024]{1,0:T(8,128)(2,1)}, bf16[256,1024]{1,0:T(8,128)(2,1)S(1)}, u32[]{:S(2)}, u32[]{:S(2)}) %collective-permute-start.3) | collective-permute-done | bytes 524320 | tf_op jit(solution)/shard_map/ppermute | solution.py:431
  44.9 0.0 all-to-all-done.own_ref
  44.9 1.9 collective-permute-start.4
  46.8 0.0 copy-start
  46.8 1.0 copy-done
  47.9 0.9 prototypes.3
  48.8 0.6 collective-permute-done.4.other_ref
  49.5 3.2 %first_codes.1 = (bf16[2048,2048]{1,0:T(8,128)(2,1)S(1)}, bf16[32,16,128]{2,1,0:T(8,128)(2,1)S(1)}) custom-call(s32[4]{0:T(128)S(1)} %pad_add_fusion.flags_ref, bf16[8,256,256]{2,1,0:T(8,128)(2,1)S(1)} %all-to-all-done.own_ref, bf16[8,256,256]{2,1,0:T(8,128)(2,1)S(1)} %collective-permute-done.4.other_ref, bf16[256,2048]{1,0:T(8,128)(2,1)S(1)} %prototypes.2.protos_ref), custom_call_target="tpu_custom_call" | custom-call | flops 2147483648 | bytes 8388608 | tf_op jit(solution)/shard_map/first_codes/pallas_call | solution.py:174
  52.7 3.3 %student_expo.1 = (bf16[2048,2048]{1,0:T(8,128)(2,1)S(1)}, f32[16,128]{1,0:T(8,128)S(1)}, bf16[256,2048]{1,0:T(8,128)(2,1)S(1)}) custom-call(s32[4]{0:T(128)S(1)} %pad_add_fusion.flags_ref, bf16[8,256,256]{2,1,0:T(8,128)(2,1)S(1)} %all-to-all-done.own_ref, bf16[8,256,256]{2,1,0:T(8,128)(2,1)S(1)} %collective-permute-done.4.other_ref, ...), custom_call_target="tpu_custom_call" | custom-call | flops 2147483648 | bytes 8388608 | tf_op jit(solution)/shard_map/student_expo/pallas_call | solution.py:308
  56.0 18.0 %all_to_all.45.refs_0_ = bf16[32,16,128]{2,1,0:T(8,128)(2,1)S(1)} all-to-all(bf16[32,16,128]{2,1,0:T(8,128)(2,1)S(1)} %get-tuple-element.35), channel_id=1, replica_groups=mesh['y'=8,'core'=2,'z'=8,'xhi'=2,'xlo'=2] {'y','xhi','xlo'}, dimensions={0} | all-to-all | bytes 262144 | tf_op jit(solution)/shard_map/all_to_all | solution.py:416
  74.0 1.9 row_pass.3
  75.9 16.3 %all_to_all.46.recv_ref.refs_2_ = bf16[16,24,128]{2,1,0:T(8,128)(2,1)S(1)} all-to-all(bf16[16,24,128]{2,1,0:T(8,128)(2,1)S(1)} %row_pass.3), channel_id=1, replica_groups=mesh['y'=8,'core'=2,'z'=8,'xhi'=2,'xlo'=2] {'core','z'}, dimensions={0} | all-to-all | bytes 196608 | tf_op jit(solution)/shard_map/all_to_all | solution.py:416
  92.2 1.9 col_pass.2
  94.1 12.4 %all_to_all.47.refs_0_ = bf16[32,16,128]{2,1,0:T(8,128)(2,1)S(1)} all-to-all(bf16[32,16,128]{2,1,0:T(8,128)(2,1)S(1)} %col_pass.2), channel_id=1, replica_groups=mesh['y'=8,'core'=2,'z'=8,'xhi'=2,'xlo'=2] {'y','xhi','xlo'}, dimensions={0} | all-to-all | bytes 262144 | tf_op jit(solution)/shard_map/all_to_all | solution.py:416
  106.5 1.9 row_pass.4
  108.4 12.3 %all_to_all.48.recv_ref.norm_ref = bf16[16,24,128]{2,1,0:T(8,128)(2,1)S(1)} all-to-all(bf16[16,24,128]{2,1,0:T(8,128)(2,1)S(1)} %row_pass.4), channel_id=1, replica_groups=mesh['y'=8,'core'=2,'z'=8,'xhi'=2,'xlo'=2] {'core','z'}, dimensions={0} | all-to-all | bytes 196608 | tf_op jit(solution)/shard_map/all_to_all | solution.py:416
  120.7 1.9 col_pass.3
  122.6 12.4 %all_to_all.49.refs_0_.cols_ref = bf16[32,16,128]{2,1,0:T(8,128)(2,1)S(1)} all-to-all(bf16[32,16,128]{2,1,0:T(8,128)(2,1)S(1)} %col_pass.3), channel_id=1, replica_groups=mesh['y'=8,'core'=2,'z'=8,'xhi'=2,'xlo'=2] {'y','xhi','xlo'}, dimensions={0} | all-to-all | bytes 262144 | tf_op jit(solution)/shard_map/all_to_all | solution.py:416
  135.0 1.9 row_pass.5
  136.9 12.2 %all_to_all.50.recv_ref = bf16[16,16,128]{2,1,0:T(8,128)(2,1)S(1)} all-to-all(bf16[16,16,128]{2,1,0:T(8,128)(2,1)S(1)} %row_pass.5), channel_id=1, replica_groups=mesh['y'=8,'core'=2,'z'=8,'xhi'=2,'xlo'=2] {'core','z'}, dimensions={0} | all-to-all | bytes 131072 | tf_op jit(solution)/shard_map/all_to_all | solution.py:416
  149.1 4.6 %grad_pieces.1 = bf16[32,128,128]{2,1,0:T(8,128)(2,1)S(1)} custom-call(bf16[16,16,128]{2,1,0:T(8,128)(2,1)S(1)} %all_to_all.50.recv_ref, bf16[16,24,128]{2,1,0:T(8,128)(2,1)S(1)} %all_to_all.48.recv_ref.norm_ref, bf16[32,16,128]{2,1,0:T(8,128)(2,1)S(1)} %all_to_all.49.refs_0_.cols_ref, bf16[256,2048]{1,0:T(8,128)(2,1)S(1)} %get-tuple-element.38.turned_ref, ...), custom_call_target="tpu_custom_call" | custom-call | flops 4294967296 | bytes 16777216 | tf_op jit(solution)/shard_map/grad_pieces/pallas_call | solution.py:346
  153.7 27.7 %all_to_all.51.recv_ref = bf16[32,128,128]{2,1,0:T(8,128)(2,1)S(1)} all-to-all(bf16[32,128,128]{2,1,0:T(8,128)(2,1)S(1)} %grad_pieces.1), channel_id=1, replica_groups=mesh['y'=8,'core'=2,'z'=8,'xhi'=2,'xlo'=2] {'xlo','xhi','y'}, dimensions={0} | all-to-all | bytes 2097152 | tf_op jit(solution)/shard_map/all_to_all | solution.py:416
  181.4 0.3 weight_back.1
  181.7 22.3 %all_to_all.52.mine_ref = bf16[16,128,128]{2,1,0:T(8,128)(2,1)S(1)} all-to-all(bf16[16,128,128]{2,1,0:T(8,128)(2,1)S(1)} %weight_back.1), channel_id=1, replica_groups=mesh['y'=8,'core'=2,'z'=8,'xhi'=2,'xlo'=2] {'xhi','y'}, dimensions={0} | all-to-all | bytes 1048576 | tf_op jit(solution)/shard_map/all_to_all | solution.py:416
  204.1 1.3 collective-permute-start.5
  205.3 5.0 %collective-permute-done.5.other_ref = bf16[16,128,128]{2,1,0:T(8,128)(2,1)S(1)} collective-permute-done((bf16[16,128,128]{2,1,0:T(8,128)(2,1)S(1)}, bf16[16,128,128]{2,1,0:T(8,128)(2,1)S(1)}, u32[]{:S(2)}, u32[]{:S(2)}) %collective-permute-start.5) | collective-permute-done | bytes 524320 | tf_op jit(solution)/shard_map/ppermute | solution.py:464
  210.3 1.6 join_pieces.1
Async XLA Ops:
  2.5 42.4 %all-to-all-start = ((bf16[8,256,256]{2,1,0:T(8,128)(2,1)}), bf16[8,256,256]{2,1,0:T(8,128)(2,1)S(1)}, u32[]{:S(2)}, u32[]{:S(2)}) async-start(bf16[8,256,256]{2,1,0:T(8,128)(2,1)} %masked_rows.1), calls=%async_computation | async-start | bytes 2097152 | tf_op jit(solution)/shard_map/all_to_all | solution.py:416
  13.4 18.5 %collective-permute-start = (bf16[256,1024]{1,0:T(8,128)(2,1)}, bf16[256,1024]{1,0:T(8,128)(2,1)S(1)}, u32[]{:S(2)}, u32[]{:S(2)}) collective-permute-start(bf16[256,1024]{1,0:T(8,128)(2,1)} %own_ref.2), channel_id=1, source_target_pairs={{1,0},{0,1},{32,2},{33,3},{2,32},{3,33},{35,34},{34,35},{5,4},{4,5... | collective-permute-start | bytes 1572872 | tf_op jit(solution)/shard_map/ppermute | solution.py:431
  18.9 17.0 %collective-permute-start.1 = (bf16[256,1024]{1,0:T(8,128)(2,1)}, bf16[256,1024]{1,0:T(8,128)(2,1)S(1)}, u32[]{:S(2)}, u32[]{:S(2)}) collective-permute-start(bf16[256,1024]{1,0:T(8,128)(2,1)} %own_ref.2), channel_id=1, source_target_pairs={{1,2},{0,3},{35,32},{34,33},{5,6},{4,7},{39,36},{38,37},{9,10},{8,... | collective-permute-start | bytes 1572872 | tf_op jit(solution)/shard_map/ppermute | solution.py:431
  20.2 22.5 %collective-permute-start.2 = (bf16[256,1024]{1,0:T(8,128)(2,1)}, bf16[256,1024]{1,0:T(8,128)(2,1)S(1)}, u32[]{:S(2)}, u32[]{:S(2)}) collective-permute-start(bf16[256,1024]{1,0:T(8,128)(2,1)} %own_ref.3), channel_id=1, source_target_pairs={{1,0},{0,1},{32,2},{33,3},{2,32},{3,33},{35,34},{34,35},{5,4},{4,5... | collective-permute-start | bytes 1572872 | tf_op jit(solution)/shard_map/ppermute | solution.py:431
  22.1 22.8 %collective-permute-start.3 = (bf16[256,1024]{1,0:T(8,128)(2,1)}, bf16[256,1024]{1,0:T(8,128)(2,1)S(1)}, u32[]{:S(2)}, u32[]{:S(2)}) collective-permute-start(bf16[256,1024]{1,0:T(8,128)(2,1)} %own_ref.3), channel_id=1, source_target_pairs={{1,2},{0,3},{35,32},{34,33},{5,6},{4,7},{39,36},{38,37},{9,10},{8,... | collective-permute-start | bytes 1572872 | tf_op jit(solution)/shard_map/ppermute | solution.py:431
  31.8 0.8 copy-start.2
  35.8 0.8 copy-start.4
  36.6 1.0 copy-start.1
  37.7 1.0 copy-start.3
  38.7 1.0 copy-start.5
  44.9 4.5 %collective-permute-start.4 = (bf16[8,256,256]{2,1,0:T(8,128)(2,1)S(1)}, bf16[8,256,256]{2,1,0:T(8,128)(2,1)S(1)}, u32[]{:S(2)}, u32[]{:S(2)}) collective-permute-start(bf16[8,256,256]{2,1,0:T(8,128)(2,1)S(1)} %all-to-all-done.own_ref), channel_id=1, source_target_pairs={{0,32},{32,0},{1,33},{33,1},{2,34},{34,2},{3,35},{35,3},{4,36},{36... | collective-permute-start | bytes 3145736 | tf_op jit(solution)/shard_map/ppermute | solution.py:448
  46.8 1.0 copy-start
  204.1 6.3 %collective-permute-start.5 = (bf16[16,128,128]{2,1,0:T(8,128)(2,1)S(1)}, bf16[16,128,128]{2,1,0:T(8,128)(2,1)S(1)}, u32[]{:S(2)}, u32[]{:S(2)}) collective-permute-start(bf16[16,128,128]{2,1,0:T(8,128)(2,1)S(1)} %all_to_all.52.mine_ref), channel_id=1, source_target_pairs={{0,32},{34,2},{1,33},{35,3},{4,36},{38,6},{5,37},{39,7},{8,40},{42... | collective-permute-start | bytes 1572872 | tf_op jit(solution)/shard_map/ppermute | solution.py:464

commit v7 on v5

--- a/solution.py
+++ b/solution.py
@@ -50,11 +50,15 @@
     return pltpu.with_memory_space_constraint(values, pltpu.HBM)
 
 
-def rows_kernel(mask_ref, teacher_ref, student_ref, out_ref, index_ref, held_ref, sems):
+def rows_kernel(
+    mask_ref, teacher_ref, student_ref, teacher_weight_ref, student_weight_ref, out_ref, weights_ref, index_ref, held_ref, made_ref, sems
+):
     copies = [
         pltpu.make_async_copy(mask_ref, index_ref, sems.at[0]),
         pltpu.make_async_copy(teacher_ref, held_ref.at[0], sems.at[1]),
         pltpu.make_async_copy(student_ref, held_ref.at[1], sems.at[2]),
+        pltpu.make_async_copy(teacher_weight_ref, weights_ref.at[0], sems.at[3]),
+        pltpu.make_async_copy(student_weight_ref, weights_ref.at[1], sems.at[4]),
     ]
     for copy in copies:
         copy.start()
@@ -67,25 +71,34 @@
         copies[1 + part].wait()
         rows = lax.dot_general(chosen, held_ref[part], TN, preferred_element_type=f32)
         square = jnp.sum(rows * rows, axis=1, keepdims=True)
-        rows = (rows * lax.rsqrt(square + epsilon)).astype(bf16)
-        out_ref[:, part * count : (part + 1) * count, :] = jnp.broadcast_to(rows[None], (out_ref.shape[0],) + rows.shape)
-
-
-def masked_rows(mask, teacher, student, copies):
+        made_ref[part * count : (part + 1) * count, :] = (rows * lax.rsqrt(square + epsilon)).astype(bf16)
+    sends = [pltpu.make_async_copy(made_ref, out_ref.at[i], sems.at[5 + i]) for i in range(out_ref.shape[0])]
+    for send in sends:
+        send.start()
+    for copy in copies[3:] + sends:
+        copy.wait()
+
+
+def masked_rows(mask, teacher, student, teacher_weight, student_weight, copies):
     count, width = mask.shape[1], teacher.shape[1]
+    sources = (mask, teacher, student, teacher_weight, student_weight)
     return pl.pallas_call(
         rows_kernel,
-        in_specs=[IN_HBM] * 3,
-        out_specs=IN_VMEM,
-        out_shape=jax.ShapeDtypeStruct((copies, 2 * count, width), bf16),
+        in_specs=[IN_HBM] * 5,
+        out_specs=(IN_HBM, IN_HBM),
+        out_shape=(
+            pltpu.HBM((copies, 2 * count, width), bf16),
+            pltpu.HBM((2,) + teacher_weight.shape, bf16),
+        ),
         scratch_shapes=[
             pltpu.VMEM(mask.shape, jnp.int32),
             pltpu.VMEM((2,) + teacher.shape, bf16),
-            pltpu.SemaphoreType.DMA((3,)),
+            pltpu.VMEM((2 * count, width), bf16),
+            pltpu.SemaphoreType.DMA((5 + copies,)),
         ],
         compiler_params=params(),
         name="masked_rows",
-    )(in_hbm(mask), in_hbm(teacher), in_hbm(student))
+    )(*map(in_hbm, sources))
 
 
 def two_shards(flags_ref, own_ref, near_ref, far_ref, act):
@@ -98,7 +111,7 @@
         act(near_ref, far_ref)
 
 
-def protos_kernel(flags_ref, own_ref, near_ref, far_ref, teach_ref, stud_ref, held_ref, sems):
+def protos_kernel(pieces, flags_ref, own_ref, near_ref, far_ref, teach_ref, stud_ref, piece_ref, held_ref, sems):
     def bring(first, second):
         copies = [
             pltpu.make_async_copy(first, held_ref.at[0], sems.at[0]),
@@ -111,25 +124,31 @@
 
     two_shards(flags_ref, own_ref, near_ref, far_ref, bring)
     columns = own_ref.shape[2]
-    xlo = flags_ref[1]
+    xlo, index = flags_ref[1], flags_ref[3]
     for net, out_ref in enumerate((teach_ref, stud_ref)):
         for part, place in ((0, xlo), (1, 1 - xlo)):
             values = held_ref[part, net].astype(f32)
             square = jnp.sum(values * values, axis=0, keepdims=True)
             at = pl.multiple_of(place * columns, columns)
             out_ref[:, pl.ds(at, columns)] = (values * lax.rsqrt(square + epsilon)).astype(bf16)
-
-
-def prototypes(flags, own, near, far):
+    half = columns // pieces
+    block = held_ref[0, 1, :, pl.ds(pl.multiple_of(index // 2 * LANES, LANES), LANES)].astype(f32)
+    block = jnp.where(index % 2 == 0, block[:, :half], block[:, half:])
+    rows = block.shape[0] // 2
+    piece_ref[...] = jnp.concatenate([block[:rows], block[rows:]], axis=1)
+
+
+def prototypes(flags, own, near, far, pieces):
     nets, rows, columns = own.shape
     like = jax.ShapeDtypeStruct((rows, 2 * columns), bf16)
     return pl.pallas_call(
-        protos_kernel,
+        functools.partial(protos_kernel, pieces),
         in_specs=[IN_SMEM] + [IN_HBM] * 3,
-        out_specs=(IN_VMEM, IN_VMEM),
-        out_shape=(like, like),
+        out_specs=[IN_VMEM] * 3,
+        out_shape=(like, like, jax.ShapeDtypeStruct((rows // 2, 2 * columns // pieces), f32)),
         scratch_shapes=[pltpu.VMEM((2,) + own.shape, bf16), pltpu.SemaphoreType.DMA((2,))],
         compiler_params=params(),
+        cost_estimate=cost(8 * rows * columns, 0, 16 * rows * columns),
         name="prototypes",
     )(flags, in_hbm(own), in_hbm(near), in_hbm(far))
 
@@ -141,40 +160,10 @@
     return jnp.concatenate([part[: rows // 2], part[rows // 2 :]], axis=1)
 
 
-def own_piece_kernel(pieces, flags_ref, own_ref, near_ref, out_ref, held_ref, sem):
-    index = flags_ref[3]
-    columns = pl.ds(pl.multiple_of(index // 2 * LANES, LANES), LANES)
-
-    def bring(first, _):
-        copy = pltpu.make_async_copy(first.at[1, :, columns], held_ref, sem)
-        copy.start()
-        copy.wait()
-
-    two_shards(flags_ref, own_ref, near_ref, near_ref, bring)
-    half = own_ref.shape[2] // pieces
-    block = held_ref[...].astype(f32)
-    block = jnp.where(index % 2 == 0, block[:, :half], block[:, half:])
-    rows = block.shape[0] // 2
-    out_ref[...] = jnp.concatenate([block[:rows], block[rows:]], axis=1)
-
-
-def own_piece(flags, own, near, pieces):
-    _, rows, columns = own.shape
-    return pl.pallas_call(
-        functools.partial(own_piece_kernel, pieces),
-        in_specs=[IN_SMEM, IN_HBM, IN_HBM],
-        out_specs=IN_VMEM,
-        out_shape=jax.ShapeDtypeStruct((rows // 2, 2 * columns // pieces), f32),
-        scratch_shapes=[pltpu.VMEM((rows, LANES), bf16), pltpu.SemaphoreType.DMA],
-        compiler_params=params(),
-        name="own_piece",
-    )(flags, in_hbm(own), in_hbm(near))
-
-
 def spread_cols(total, cols_ref):
-    for j in range(cols_ref.shape[1]):
-        part = total[:, j * LANES : (j + 1) * LANES]
-        cols_ref[:, j, :] = jnp.broadcast_to(part, (cols_ref.shape[0], LANES)).astype(bf16)
+    lines = cols_ref.shape[1]
+    block = jnp.concatenate([total[:, j * LANES : (j + 1) * LANES] for j in range(lines)], axis=0)
+    cols_ref[...] = jnp.broadcast_to(block[None], cols_ref.shape).astype(bf16)
 
 
 def net_rows(ref, net):
@@ -227,14 +216,22 @@
     count = codes_ref.shape[0]
     tiles = recv_ref.shape[1]
     lines = CHUNK // LANES
-    scale = lane_row(1.0 / jnp.sum(recv_ref[...].astype(f32), axis=0), 0, tiles)
+    scale = lane_row(1.0 / jnp.sum(recv_ref[...].astype(f32), axis=0), 0, tiles).astype(bf16)
     for i in range(count // CHUNK):
-        part = None
-        for j in range(tiles):
-            columns = slice(j * LANES, (j + 1) * LANES)
-            term = codes_ref[i * CHUNK : (i + 1) * CHUNK, columns].astype(f32) * scale[:, columns]
-            part = term if part is None else part + term
-        block = jnp.broadcast_to(sum_lanes(part)[None], (out_ref.shape[0], lines, LANES))
+        blocks = []
+        for k in range(lines):
+            at = i * CHUNK + k * LANES
+            total = None
+            for g in range(0, tiles, 8):
+                part = None
+                for j in range(g, g + 8):
+                    columns = slice(j * LANES, (j + 1) * LANES)
+                    term = codes_ref[at : at + LANES, columns] * scale[:, columns]
+                    part = term if part is None else part + term
+                part = part.astype(f32)
+                total = part if total is None else total + part
+            blocks.append(total.astype(bf16))
+        block = jnp.broadcast_to(sum_lanes(jnp.concatenate(blocks, axis=0))[None], (out_ref.shape[0], lines, LANES))
         out_ref[:, i * lines : (i + 1) * lines, :] = block.astype(bf16)
     first = count // LANES
     if stage == 1:
@@ -274,6 +271,7 @@
         row = jnp.where(first, lane_row(scale, i * lines, lines), 0.0).astype(bf16)
         spreads.append(lax.dot_general(row, ones, TN, preferred_element_type=f32).astype(bf16))
     width = 8 * LANES
+    totals = []
     for h in range(columns // width):
         total = jnp.zeros((16, width), f32)
         for i, spread in enumerate(spreads):
@@ -289,10 +287,8 @@
                         part = term if part is None else part + term
                     parts.append(part.astype(f32))
                 total = total + jnp.concatenate(parts, axis=1)
-        total = jnp.sum(total, axis=0, keepdims=True)
-        for j in range(width // LANES):
-            part = jnp.broadcast_to(total[:, j * LANES : (j + 1) * LANES], (cols_ref.shape[0], LANES))
-            cols_ref[:, h * (width // LANES) + j, :] = part.astype(bf16)
+        totals.append(jnp.sum(total, axis=0, keepdims=True))
+    spread_cols(jnp.concatenate(totals, axis=1), cols_ref)
 
 
 def col_pass(recv, codes, groups):
@@ -464,13 +460,15 @@
     matched = (core == xhi).astype(jnp.int32)
     flags = jnp.stack([core, xlo, matched, lax.axis_index(SHARD_PEERS)]).astype(jnp.int32)
 
-    weights = jnp.stack([teacher_weight, student_weight])
+    line, weights = masked_rows(
+        mask_index.reshape(1, -1), teacher_patches, student_patches, teacher_weight, student_weight, size("z")
+    )
     near, far = shard_permutes(weights)
-    teach_protos, stud_protos = prototypes(flags, weights, near, far)
-    line = masked_rows(mask_index.reshape(1, -1), teacher_patches, student_patches, size("z"))
     line = exchange(line, "z")
-    line, teach_protos, stud_protos = lax.optimization_barrier((line, teach_protos, stud_protos))
+    line, near, far = lax.optimization_barrier((line, near, far))
     other = lax.ppermute(line, "core", [(0, 1), (1, 0)])
+    teach_protos, stud_protos, weight = prototypes(flags, weights, near, far, shard_pieces)
+    other, teach_protos, stud_protos, weight = lax.optimization_barrier((other, teach_protos, stud_protos, weight))
 
     codes, cols = first_codes(flags, line, other, teach_protos, column_peers)
     expo, norm, turned = student_expo(flags, line, other, stud_protos)
@@ -483,7 +481,6 @@
     cols = exchange(col_pass(rows, codes, column_peers), COLUMN_PEERS)
     rows = exchange(row_pass(cols, codes, row_peers), ROW_PEERS)
     pieces = exchange(grad_pieces(rows, norm, cols, turned, codes, expo, 2 * shard_pieces), PIECE_PEERS)
-    weight = own_piece(flags, weights, near, shard_pieces)
     mine = exchange(weight_back(pieces, weight, shard_pieces), SHARD_PEERS)
     other = lax.ppermute(mine, ("core", "xhi"), [(0, 2), (3, 1)])
     return join_pieces(flags, mine, other)

time: 227 us -> 243 us (1.070)
  blocking collectives: 106 us -> 133 us
  waiting for transfers between devices: 52.5 us -> 28.3 us
  Pallas kernels: 39 us -> 57 us
  starting transfers between devices: 26.1 us -> 22.2 us
    pallas_call x3 -> x2, Pallas kernels: 6.88 us -> 35.8 us  [the longest x1 33 us: masked_rows(): pl.pallas_call(rows_kernel, in_specs=[IN_HBM] * 5, out_specs=(IN_HBM, IN_...]
    all_to_all x7 -> x8, blocking collectives: 106 us -> 133 us  [exchange(): return lax.all_to_all(values, axes, 0, 0, tiled=True)]
    all_to_all x2 -> x1, waiting for transfers between devices: 23.1 us -> 0.01 us  [exchange(): return lax.all_to_all(values, axes, 0, 0, tiled=True)]
    pallas_call x3, Pallas kernels: 14.4 us -> 4.47 us  [row_pass(): pl.pallas_call(functools.partial(row_pass_kernel, stage), in_specs=[IN_VM...]
    all_to_all x2 -> x1, starting transfers between devices: 14.8 us -> 10.9 us  [exchange(): return lax.all_to_all(values, axes, 0, 0, tiled=True)]
  transfers between devices with their start and end apart: 6 -> 5, of which waited for: 5 -> 3; matrix products, arithmetic and copies ran while one was open for 1% -> 0% of each run, Pallas kernels for 2% -> 1%
where the time goes in v7:
time: 243 us; the launch traced here: 242 us
  blocking collectives  133 us (55%)
  Pallas kernels  57 us (23%)
  waiting for transfers between devices  28.3 us (12%)
  starting transfers between devices  22.2 us (9%)
    all_to_all x8, blocking collectives, exchange(): return lax.all_to_all(values, axes, 0, 0, tiled=True)  133 us
    pallas_call x1, Pallas kernels, masked_rows(): pl.pallas_call(rows_kernel, in_specs=[IN_HBM] * 5, out_specs=(IN_HBM, IN_...  33 us
    ppermute x2, waiting for transfers between devices, shard_permutes(): return (lax.ppermute(weight, axes, near), lax.ppermute(weight, axes, far))  23.3 us
    all_to_all x1, starting transfers between devices, exchange(): return lax.all_to_all(values, axes, 0, 0, tiled=True)  10.9 us
    ppermute x2, starting transfers between devices, shard_permutes(): return (lax.ppermute(weight, axes, near), lax.ppermute(weight, axes, far))  6.77 us
    ppermute x1, waiting for transfers between devices, shards(): other = lax.ppermute(mine, ('core', 'xhi'), [(0, 2), (3, 1)])  4.97 us
  transfers between devices with their start and end apart: 5, of which 3 were waited for; matrix products, arithmetic and copies ran while one was open for 0% of the time, Pallas kernels for 1%

profile of v7, /device:TPU:1, one launch (start us, length us, event | category | flops | bytes accessed | tf_op | source)
XLA Modules:
  0.0 242.1 jit_solution(4002508706456597611)
XLA Ops:
  0.0 33.0 %masked_rows.1 = (bf16[8,256,256]{2,1,0:T(8,128)(2,1)}, bf16[2,256,1024]{2,1,0:T(8,128)(2,1)}) custom-call(s32[1,128]{1,0:T(1,128)} %bitcast.5, bf16[256,256]{1,0:T(8,128)(2,1)} %teacher_ref.1, bf16[256,256]{1,0:T(8,128)(2,1)} %student_ref.1, bf16[256,1024]{1,0:T(8,128)(2,1)} %teacher_weight_ref.1, bf16[256,1024]{1,0:T(8,128)(2,1)} %student_weight_ref.1), custom_call_target="tpu_custom_call" | custom-call | tf_op jit(solution)/shard_map/masked_rows/pallas_call | solution.py:85
  33.0 10.9 %all-to-all-start = ((bf16[8,256,256]{2,1,0:T(8,128)(2,1)}), bf16[8,256,256]{2,1,0:T(8,128)(2,1)S(1)}, u32[]{:S(2)}, u32[]{:S(2)}) async-start(bf16[8,256,256]{2,1,0:T(8,128)(2,1)} %get-tuple-element.26), calls=%async_computation | async-start | bytes 2097152 | tf_op jit(solution)/shard_map/all_to_all | solution.py:437
  43.9 1.3 collective-permute-start.1
  45.2 5.5 %collective-permute-start = (bf16[2,256,1024]{2,1,0:T(8,128)(2,1)}, bf16[2,256,1024]{2,1,0:T(8,128)(2,1)S(1)}, u32[]{:S(2)}, u32[]{:S(2)}) collective-permute-start(bf16[2,256,1024]{2,1,0:T(8,128)(2,1)} %get-tuple-element.27.own_ref), channel_id=1, source_target_pairs={{1,0},{0,1},{32,2},{33,3},{2,32},{3,33},{35,34},{34,35},{5,4},{4,5... | collective-permute-start | bytes 3145736 | tf_op jit(solution)/shard_map/ppermute | solution.py:452
  50.7 19.8 %collective-permute-done.1.far_ref = bf16[2,256,1024]{2,1,0:T(8,128)(2,1)S(1)} collective-permute-done((bf16[2,256,1024]{2,1,0:T(8,128)(2,1)}, bf16[2,256,1024]{2,1,0:T(8,128)(2,1)S(1)}, u32[]{:S(2)}, u32[]{:S(2)}) %collective-permute-start.1) | collective-permute-done | bytes 1048608 | tf_op jit(solution)/shard_map/ppermute | solution.py:452
  70.4 0.0 copy-start
  70.4 3.5 %collective-permute-done.near_ref = bf16[2,256,1024]{2,1,0:T(8,128)(2,1)S(1)} collective-permute-done((bf16[2,256,1024]{2,1,0:T(8,128)(2,1)}, bf16[2,256,1024]{2,1,0:T(8,128)(2,1)S(1)}, u32[]{:S(2)}, u32[]{:S(2)}) %collective-permute-start) | collective-permute-done | bytes 1048608 | tf_op jit(solution)/shard_map/ppermute | solution.py:452
  74.0 0.0 copy-start.1
  74.0 1.0 copy-done.1
  75.0 0.0 all-to-all-done.own_ref
  75.0 3.2 %collective-permute-start.2 = (bf16[8,256,256]{2,1,0:T(8,128)(2,1)S(1)}, bf16[8,256,256]{2,1,0:T(8,128)(2,1)S(1)}, u32[]{:S(2)}, u32[]{:S(2)}) collective-permute-start(bf16[8,256,256]{2,1,0:T(8,128)(2,1)S(1)} %all-to-all-done.own_ref), channel_id=1, source_target_pairs={{0,32},{32,0},{1,33},{33,1},{2,34},{34,2},{3,35},{35,3},{4,36},{36... | collective-permute-start | bytes 3145736 | tf_op jit(solution)/shard_map/ppermute | solution.py:469
  78.2 0.1 pad_add_fusion.flags_ref
  78.3 0.0 copy-done
  78.3 2.8 %prototypes.1 = (bf16[256,2048]{1,0:T(8,128)(2,1)S(1)}, bf16[256,2048]{1,0:T(8,128)(2,1)S(1)}, f32[128,128]{1,0:T(8,128)S(1)}) custom-call(s32[4]{0:T(128)S(1)} %pad_add_fusion.flags_ref, bf16[2,256,1024]{2,1,0:T(8,128)(2,1)} %get-tuple-element.27.own_ref, bf16[2,256,1024]{2,1,0:T(8,128)(2,1)} %copy-done.1, bf16[2,256,1024]{2,1,0:T(8,128)(2,1)} %copy-done), custom_call_target="tpu_custom_call" | custom-call | flops 2097152 | bytes 4194304 | tf_op jit(solution)/shard_map/prototypes/pallas_call | solution.py:144
  81.2 0.0 collective-permute-done.2.other_ref
  81.2 2.9 %first_codes.1 = (bf16[2048,2048]{1,0:T(8,128)(2,1)S(1)}, bf16[32,16,128]{2,1,0:T(8,128)(2,1)S(1)}) custom-call(s32[4]{0:T(128)S(1)} %pad_add_fusion.flags_ref, bf16[8,256,256]{2,1,0:T(8,128)(2,1)S(1)} %all-to-all-done.own_ref, bf16[8,256,256]{2,1,0:T(8,128)(2,1)S(1)} %collective-permute-done.2.other_ref, bf16[256,2048]{1,0:T(8,128)(2,1)S(1)} %get-tuple-element.35.protos_ref), custom_call_target="tpu_custom_call" | custom-call | flops 2147483648 | bytes 8388608 | tf_op jit(solution)/shard_map/first_codes/pallas_call | solution.py:192
  84.1 3.3 %student_expo.1 = (bf16[2048,2048]{1,0:T(8,128)(2,1)S(1)}, f32[16,128]{1,0:T(8,128)S(1)}, bf16[256,2048]{1,0:T(8,128)(2,1)S(1)}) custom-call(s32[4]{0:T(128)S(1)} %pad_add_fusion.flags_ref, bf16[8,256,256]{2,1,0:T(8,128)(2,1)S(1)} %all-to-all-done.own_ref, bf16[8,256,256]{2,1,0:T(8,128)(2,1)S(1)} %collective-permute-done.2.other_ref, ...), custom_call_target="tpu_custom_call" | custom-call | flops 2147483648 | bytes 8388608 | tf_op jit(solution)/shard_map/student_expo/pallas_call | solution.py:329
  87.4 18.2 %all_to_all.45.refs_0_ = bf16[32,16,128]{2,1,0:T(8,128)(2,1)S(1)} all-to-all(bf16[32,16,128]{2,1,0:T(8,128)(2,1)S(1)} %get-tuple-element.41), channel_id=1, replica_groups=mesh['y'=8,'core'=2,'z'=8,'xhi'=2,'xlo'=2] {'y','xhi','xlo'}, dimensions={0} | all-to-all | bytes 262144 | tf_op jit(solution)/shard_map/all_to_all | solution.py:437
  105.5 1.5 row_pass.3
  107.0 15.8 %all_to_all.46.recv_ref.refs_2_ = bf16[16,24,128]{2,1,0:T(8,128)(2,1)S(1)} all-to-all(bf16[16,24,128]{2,1,0:T(8,128)(2,1)S(1)} %row_pass.3), channel_id=1, replica_groups=mesh['y'=8,'core'=2,'z'=8,'xhi'=2,'xlo'=2] {'core','z'}, dimensions={0} | all-to-all | bytes 196608 | tf_op jit(solution)/shard_map/all_to_all | solution.py:437
  122.8 2.0 col_pass.2
  124.8 12.4 %all_to_all.47.refs_0_ = bf16[32,16,128]{2,1,0:T(8,128)(2,1)S(1)} all-to-all(bf16[32,16,128]{2,1,0:T(8,128)(2,1)S(1)} %col_pass.2), channel_id=1, replica_groups=mesh['y'=8,'core'=2,'z'=8,'xhi'=2,'xlo'=2] {'y','xhi','xlo'}, dimensions={0} | all-to-all | bytes 262144 | tf_op jit(solution)/shard_map/all_to_all | solution.py:437
  137.2 1.5 row_pass.4
  138.7 12.3 %all_to_all.48.recv_ref.norm_ref = bf16[16,24,128]{2,1,0:T(8,128)(2,1)S(1)} all-to-all(bf16[16,24,128]{2,1,0:T(8,128)(2,1)S(1)} %row_pass.4), channel_id=1, replica_groups=mesh['y'=8,'core'=2,'z'=8,'xhi'=2,'xlo'=2] {'core','z'}, dimensions={0} | all-to-all | bytes 196608 | tf_op jit(solution)/shard_map/all_to_all | solution.py:437
  151.1 2.0 col_pass.3
  153.0 12.5 %all_to_all.49.refs_0_.cols_ref = bf16[32,16,128]{2,1,0:T(8,128)(2,1)S(1)} all-to-all(bf16[32,16,128]{2,1,0:T(8,128)(2,1)S(1)} %col_pass.3), channel_id=1, replica_groups=mesh['y'=8,'core'=2,'z'=8,'xhi'=2,'xlo'=2] {'y','xhi','xlo'}, dimensions={0} | all-to-all | bytes 262144 | tf_op jit(solution)/shard_map/all_to_all | solution.py:437
  165.5 1.5 row_pass.5
  167.0 12.1 %all_to_all.50.recv_ref = bf16[16,16,128]{2,1,0:T(8,128)(2,1)S(1)} all-to-all(bf16[16,16,128]{2,1,0:T(8,128)(2,1)S(1)} %row_pass.5), channel_id=1, replica_groups=mesh['y'=8,'core'=2,'z'=8,'xhi'=2,'xlo'=2] {'core','z'}, dimensions={0} | all-to-all | bytes 131072 | tf_op jit(solution)/shard_map/all_to_all | solution.py:437
  179.1 4.7 %grad_pieces.1 = bf16[32,128,128]{2,1,0:T(8,128)(2,1)S(1)} custom-call(bf16[16,16,128]{2,1,0:T(8,128)(2,1)S(1)} %all_to_all.50.recv_ref, bf16[16,24,128]{2,1,0:T(8,128)(2,1)S(1)} %all_to_all.48.recv_ref.norm_ref, bf16[32,16,128]{2,1,0:T(8,128)(2,1)S(1)} %all_to_all.49.refs_0_.cols_ref, bf16[256,2048]{1,0:T(8,128)(2,1)S(1)} %get-tuple-element.44.turned_ref, ...), custom_call_target="tpu_custom_call" | custom-call | flops 4294967296 | bytes 16777216 | tf_op jit(solution)/shard_map/grad_pieces/pallas_call | solution.py:367
  183.8 27.7 %all_to_all.51.recv_ref = bf16[32,128,128]{2,1,0:T(8,128)(2,1)S(1)} all-to-all(bf16[32,128,128]{2,1,0:T(8,128)(2,1)S(1)} %grad_pieces.1), channel_id=1, replica_groups=mesh['y'=8,'core'=2,'z'=8,'xhi'=2,'xlo'=2] {'xlo','xhi','y'}, dimensions={0} | all-to-all | bytes 2097152 | tf_op jit(solution)/shard_map/all_to_all | solution.py:437
  211.5 0.3 weight_back.1
  211.9 22.4 %all_to_all.52.mine_ref = bf16[16,128,128]{2,1,0:T(8,128)(2,1)S(1)} all-to-all(bf16[16,128,128]{2,1,0:T(8,128)(2,1)S(1)} %weight_back.1), channel_id=1, replica_groups=mesh['y'=8,'core'=2,'z'=8,'xhi'=2,'xlo'=2] {'xhi','y'}, dimensions={0} | all-to-all | bytes 1048576 | tf_op jit(solution)/shard_map/all_to_all | solution.py:437
  234.3 1.3 collective-permute-start.3
  235.6 5.0 %collective-permute-done.3.other_ref = bf16[16,128,128]{2,1,0:T(8,128)(2,1)S(1)} collective-permute-done((bf16[16,128,128]{2,1,0:T(8,128)(2,1)S(1)}, bf16[16,128,128]{2,1,0:T(8,128)(2,1)S(1)}, u32[]{:S(2)}, u32[]{:S(2)}) %collective-permute-start.3) | collective-permute-done | bytes 524320 | tf_op jit(solution)/shard_map/ppermute | solution.py:485
  240.5 1.6 join_pieces.1
Async XLA Ops:
  33.0 42.0 %all-to-all-start = ((bf16[8,256,256]{2,1,0:T(8,128)(2,1)}), bf16[8,256,256]{2,1,0:T(8,128)(2,1)S(1)}, u32[]{:S(2)}, u32[]{:S(2)}) async-start(bf16[8,256,256]{2,1,0:T(8,128)(2,1)} %get-tuple-element.26), calls=%async_computation | async-start | bytes 2097152 | tf_op jit(solution)/shard_map/all_to_all | solution.py:437
  43.9 26.6 %collective-permute-start.1 = (bf16[2,256,1024]{2,1,0:T(8,128)(2,1)}, bf16[2,256,1024]{2,1,0:T(8,128)(2,1)S(1)}, u32[]{:S(2)}, u32[]{:S(2)}) collective-permute-start(bf16[2,256,1024]{2,1,0:T(8,128)(2,1)} %get-tuple-element.27.own_ref), channel_id=1, source_target_pairs={{1,2},{0,3},{35,32},{34,33},{5,6},{4,7},{39,36},{38,37},{9,10},{8,... | collective-permute-start | bytes 3145736 | tf_op jit(solution)/shard_map/ppermute | solution.py:452
  45.2 28.8 %collective-permute-start = (bf16[2,256,1024]{2,1,0:T(8,128)(2,1)}, bf16[2,256,1024]{2,1,0:T(8,128)(2,1)S(1)}, u32[]{:S(2)}, u32[]{:S(2)}) collective-permute-start(bf16[2,256,1024]{2,1,0:T(8,128)(2,1)} %get-tuple-element.27.own_ref), channel_id=1, source_target_pairs={{1,0},{0,1},{32,2},{33,3},{2,32},{3,33},{35,34},{34,35},{5,4},{4,5... | collective-permute-start | bytes 3145736 | tf_op jit(solution)/shard_map/ppermute | solution.py:452
  70.4 7.9 %copy-start = (bf16[2,256,1024]{2,1,0:T(8,128)(2,1)}, bf16[2,256,1024]{2,1,0:T(8,128)(2,1)S(1)}, u32[]{:S(2)}) copy-start(bf16[2,256,1024]{2,1,0:T(8,128)(2,1)S(1)} %collective-permute-done.1.far_ref) | copy-start | bytes 3145732
  74.0 1.0 copy-start.1
  75.0 6.2 %collective-permute-start.2 = (bf16[8,256,256]{2,1,0:T(8,128)(2,1)S(1)}, bf16[8,256,256]{2,1,0:T(8,128)(2,1)S(1)}, u32[]{:S(2)}, u32[]{:S(2)}) collective-permute-start(bf16[8,256,256]{2,1,0:T(8,128)(2,1)S(1)} %all-to-all-done.own_ref), channel_id=1, source_target_pairs={{0,32},{32,0},{1,33},{33,1},{2,34},{34,2},{3,35},{35,3},{4,36},{36... | collective-permute-start | bytes 3145736 | tf_op jit(solution)/shard_map/ppermute | solution.py:469
  234.3 6.3 %collective-permute-start.3 = (bf16[16,128,128]{2,1,0:T(8,128)(2,1)S(1)}, bf16[16,128,128]{2,1,0:T(8,128)(2,1)S(1)}, u32[]{:S(2)}, u32[]{:S(2)}) collective-permute-start(bf16[16,128,128]{2,1,0:T(8,128)(2,1)S(1)} %all_to_all.52.mine_ref), channel_id=1, source_target_pairs={{0,32},{34,2},{1,33},{35,3},{4,36},{38,6},{5,37},{39,7},{8,40},{42... | collective-permute-start | bytes 1572872 | tf_op jit(solution)/shard_map/ppermute | solution.py:485

commit v8 on v6

--- a/solution.py
+++ b/solution.py
@@ -50,7 +50,7 @@
     return pltpu.with_memory_space_constraint(values, pltpu.HBM)
 
 
-def rows_kernel(mask_ref, teacher_ref, student_ref, out_ref, index_ref, held_ref, sems):
+def rows_kernel(mask_ref, teacher_ref, student_ref, out_ref, index_ref, held_ref, made_ref, sems):
     copies = [
         pltpu.make_async_copy(mask_ref, index_ref, sems.at[0]),
         pltpu.make_async_copy(teacher_ref, held_ref.at[0], sems.at[1]),
@@ -67,8 +67,12 @@
         copies[1 + part].wait()
         rows = lax.dot_general(chosen, held_ref[part], TN, preferred_element_type=f32)
         square = jnp.sum(rows * rows, axis=1, keepdims=True)
-        rows = (rows * lax.rsqrt(square + epsilon)).astype(bf16)
-        out_ref[:, part * count : (part + 1) * count, :] = jnp.broadcast_to(rows[None], (out_ref.shape[0],) + rows.shape)
+        made_ref[part * count : (part + 1) * count, :] = (rows * lax.rsqrt(square + epsilon)).astype(bf16)
+    sends = [pltpu.make_async_copy(made_ref, out_ref.at[i], sems.at[3 + i]) for i in range(out_ref.shape[0])]
+    for send in sends:
+        send.start()
+    for send in sends:
+        send.wait()
 
 
 def masked_rows(mask, teacher, student, copies):
@@ -76,29 +80,30 @@
     return pl.pallas_call(
         rows_kernel,
         in_specs=[IN_HBM] * 3,
-        out_specs=IN_VMEM,
-        out_shape=jax.ShapeDtypeStruct((copies, 2 * count, width), bf16),
+        out_specs=IN_HBM,
+        out_shape=pltpu.HBM((copies, 2 * count, width), bf16),
         scratch_shapes=[
             pltpu.VMEM(mask.shape, jnp.int32),
             pltpu.VMEM((2,) + teacher.shape, bf16),
-            pltpu.SemaphoreType.DMA((3,)),
+            pltpu.VMEM((2 * count, width), bf16),
+            pltpu.SemaphoreType.DMA((3 + copies,)),
         ],
         compiler_params=params(),
         name="masked_rows",
     )(in_hbm(mask), in_hbm(teacher), in_hbm(student))
 
 
-def two_shards(flags_ref, own_ref, near_ref, far_ref, act):
+def two_shards(flags_ref, own_ref, first_ref, second_ref, act):
     @pl.when(flags_ref[2] == 1)
     def _():
-        act(own_ref, near_ref)
+        act(own_ref, first_ref)
 
     @pl.when(flags_ref[2] == 0)
     def _():
-        act(near_ref, far_ref)
-
-
-def protos_kernel(pieces, flags_ref, own_ref, near_ref, far_ref, out_ref, *piece_ref):
+        act(second_ref, first_ref)
+
+
+def protos_kernel(pieces, flags_ref, own_ref, first_in_ref, second_in_ref, out_ref, *piece_ref):
     columns = own_ref.shape[1]
     xlo = flags_ref[1]
 
@@ -116,10 +121,10 @@
             rows = block.shape[0] // 2
             piece_ref[0][...] = jnp.concatenate([block[:rows], block[rows:]], axis=1)
 
-    two_shards(flags_ref, own_ref, near_ref, far_ref, scaled)
-
-
-def prototypes(flags, own, near, far, pieces=0):
+    two_shards(flags_ref, own_ref, first_in_ref, second_in_ref, scaled)
+
+
+def prototypes(flags, own, first_in, second_in, pieces=0):
     rows, columns = own.shape
     shapes = [jax.ShapeDtypeStruct((rows, 2 * columns), bf16)]
     if pieces:
@@ -132,7 +137,7 @@
         compiler_params=params(),
         cost_estimate=cost(4 * rows * columns, 0, 8 * rows * columns),
         name="prototypes",
-    )(flags, own, near, far)
+    )(flags, own, first_in, second_in)
 
 
 def pack_piece(block, piece, pieces):
@@ -143,9 +148,9 @@
 
 
 def spread_cols(total, cols_ref):
-    for j in range(cols_ref.shape[1]):
-        part = total[:, j * LANES : (j + 1) * LANES]
-        cols_ref[:, j, :] = jnp.broadcast_to(part, (cols_ref.shape[0], LANES)).astype(bf16)
+    lines = cols_ref.shape[1]
+    block = jnp.concatenate([total[:, j * LANES : (j + 1) * LANES] for j in range(lines)], axis=0)
+    cols_ref[...] = jnp.broadcast_to(block[None], cols_ref.shape).astype(bf16)
 
 
 def net_rows(ref, net):
@@ -198,17 +203,21 @@
     count = codes_ref.shape[0]
     tiles = recv_ref.shape[1]
     lines = CHUNK // LANES
-    scale = lane_row(1.0 / jnp.sum(recv_ref[...].astype(f32), axis=0), 0, tiles)
+    scale = lane_row(1.0 / jnp.sum(recv_ref[...].astype(f32), axis=0), 0, tiles).astype(bf16)
     for i in range(count // CHUNK):
         blocks = []
         for k in range(lines):
             at = i * CHUNK + k * LANES
-            part = None
-            for j in range(tiles):
-                columns = slice(j * LANES, (j + 1) * LANES)
-                term = codes_ref[at : at + LANES, columns].astype(f32) * scale[:, columns]
-                part = term if part is None else part + term
-            blocks.append(part.astype(bf16))
+            total = None
+            for g in range(0, tiles, 8):
+                part = None
+                for j in range(g, g + 8):
+                    columns = slice(j * LANES, (j + 1) * LANES)
+                    term = codes_ref[at : at + LANES, columns] * scale[:, columns]
+                    part = term if part is None else part + term
+                part = part.astype(f32)
+                total = part if total is None else total + part
+            blocks.append(total.astype(bf16))
         block = jnp.broadcast_to(sum_lanes(jnp.concatenate(blocks, axis=0))[None], (out_ref.shape[0], lines, LANES))
         out_ref[:, i * lines : (i + 1) * lines, :] = block.astype(bf16)
     first = count // LANES
@@ -249,6 +258,7 @@
         row = jnp.where(first, lane_row(scale, i * lines, lines), 0.0).astype(bf16)
         spreads.append(lax.dot_general(row, ones, TN, preferred_element_type=f32).astype(bf16))
     width = 8 * LANES
+    totals = []
     for h in range(columns // width):
         total = jnp.zeros((16, width), f32)
         for i, spread in enumerate(spreads):
@@ -264,10 +274,8 @@
                         part = term if part is None else part + term
                     parts.append(part.astype(f32))
                 total = total + jnp.concatenate(parts, axis=1)
-        total = jnp.sum(total, axis=0, keepdims=True)
-        for j in range(width // LANES):
-            part = jnp.broadcast_to(total[:, j * LANES : (j + 1) * LANES], (cols_ref.shape[0], LANES))
-            cols_ref[:, h * (width // LANES) + j, :] = part.astype(bf16)
+        totals.append(jnp.sum(total, axis=0, keepdims=True))
+    spread_cols(jnp.concatenate(totals, axis=1), cols_ref)
 
 
 def col_pass(recv, codes, groups):
@@ -416,19 +424,20 @@
     return lax.all_to_all(values, axes, 0, 0, tiled=True)
 
 
-def shard_permutes(weight):
+def shard_permutes(weight, pair):
     axes = ("core", "xhi", "xlo")
-    near, far = [], []
+    first, second = [], []
     for core in range(2):
         for xhi in range(2):
             for xlo in range(2):
                 here = core * 4 + xhi * 2 + xlo
                 if xhi == core:
-                    near.append((core * 4 + xhi * 2 + 1 - xlo, here))
+                    first.append((core * 4 + xhi * 2 + 1 - xlo, here))
                 else:
-                    near.append(((1 - core) * 4 + core * 2 + xlo, here))
-                    far.append((core * 4 + core * 2 + 1 - xlo, here))
-    return lax.ppermute(weight, axes, near), lax.ppermute(weight, axes, far)
+                    first.append(((1 - core) * 4 + core * 2 + 1 - xlo, here))
+                    second.append((core * 4 + (xhi if pair else core) * 2 + 1 - xlo, here))
+    once = lax.ppermute(weight, axes, first)
+    return once, lax.ppermute(once, axes, second)
 
 
 def shards(teacher_patches, student_patches, mask_index, teacher_weight, student_weight):
@@ -439,14 +448,14 @@
     matched = (core == xhi).astype(jnp.int32)
     flags = jnp.stack([core, xlo, matched, lax.axis_index(SHARD_PEERS)]).astype(jnp.int32)
 
-    teach_near, teach_far = shard_permutes(teacher_weight)
-    stud_near, stud_far = shard_permutes(student_weight)
-    (teach_protos,) = prototypes(flags, teacher_weight, teach_near, teach_far)
+    teach_first, teach_second = shard_permutes(teacher_weight, True)
+    stud_first, stud_second = shard_permutes(student_weight, False)
+    (teach_protos,) = prototypes(flags, teacher_weight, teach_first, teach_second)
     line = masked_rows(mask_index.reshape(1, -1), teacher_patches, student_patches, size("z"))
     line = exchange(line, "z")
-    line, teach_protos, stud_near, stud_far = lax.optimization_barrier((line, teach_protos, stud_near, stud_far))
+    line, teach_protos, stud_first, stud_second = lax.optimization_barrier((line, teach_protos, stud_first, stud_second))
     other = lax.ppermute(line, "core", [(0, 1), (1, 0)])
-    stud_protos, weight = prototypes(flags, student_weight, stud_near, stud_far, shard_pieces)
+    stud_protos, weight = prototypes(flags, student_weight, stud_first, stud_second, shard_pieces)
     other, stud_protos, weight = lax.optimization_barrier((other, stud_protos, weight))
 
     codes, cols = first_codes(flags, line, other, teach_protos, column_peers)

time: 213 us -> 210 us (0.986)
  waiting for transfers between devices: 21.4 us -> 18.4 us
    ppermute x4, waiting for transfers between devices: 15.8 us -> 13.2 us  [the longest x2 8.33 us: shard_permutes(): once = lax.ppermute(weight, axes, first)]
where the time goes in v8:
time: 210 us
  blocking collectives  135 us (64%)
  Pallas kernels  24.9 us (12%)
  starting transfers between devices  24.9 us (12%)
  waiting for transfers between devices  18.4 us (9%)
  local copies, waits for them, and re-layouts  5.77 us (3%)
    all_to_all x8, blocking collectives, exchange(): return lax.all_to_all(values, axes, 0, 0, tiled=True)  135 us
    all_to_all x1, starting transfers between devices, exchange(): return lax.all_to_all(values, axes, 0, 0, tiled=True)  10.9 us
    ppermute x2, waiting for transfers between devices, shard_permutes(): once = lax.ppermute(weight, axes, first)  8.33 us
    ppermute x2, starting transfers between devices, shard_permutes(): once = lax.ppermute(weight, axes, first)  7.14 us
    unnamed x12, local copies, waits for them, and re-layouts  5.77 us
    ppermute x1, waiting for transfers between devices, shards(): other = lax.ppermute(mine, ('core', 'xhi'), [(0, 2), (3, 1)])  4.95 us
    ppermute x2, waiting for transfers between devices, shard_permutes(): return (once, lax.ppermute(once, axes, second))  4.9 us
    pallas_call x1, Pallas kernels, grad_pieces(): pl.pallas_call(grad_kernel, in_specs=[IN_VMEM] * 6, out_specs=IN_VMEM, ou...  4.59 us
  transfers between devices with their start and end apart: 7, of which 6 were waited for; matrix products, arithmetic and copies ran while one was open for 0% of the time, Pallas kernels for 1%

profile of v8, /device:TPU:1, one launch (start us, length us, event | category | flops | bytes accessed | tf_op | source)
XLA Modules:
  0.0 209.6 jit_solution(1605753411895017510)
XLA Ops:
  0.0 2.5 %masked_rows.1 = bf16[8,256,256]{2,1,0:T(8,128)(2,1)} custom-call(s32[1,128]{1,0:T(1,128)} %bitcast.5, bf16[256,256]{1,0:T(8,128)(2,1)} %teacher_ref.1, bf16[256,256]{1,0:T(8,128)(2,1)} %student_ref.1), custom_call_target="tpu_custom_call" | custom-call | tf_op jit(solution)/shard_map/masked_rows/pallas_call | solution.py:80
  2.6 10.9 %all-to-all-start = ((bf16[8,256,256]{2,1,0:T(8,128)(2,1)}), bf16[8,256,256]{2,1,0:T(8,128)(2,1)S(1)}, u32[]{:S(2)}, u32[]{:S(2)}) async-start(bf16[8,256,256]{2,1,0:T(8,128)(2,1)} %masked_rows.1), calls=%async_computation | async-start | bytes 2097152 | tf_op jit(solution)/shard_map/all_to_all | solution.py:424
  13.4 5.2 %collective-permute-start = (bf16[256,1024]{1,0:T(8,128)(2,1)}, bf16[256,1024]{1,0:T(8,128)(2,1)S(1)}, u32[]{:S(2)}, u32[]{:S(2)}) collective-permute-start(bf16[256,1024]{1,0:T(8,128)(2,1)} %own_ref.2), channel_id=1, source_target_pairs={{1,0},{0,1},{33,2},{32,3},{3,32},{2,33},{35,34},{34,35},{5,4},{4,5... | collective-permute-start | bytes 1572872 | tf_op jit(solution)/shard_map/ppermute | solution.py:439
  18.7 1.9 collective-permute-start.2
  20.6 5.4 %collective-permute-done.first_in_ref = bf16[256,1024]{1,0:T(8,128)(2,1)S(1)} collective-permute-done((bf16[256,1024]{1,0:T(8,128)(2,1)}, bf16[256,1024]{1,0:T(8,128)(2,1)S(1)}, u32[]{:S(2)}, u32[]{:S(2)}) %collective-permute-start) | collective-permute-done | bytes 524320 | tf_op jit(solution)/shard_map/ppermute | solution.py:439
  26.0 1.9 collective-permute-start.1
  27.9 0.0 copy-start.2
  27.9 0.8 copy-done.2
  28.7 2.9 %collective-permute-done.2.first_in_ref = bf16[256,1024]{1,0:T(8,128)(2,1)S(1)} collective-permute-done((bf16[256,1024]{1,0:T(8,128)(2,1)}, bf16[256,1024]{1,0:T(8,128)(2,1)S(1)}, u32[]{:S(2)}, u32[]{:S(2)}) %collective-permute-start.2) | collective-permute-done | bytes 524320 | tf_op jit(solution)/shard_map/ppermute | solution.py:439
  31.6 1.3 collective-permute-start.3
  32.9 0.1 pad_add_fusion.flags_ref
  33.0 3.2 %collective-permute-done.1.second_in_ref = bf16[256,1024]{1,0:T(8,128)(2,1)S(1)} collective-permute-done((bf16[256,1024]{1,0:T(8,128)(2,1)S(1)}, bf16[256,1024]{1,0:T(8,128)(2,1)S(1)}, u32[]{:S(2)}, u32[]{:S(2)}) %collective-permute-start.1) | collective-permute-done | bytes 524320 | tf_op jit(solution)/shard_map/ppermute | solution.py:440
  36.2 0.0 copy-start.4
  36.2 0.8 copy-done.4
  37.0 0.0 copy-start.1
  37.0 1.0 copy-done.1
  38.1 0.0 copy-start.3
  38.1 1.0 copy-done.3
  39.1 0.0 copy-start.5
  39.1 1.0 copy-done.5
  40.2 0.9 prototypes.2.protos_ref
  41.1 1.7 collective-permute-done.3.second_in_ref
  42.8 0.0 all-to-all-done.own_ref
  42.8 2.4 %collective-permute-start.4 = (bf16[8,256,256]{2,1,0:T(8,128)(2,1)S(1)}, bf16[8,256,256]{2,1,0:T(8,128)(2,1)S(1)}, u32[]{:S(2)}, u32[]{:S(2)}) collective-permute-start(bf16[8,256,256]{2,1,0:T(8,128)(2,1)S(1)} %all-to-all-done.own_ref), channel_id=1, source_target_pairs={{0,32},{32,0},{1,33},{33,1},{2,34},{34,2},{3,35},{35,3},{4,36},{36... | collective-permute-start | bytes 3145736 | tf_op jit(solution)/shard_map/ppermute | solution.py:457
  45.2 0.0 copy-start
  45.2 1.0 copy-done
  46.2 0.9 prototypes.3
  47.2 0.3 collective-permute-done.4.other_ref
  47.4 2.9 %first_codes.1 = (bf16[2048,2048]{1,0:T(8,128)(2,1)S(1)}, bf16[32,16,128]{2,1,0:T(8,128)(2,1)S(1)}) custom-call(s32[4]{0:T(128)S(1)} %pad_add_fusion.flags_ref, bf16[8,256,256]{2,1,0:T(8,128)(2,1)S(1)} %all-to-all-done.own_ref, bf16[8,256,256]{2,1,0:T(8,128)(2,1)S(1)} %collective-permute-done.4.other_ref, bf16[256,2048]{1,0:T(8,128)(2,1)S(1)} %prototypes.2.protos_ref), custom_call_target="tpu_custom_call" | custom-call | flops 2147483648 | bytes 8388608 | tf_op jit(solution)/shard_map/first_codes/pallas_call | solution.py:179
  50.4 3.3 %student_expo.1 = (bf16[2048,2048]{1,0:T(8,128)(2,1)S(1)}, f32[16,128]{1,0:T(8,128)S(1)}, bf16[256,2048]{1,0:T(8,128)(2,1)S(1)}) custom-call(s32[4]{0:T(128)S(1)} %pad_add_fusion.flags_ref, bf16[8,256,256]{2,1,0:T(8,128)(2,1)S(1)} %all-to-all-done.own_ref, bf16[8,256,256]{2,1,0:T(8,128)(2,1)S(1)} %collective-permute-done.4.other_ref, ...), custom_call_target="tpu_custom_call" | custom-call | flops 2147483648 | bytes 8388608 | tf_op jit(solution)/shard_map/student_expo/pallas_call | solution.py:316
  53.6 19.5 %all_to_all.45.refs_0_ = bf16[32,16,128]{2,1,0:T(8,128)(2,1)S(1)} all-to-all(bf16[32,16,128]{2,1,0:T(8,128)(2,1)S(1)} %get-tuple-element.35), channel_id=1, replica_groups=mesh['y'=8,'core'=2,'z'=8,'xhi'=2,'xlo'=2] {'y','xhi','xlo'}, dimensions={0} | all-to-all | bytes 262144 | tf_op jit(solution)/shard_map/all_to_all | solution.py:424
  73.1 1.5 row_pass.3
  74.6 16.5 %all_to_all.46.recv_ref.refs_2_ = bf16[16,24,128]{2,1,0:T(8,128)(2,1)S(1)} all-to-all(bf16[16,24,128]{2,1,0:T(8,128)(2,1)S(1)} %row_pass.3), channel_id=1, replica_groups=mesh['y'=8,'core'=2,'z'=8,'xhi'=2,'xlo'=2] {'core','z'}, dimensions={0} | all-to-all | bytes 196608 | tf_op jit(solution)/shard_map/all_to_all | solution.py:424
  91.0 1.7 col_pass.2
  92.8 12.5 %all_to_all.47.refs_0_ = bf16[32,16,128]{2,1,0:T(8,128)(2,1)S(1)} all-to-all(bf16[32,16,128]{2,1,0:T(8,128)(2,1)S(1)} %col_pass.2), channel_id=1, replica_groups=mesh['y'=8,'core'=2,'z'=8,'xhi'=2,'xlo'=2] {'y','xhi','xlo'}, dimensions={0} | all-to-all | bytes 262144 | tf_op jit(solution)/shard_map/all_to_all | solution.py:424
  105.2 1.5 row_pass.4
  106.7 12.2 %all_to_all.48.recv_ref.norm_ref = bf16[16,24,128]{2,1,0:T(8,128)(2,1)S(1)} all-to-all(bf16[16,24,128]{2,1,0:T(8,128)(2,1)S(1)} %row_pass.4), channel_id=1, replica_groups=mesh['y'=8,'core'=2,'z'=8,'xhi'=2,'xlo'=2] {'core','z'}, dimensions={0} | all-to-all | bytes 196608 | tf_op jit(solution)/shard_map/all_to_all | solution.py:424
  118.9 1.8 col_pass.3
  120.7 12.5 %all_to_all.49.refs_0_.cols_ref = bf16[32,16,128]{2,1,0:T(8,128)(2,1)S(1)} all-to-all(bf16[32,16,128]{2,1,0:T(8,128)(2,1)S(1)} %col_pass.3), channel_id=1, replica_groups=mesh['y'=8,'core'=2,'z'=8,'xhi'=2,'xlo'=2] {'y','xhi','xlo'}, dimensions={0} | all-to-all | bytes 262144 | tf_op jit(solution)/shard_map/all_to_all | solution.py:424
  133.2 1.4 row_pass.5
  134.6 12.1 %all_to_all.50.recv_ref = bf16[16,16,128]{2,1,0:T(8,128)(2,1)S(1)} all-to-all(bf16[16,16,128]{2,1,0:T(8,128)(2,1)S(1)} %row_pass.5), channel_id=1, replica_groups=mesh['y'=8,'core'=2,'z'=8,'xhi'=2,'xlo'=2] {'core','z'}, dimensions={0} | all-to-all | bytes 131072 | tf_op jit(solution)/shard_map/all_to_all | solution.py:424
  146.7 4.6 %grad_pieces.1 = bf16[32,128,128]{2,1,0:T(8,128)(2,1)S(1)} custom-call(bf16[16,16,128]{2,1,0:T(8,128)(2,1)S(1)} %all_to_all.50.recv_ref, bf16[16,24,128]{2,1,0:T(8,128)(2,1)S(1)} %all_to_all.48.recv_ref.norm_ref, bf16[32,16,128]{2,1,0:T(8,128)(2,1)S(1)} %all_to_all.49.refs_0_.cols_ref, bf16[256,2048]{1,0:T(8,128)(2,1)S(1)} %get-tuple-element.38.turned_ref, ...), custom_call_target="tpu_custom_call" | custom-call | flops 4294967296 | bytes 16777216 | tf_op jit(solution)/shard_map/grad_pieces/pallas_call | solution.py:354
  151.3 27.7 %all_to_all.51.recv_ref = bf16[32,128,128]{2,1,0:T(8,128)(2,1)S(1)} all-to-all(bf16[32,128,128]{2,1,0:T(8,128)(2,1)S(1)} %grad_pieces.1), channel_id=1, replica_groups=mesh['y'=8,'core'=2,'z'=8,'xhi'=2,'xlo'=2] {'xlo','xhi','y'}, dimensions={0} | all-to-all | bytes 2097152 | tf_op jit(solution)/shard_map/all_to_all | solution.py:424
  179.0 0.3 weight_back.1
  179.4 22.4 %all_to_all.52.mine_ref = bf16[16,128,128]{2,1,0:T(8,128)(2,1)S(1)} all-to-all(bf16[16,128,128]{2,1,0:T(8,128)(2,1)S(1)} %weight_back.1), channel_id=1, replica_groups=mesh['y'=8,'core'=2,'z'=8,'xhi'=2,'xlo'=2] {'xhi','y'}, dimensions={0} | all-to-all | bytes 1048576 | tf_op jit(solution)/shard_map/all_to_all | solution.py:424
  201.8 1.3 collective-permute-start.5
  203.1 5.0 %collective-permute-done.5.other_ref = bf16[16,128,128]{2,1,0:T(8,128)(2,1)S(1)} collective-permute-done((bf16[16,128,128]{2,1,0:T(8,128)(2,1)S(1)}, bf16[16,128,128]{2,1,0:T(8,128)(2,1)S(1)}, u32[]{:S(2)}, u32[]{:S(2)}) %collective-permute-start.5) | collective-permute-done | bytes 524320 | tf_op jit(solution)/shard_map/ppermute | solution.py:473
  208.0 1.6 join_pieces.1
Async XLA Ops:
  2.6 40.2 %all-to-all-start = ((bf16[8,256,256]{2,1,0:T(8,128)(2,1)}), bf16[8,256,256]{2,1,0:T(8,128)(2,1)S(1)}, u32[]{:S(2)}, u32[]{:S(2)}) async-start(bf16[8,256,256]{2,1,0:T(8,128)(2,1)} %masked_rows.1), calls=%async_computation | async-start | bytes 2097152 | tf_op jit(solution)/shard_map/all_to_all | solution.py:424
  13.4 12.6 %collective-permute-start = (bf16[256,1024]{1,0:T(8,128)(2,1)}, bf16[256,1024]{1,0:T(8,128)(2,1)S(1)}, u32[]{:S(2)}, u32[]{:S(2)}) collective-permute-start(bf16[256,1024]{1,0:T(8,128)(2,1)} %own_ref.2), channel_id=1, source_target_pairs={{1,0},{0,1},{33,2},{32,3},{3,32},{2,33},{35,34},{34,35},{5,4},{4,5... | collective-permute-start | bytes 1572872 | tf_op jit(solution)/shard_map/ppermute | solution.py:439
  18.7 13.0 %collective-permute-start.2 = (bf16[256,1024]{1,0:T(8,128)(2,1)}, bf16[256,1024]{1,0:T(8,128)(2,1)S(1)}, u32[]{:S(2)}, u32[]{:S(2)}) collective-permute-start(bf16[256,1024]{1,0:T(8,128)(2,1)} %own_ref.3), channel_id=1, source_target_pairs={{1,0},{0,1},{33,2},{32,3},{3,32},{2,33},{35,34},{34,35},{5,4},{4,5... | collective-permute-start | bytes 1572872 | tf_op jit(solution)/shard_map/ppermute | solution.py:439
  26.0 10.2 %collective-permute-start.1 = (bf16[256,1024]{1,0:T(8,128)(2,1)S(1)}, bf16[256,1024]{1,0:T(8,128)(2,1)S(1)}, u32[]{:S(2)}, u32[]{:S(2)}) collective-permute-start(bf16[256,1024]{1,0:T(8,128)(2,1)S(1)} %collective-permute-done.first_in_ref), channel_id=1, source_target_pairs={{3,2},{2,3},{33,32},{32,33},{7,6},{6,7},{37,36},{36,37},{11,10},{1... | collective-permute-start | bytes 1572872 | tf_op jit(solution)/shard_map/ppermute | solution.py:440
  27.9 0.8 copy-start.2
  31.6 11.1 %collective-permute-start.3 = (bf16[256,1024]{1,0:T(8,128)(2,1)S(1)}, bf16[256,1024]{1,0:T(8,128)(2,1)S(1)}, u32[]{:S(2)}, u32[]{:S(2)}) collective-permute-start(bf16[256,1024]{1,0:T(8,128)(2,1)S(1)} %collective-permute-done.2.first_in_ref), channel_id=1, source_target_pairs={{1,2},{0,3},{35,32},{34,33},{5,6},{4,7},{39,36},{38,37},{9,10},{8,... | collective-permute-start | bytes 1572872 | tf_op jit(solution)/shard_map/ppermute | solution.py:440
  36.2 0.8 copy-start.4
  37.0 1.0 copy-start.1
  38.1 1.0 copy-start.3
  39.1 1.0 copy-start.5
  42.8 4.7 %collective-permute-start.4 = (bf16[8,256,256]{2,1,0:T(8,128)(2,1)S(1)}, bf16[8,256,256]{2,1,0:T(8,128)(2,1)S(1)}, u32[]{:S(2)}, u32[]{:S(2)}) collective-permute-start(bf16[8,256,256]{2,1,0:T(8,128)(2,1)S(1)} %all-to-all-done.own_ref), channel_id=1, source_target_pairs={{0,32},{32,0},{1,33},{33,1},{2,34},{34,2},{3,35},{35,3},{4,36},{36... | collective-permute-start | bytes 3145736 | tf_op jit(solution)/shard_map/ppermute | solution.py:457
  45.2 1.0 copy-start
  201.8 6.2 %collective-permute-start.5 = (bf16[16,128,128]{2,1,0:T(8,128)(2,1)S(1)}, bf16[16,128,128]{2,1,0:T(8,128)(2,1)S(1)}, u32[]{:S(2)}, u32[]{:S(2)}) collective-permute-start(bf16[16,128,128]{2,1,0:T(8,128)(2,1)S(1)} %all_to_all.52.mine_ref), channel_id=1, source_target_pairs={{0,32},{34,2},{1,33},{35,3},{4,36},{38,6},{5,37},{39,7},{8,40},{42... | collective-permute-start | bytes 1572872 | tf_op jit(solution)/shard_map/ppermute | solution.py:473

commit v9 on v8

--- a/solution.py
+++ b/solution.py
@@ -103,41 +103,51 @@
         act(second_ref, first_ref)
 
 
-def protos_kernel(pieces, flags_ref, own_ref, first_in_ref, second_in_ref, out_ref, *piece_ref):
+def protos_kernel(pieces, flags_ref, own_ref, first_ref, second_ref, out_ref, *rest):
+    piece_ref, held_ref, sems = rest if pieces else (None,) + rest
+
+    def bring(one, other):
+        copies = [
+            pltpu.make_async_copy(one, held_ref.at[0], sems.at[0]),
+            pltpu.make_async_copy(other, held_ref.at[1], sems.at[1]),
+        ]
+        for copy in copies:
+            copy.start()
+        for copy in copies:
+            copy.wait()
+
+    two_shards(flags_ref, own_ref, first_ref, second_ref, bring)
     columns = own_ref.shape[1]
     xlo = flags_ref[1]
-
-    def scaled(first, second):
-        for ref, place in ((first, xlo), (second, 1 - xlo)):
-            values = ref[...].astype(f32)
-            square = jnp.sum(values * values, axis=0, keepdims=True)
-            at = pl.multiple_of(place * columns, columns)
-            out_ref[:, pl.ds(at, columns)] = (values * lax.rsqrt(square + epsilon)).astype(bf16)
-        if pieces:
-            index = flags_ref[3]
-            half = columns // pieces
-            block = first[:, pl.ds(pl.multiple_of(index // 2 * LANES, LANES), LANES)].astype(f32)
-            block = jnp.where(index % 2 == 0, block[:, :half], block[:, half:])
-            rows = block.shape[0] // 2
-            piece_ref[0][...] = jnp.concatenate([block[:rows], block[rows:]], axis=1)
-
-    two_shards(flags_ref, own_ref, first_in_ref, second_in_ref, scaled)
-
-
-def prototypes(flags, own, first_in, second_in, pieces=0):
+    for part, place in ((0, xlo), (1, 1 - xlo)):
+        values = held_ref[part].astype(f32)
+        square = jnp.sum(values * values, axis=0, keepdims=True)
+        at = pl.multiple_of(place * columns, columns)
+        out_ref[:, pl.ds(at, columns)] = (values * lax.rsqrt(square + epsilon)).astype(bf16)
+    if pieces:
+        index = flags_ref[3]
+        half = columns // pieces
+        block = held_ref[0, :, pl.ds(pl.multiple_of(index // 2 * LANES, LANES), LANES)].astype(f32)
+        block = jnp.where(index % 2 == 0, block[:, :half], block[:, half:])
+        rows = block.shape[0] // 2
+        piece_ref[...] = jnp.concatenate([block[:rows], block[rows:]], axis=1)
+
+
+def prototypes(flags, own, first, second, pieces=0):
     rows, columns = own.shape
     shapes = [jax.ShapeDtypeStruct((rows, 2 * columns), bf16)]
     if pieces:
         shapes.append(jax.ShapeDtypeStruct((rows // 2, 2 * columns // pieces), f32))
     return pl.pallas_call(
         functools.partial(protos_kernel, pieces),
-        in_specs=[IN_SMEM] + [IN_VMEM] * 3,
+        in_specs=[IN_SMEM] + [IN_HBM] * 3,
         out_specs=[IN_VMEM] * len(shapes),
         out_shape=shapes,
+        scratch_shapes=[pltpu.VMEM((2, rows, columns), bf16), pltpu.SemaphoreType.DMA((2,))],
         compiler_params=params(),
         cost_estimate=cost(4 * rows * columns, 0, 8 * rows * columns),
         name="prototypes",
-    )(flags, own, first_in, second_in)
+    )(flags, in_hbm(own), in_hbm(first), in_hbm(second))
 
 
 def pack_piece(block, piece, pieces):
@@ -374,50 +384,41 @@
     inverse = lax.rsqrt(column_sum(weight * weight) + epsilon)
     along = column_sum(grad * weight)
     back = (grad * inverse - weight * (inverse * inverse * inverse * along)).astype(bf16)
-    out_ref[...] = jnp.broadcast_to(back[None], out_ref.shape)
-
-
-def weight_back(recv, weight, copies):
+    out_ref[...] = back
+
+
+def weight_back(recv, weight):
     return pl.pallas_call(
         back_kernel,
         in_specs=[IN_VMEM, IN_VMEM],
         out_specs=IN_VMEM,
-        out_shape=jax.ShapeDtypeStruct((copies,) + weight.shape, bf16),
+        out_shape=jax.ShapeDtypeStruct(weight.shape, bf16),
         compiler_params=params(),
         name="weight_back",
     )(recv, weight)
 
 
-def join_kernel(flags_ref, mine_ref, other_ref, out_ref):
-    pieces, rows, lanes = mine_ref.shape
+def join_kernel(pieces_ref, out_ref):
+    pieces, rows, lanes = pieces_ref.shape
     half = lanes // 2
-
-    def join(ref):
-        for pair in range(pieces // 2):
-            left, right = ref[2 * pair], ref[2 * pair + 1]
-            columns = pl.ds(pair * lanes, lanes)
-            out_ref[:rows, columns] = jnp.concatenate([left[:, :half], right[:, :half]], axis=1)
-            out_ref[rows:, columns] = jnp.concatenate([left[:, half:], right[:, half:]], axis=1)
-
-    @pl.when(flags_ref[2] == 1)
-    def _():
-        join(mine_ref)
-
-    @pl.when(flags_ref[2] == 0)
-    def _():
-        join(other_ref)
-
-
-def join_pieces(flags, mine, other):
-    count, rows, lanes = mine.shape
+    for pair in range(pieces // 2):
+        at = [2 * (index % (pieces // 2)) + index // (pieces // 2) for index in (2 * pair, 2 * pair + 1)]
+        left, right = pieces_ref[at[0]], pieces_ref[at[1]]
+        columns = pl.ds(pair * lanes, lanes)
+        out_ref[:rows, columns] = jnp.concatenate([left[:, :half], right[:, :half]], axis=1)
+        out_ref[rows:, columns] = jnp.concatenate([left[:, half:], right[:, half:]], axis=1)
+
+
+def join_pieces(pieces):
+    count, rows, lanes = pieces.shape
     return pl.pallas_call(
         join_kernel,
-        in_specs=[IN_SMEM, IN_VMEM, IN_VMEM],
+        in_specs=[IN_VMEM],
         out_specs=IN_VMEM,
-        out_shape=jax.ShapeDtypeStruct((2 * rows, count * lanes // 2), mine.dtype),
+        out_shape=jax.ShapeDtypeStruct((2 * rows, count * lanes // 2), pieces.dtype),
         compiler_params=params(),
         name="join_pieces",
-    )(flags, mine, other)
+    )(pieces)
 
 
 def exchange(values, axes):
@@ -450,13 +451,15 @@
 
     teach_first, teach_second = shard_permutes(teacher_weight, True)
     stud_first, stud_second = shard_permutes(student_weight, False)
-    (teach_protos,) = prototypes(flags, teacher_weight, teach_first, teach_second)
     line = masked_rows(mask_index.reshape(1, -1), teacher_patches, student_patches, size("z"))
     line = exchange(line, "z")
-    line, teach_protos, stud_first, stud_second = lax.optimization_barrier((line, teach_protos, stud_first, stud_second))
+    line, teach_first, teach_second, stud_first, stud_second = lax.optimization_barrier(
+        (line, teach_first, teach_second, stud_first, stud_second)
+    )
     other = lax.ppermute(line, "core", [(0, 1), (1, 0)])
+    (teach_protos,) = prototypes(flags, teacher_weight, teach_first, teach_second)
     stud_protos, weight = prototypes(flags, student_weight, stud_first, stud_second, shard_pieces)
-    other, stud_protos, weight = lax.optimization_barrier((other, stud_protos, weight))
+    other, teach_protos, stud_protos, weight = lax.optimization_barrier((other, teach_protos, stud_protos, weight))
 
     codes, cols = first_codes(flags, line, other, teach_protos, column_peers)
     expo, norm, turned = student_expo(flags, line, other, stud_protos)
@@ -469,9 +472,10 @@
     cols = exchange(col_pass(rows, codes, column_peers), COLUMN_PEERS)
     rows = exchange(row_pass(cols, codes, row_peers), ROW_PEERS)
     pieces = exchange(grad_pieces(rows, norm, cols, turned, codes, expo, 2 * shard_pieces), PIECE_PEERS)
-    mine = exchange(weight_back(pieces, weight, shard_pieces), SHARD_PEERS)
-    other = lax.ppermute(mine, ("core", "xhi"), [(0, 2), (3, 1)])
-    return join_pieces(flags, mine, other)
+    mine = weight_back(pieces, weight)
+    other = lax.ppermute(mine, ("core", "xhi"), [(1, 2), (2, 1)])
+    piece = jnp.where(matched == 1, mine, other)
+    return join_pieces(lax.all_gather(piece, ("y", "core"), axis=0))
 
 
 def solution(mesh):

time: 210 us -> 209 us (level)
  blocking collectives: 135 us -> 129 us
  starting transfers between devices: 24.9 us -> 30.9 us
  local copies, waits for them, and re-layouts: 5.77 us -> 0.01 us
  waiting for transfers between devices: 18.4 us -> 20.5 us
    all_to_all x8 -> x7, blocking collectives: 135 us -> 113 us  [exchange(): return lax.all_to_all(values, axes, 0, 0, tiled=True)]
    all_gather x0 -> x1, blocking collectives: none -> 16.4 us  [shards(): return join_pieces(lax.all_gather(piece, ('y', 'core'), axis=0))]
    ppermute x1, starting transfers between devices: 1.28 us -> 7.27 us  [shards(): other = lax.ppermute(mine, ('core', 'xhi'), [(1, 2), (2, 1)])]
    unnamed x12 -> x8, local copies, waits for them, and re-layouts: 5.77 us -> 0.01 us
    ppermute x2, waiting for transfers between devices: 4.9 us -> 9.83 us  [shard_permutes(): return (once, lax.ppermute(once, axes, second))]
    ppermute x1, waiting for transfers between devices: 4.95 us -> 1.58 us  [shards(): other = lax.ppermute(mine, ('core', 'xhi'), [(1, 2), (2, 1)])]
    pallas_call x2, Pallas kernels: 1.84 us -> 4.31 us  [prototypes(): pl.pallas_call(functools.partial(protos_kernel, pieces), in_specs=[IN_SME...]
  transfers between devices with their start and end apart: 7 -> 7, of which waited for: 6 -> 5; matrix products, arithmetic and copies ran while one was open for 0% -> 0% of each run, Pallas kernels for 1% -> 2%
where the time goes in v9:
time: 209 us; the launch traced here: 208 us
  blocking collectives  129 us (62%)
  starting transfers between devices  30.9 us (15%)
  Pallas kernels  26.8 us (13%)
  waiting for transfers between devices  20.5 us (10%)
    all_to_all x7, blocking collectives, exchange(): return lax.all_to_all(values, axes, 0, 0, tiled=True)  113 us
    all_gather x1, blocking collectives, shards(): return join_pieces(lax.all_gather(piece, ('y', 'core'), axis=0))  16.4 us
    all_to_all x1, starting transfers between devices, exchange(): return lax.all_to_all(values, axes, 0, 0, tiled=True)  10.9 us
    ppermute x2, waiting for transfers between devices, shard_permutes(): return (once, lax.ppermute(once, axes, second))  9.83 us
    ppermute x2, waiting for transfers between devices, shard_permutes(): once = lax.ppermute(weight, axes, first)  9.12 us
    ppermute x1, starting transfers between devices, shards(): other = lax.ppermute(mine, ('core', 'xhi'), [(1, 2), (2, 1)])  7.27 us
    ppermute x2, starting transfers between devices, shard_permutes(): once = lax.ppermute(weight, axes, first)  7.14 us
    pallas_call x1, Pallas kernels, grad_pieces(): pl.pallas_call(grad_kernel, in_specs=[IN_VMEM] * 6, out_specs=IN_VMEM, ou...  4.59 us
  transfers between devices with their start and end apart: 7, of which 5 were waited for; matrix products, arithmetic and copies ran while one was open for 0% of the time, Pallas kernels for 2%

profile of v9, /device:TPU:1, one launch (start us, length us, event | category | flops | bytes accessed | tf_op | source)
XLA Modules:
  0.0 207.8 jit_solution(18293226759882537893)
XLA Ops:
  0.0 2.6 %masked_rows.1 = bf16[8,256,256]{2,1,0:T(8,128)(2,1)} custom-call(s32[1,128]{1,0:T(1,128)} %bitcast.7, bf16[256,256]{1,0:T(8,128)(2,1)} %teacher_ref.1, bf16[256,256]{1,0:T(8,128)(2,1)} %student_ref.1), custom_call_target="tpu_custom_call" | custom-call | tf_op jit(solution)/shard_map/masked_rows/pallas_call | solution.py:80
  2.6 10.9 %all-to-all-start = ((bf16[8,256,256]{2,1,0:T(8,128)(2,1)}), bf16[8,256,256]{2,1,0:T(8,128)(2,1)S(1)}, u32[]{:S(2)}, u32[]{:S(2)}) async-start(bf16[8,256,256]{2,1,0:T(8,128)(2,1)} %masked_rows.1), calls=%async_computation | async-start | bytes 2097152 | tf_op jit(solution)/shard_map/all_to_all | solution.py:425
  13.4 5.2 %collective-permute-start = (bf16[256,1024]{1,0:T(8,128)(2,1)}, bf16[256,1024]{1,0:T(8,128)(2,1)S(1)}, u32[]{:S(2)}, u32[]{:S(2)}) collective-permute-start(bf16[256,1024]{1,0:T(8,128)(2,1)} %own_ref.2), channel_id=1, source_target_pairs={{1,0},{0,1},{33,2},{32,3},{3,32},{2,33},{35,34},{34,35},{5,4},{4,5... | collective-permute-start | bytes 1572872 | tf_op jit(solution)/shard_map/ppermute | solution.py:440
  18.7 1.9 collective-permute-start.2
  20.6 5.4 %collective-permute-done.first_ref = bf16[256,1024]{1,0:T(8,128)(2,1)S(1)} collective-permute-done((bf16[256,1024]{1,0:T(8,128)(2,1)}, bf16[256,1024]{1,0:T(8,128)(2,1)S(1)}, u32[]{:S(2)}, u32[]{:S(2)}) %collective-permute-start) | collective-permute-done | bytes 524320 | tf_op jit(solution)/shard_map/ppermute | solution.py:440
  26.0 0.0 copy-start.2
  26.0 1.9 collective-permute-start.1
  27.9 3.7 %collective-permute-done.2.first_ref = bf16[256,1024]{1,0:T(8,128)(2,1)S(1)} collective-permute-done((bf16[256,1024]{1,0:T(8,128)(2,1)}, bf16[256,1024]{1,0:T(8,128)(2,1)S(1)}, u32[]{:S(2)}, u32[]{:S(2)}) %collective-permute-start.2) | collective-permute-done | bytes 524320 | tf_op jit(solution)/shard_map/ppermute | solution.py:440
  31.6 0.0 copy-start
  31.6 1.3 collective-permute-start.3
  32.9 3.3 %collective-permute-done.1.second_ref = bf16[256,1024]{1,0:T(8,128)(2,1)S(1)} collective-permute-done((bf16[256,1024]{1,0:T(8,128)(2,1)S(1)}, bf16[256,1024]{1,0:T(8,128)(2,1)S(1)}, u32[]{:S(2)}, u32[]{:S(2)}) %collective-permute-start.1) | collective-permute-done | bytes 524320 | tf_op jit(solution)/shard_map/ppermute | solution.py:441
  36.2 0.0 copy-start.3
  36.2 6.5 %collective-permute-done.3.second_ref = bf16[256,1024]{1,0:T(8,128)(2,1)S(1)} collective-permute-done((bf16[256,1024]{1,0:T(8,128)(2,1)S(1)}, bf16[256,1024]{1,0:T(8,128)(2,1)S(1)}, u32[]{:S(2)}, u32[]{:S(2)}) %collective-permute-start.3) | collective-permute-done | bytes 524320 | tf_op jit(solution)/shard_map/ppermute | solution.py:441
  42.8 0.0 copy-done.2
  42.8 0.0 copy-done.3
  42.8 0.0 copy-start.1
  42.8 0.0 all-to-all-done.own_ref
  42.8 2.4 %collective-permute-start.4 = (bf16[8,256,256]{2,1,0:T(8,128)(2,1)S(1)}, bf16[8,256,256]{2,1,0:T(8,128)(2,1)S(1)}, u32[]{:S(2)}, u32[]{:S(2)}) collective-permute-start(bf16[8,256,256]{2,1,0:T(8,128)(2,1)S(1)} %all-to-all-done.own_ref), channel_id=1, source_target_pairs={{0,32},{32,0},{1,33},{33,1},{2,34},{34,2},{3,35},{35,3},{4,36},{36... | collective-permute-start | bytes 3145736 | tf_op jit(solution)/shard_map/ppermute | solution.py:459
  45.2 0.1 pad_add_fusion.flags_ref
  45.3 2.1 %prototypes.2.protos_ref = bf16[256,2048]{1,0:T(8,128)(2,1)S(1)} custom-call(s32[4]{0:T(128)S(1)} %pad_add_fusion.flags_ref, bf16[256,1024]{1,0:T(8,128)(2,1)} %own_ref.2, bf16[256,1024]{1,0:T(8,128)(2,1)} %copy-done.2, bf16[256,1024]{1,0:T(8,128)(2,1)} %copy-done.3), custom_call_target="tpu_custom_call" | custom-call | flops 1048576 | bytes 2097152 | tf_op jit(solution)/shard_map/prototypes/pallas_call | solution.py:141
  47.4 0.0 copy-done
  47.4 0.0 copy-done.1
  47.5 2.2 %prototypes.3 = (bf16[256,2048]{1,0:T(8,128)(2,1)S(1)}, f32[128,128]{1,0:T(8,128)S(1)}) custom-call(s32[4]{0:T(128)S(1)} %pad_add_fusion.flags_ref, bf16[256,1024]{1,0:T(8,128)(2,1)} %own_ref.3, bf16[256,1024]{1,0:T(8,128)(2,1)} %copy-done, bf16[256,1024]{1,0:T(8,128)(2,1)} %copy-done.1), custom_call_target="tpu_custom_call" | custom-call | flops 1048576 | bytes 2097152 | tf_op jit(solution)/shard_map/prototypes/pallas_call | solution.py:141
  49.6 0.0 collective-permute-done.4.other_ref
  49.6 2.9 %first_codes.1 = (bf16[2048,2048]{1,0:T(8,128)(2,1)S(1)}, bf16[32,16,128]{2,1,0:T(8,128)(2,1)S(1)}) custom-call(s32[4]{0:T(128)S(1)} %pad_add_fusion.flags_ref, bf16[8,256,256]{2,1,0:T(8,128)(2,1)S(1)} %all-to-all-done.own_ref, bf16[8,256,256]{2,1,0:T(8,128)(2,1)S(1)} %collective-permute-done.4.other_ref, bf16[256,2048]{1,0:T(8,128)(2,1)S(1)} %prototypes.2.protos_ref), custom_call_target="tpu_custom_call" | custom-call | flops 2147483648 | bytes 8388608 | tf_op jit(solution)/shard_map/first_codes/pallas_call | solution.py:189
  52.6 3.3 %student_expo.1 = (bf16[2048,2048]{1,0:T(8,128)(2,1)S(1)}, f32[16,128]{1,0:T(8,128)S(1)}, bf16[256,2048]{1,0:T(8,128)(2,1)S(1)}) custom-call(s32[4]{0:T(128)S(1)} %pad_add_fusion.flags_ref, bf16[8,256,256]{2,1,0:T(8,128)(2,1)S(1)} %all-to-all-done.own_ref, bf16[8,256,256]{2,1,0:T(8,128)(2,1)S(1)} %collective-permute-done.4.other_ref, ...), custom_call_target="tpu_custom_call" | custom-call | flops 2147483648 | bytes 8388608 | tf_op jit(solution)/shard_map/student_expo/pallas_call | solution.py:326
  55.8 20.1 %all_to_all.40.refs_0_ = bf16[32,16,128]{2,1,0:T(8,128)(2,1)S(1)} all-to-all(bf16[32,16,128]{2,1,0:T(8,128)(2,1)S(1)} %get-tuple-element.39), channel_id=1, replica_groups=mesh['y'=8,'core'=2,'z'=8,'xhi'=2,'xlo'=2] {'y','xhi','xlo'}, dimensions={0} | all-to-all | bytes 262144 | tf_op jit(solution)/shard_map/all_to_all | solution.py:425
  75.9 1.5 row_pass.3
  77.4 15.8 %all_to_all.41.recv_ref.refs_2_ = bf16[16,24,128]{2,1,0:T(8,128)(2,1)S(1)} all-to-all(bf16[16,24,128]{2,1,0:T(8,128)(2,1)S(1)} %row_pass.3), channel_id=1, replica_groups=mesh['y'=8,'core'=2,'z'=8,'xhi'=2,'xlo'=2] {'core','z'}, dimensions={0} | all-to-all | bytes 196608 | tf_op jit(solution)/shard_map/all_to_all | solution.py:425
  93.1 1.8 col_pass.2
  94.9 12.5 %all_to_all.42.refs_0_ = bf16[32,16,128]{2,1,0:T(8,128)(2,1)S(1)} all-to-all(bf16[32,16,128]{2,1,0:T(8,128)(2,1)S(1)} %col_pass.2), channel_id=1, replica_groups=mesh['y'=8,'core'=2,'z'=8,'xhi'=2,'xlo'=2] {'y','xhi','xlo'}, dimensions={0} | all-to-all | bytes 262144 | tf_op jit(solution)/shard_map/all_to_all | solution.py:425
  107.4 1.5 row_pass.4
  108.9 12.2 %all_to_all.43.recv_ref.norm_ref = bf16[16,24,128]{2,1,0:T(8,128)(2,1)S(1)} all-to-all(bf16[16,24,128]{2,1,0:T(8,128)(2,1)S(1)} %row_pass.4), channel_id=1, replica_groups=mesh['y'=8,'core'=2,'z'=8,'xhi'=2,'xlo'=2] {'core','z'}, dimensions={0} | all-to-all | bytes 196608 | tf_op jit(solution)/shard_map/all_to_all | solution.py:425
  121.1 1.8 col_pass.3
  122.9 12.5 %all_to_all.44.refs_0_.cols_ref = bf16[32,16,128]{2,1,0:T(8,128)(2,1)S(1)} all-to-all(bf16[32,16,128]{2,1,0:T(8,128)(2,1)S(1)} %col_pass.3), channel_id=1, replica_groups=mesh['y'=8,'core'=2,'z'=8,'xhi'=2,'xlo'=2] {'y','xhi','xlo'}, dimensions={0} | all-to-all | bytes 262144 | tf_op jit(solution)/shard_map/all_to_all | solution.py:425
  135.4 1.4 row_pass.5
  136.8 12.1 %all_to_all.45.recv_ref = bf16[16,16,128]{2,1,0:T(8,128)(2,1)S(1)} all-to-all(bf16[16,16,128]{2,1,0:T(8,128)(2,1)S(1)} %row_pass.5), channel_id=1, replica_groups=mesh['y'=8,'core'=2,'z'=8,'xhi'=2,'xlo'=2] {'core','z'}, dimensions={0} | all-to-all | bytes 131072 | tf_op jit(solution)/shard_map/all_to_all | solution.py:425
  148.9 4.6 %grad_pieces.1 = bf16[32,128,128]{2,1,0:T(8,128)(2,1)S(1)} custom-call(bf16[16,16,128]{2,1,0:T(8,128)(2,1)S(1)} %all_to_all.45.recv_ref, bf16[16,24,128]{2,1,0:T(8,128)(2,1)S(1)} %all_to_all.43.recv_ref.norm_ref, bf16[32,16,128]{2,1,0:T(8,128)(2,1)S(1)} %all_to_all.44.refs_0_.cols_ref, bf16[256,2048]{1,0:T(8,128)(2,1)S(1)} %get-tuple-element.42.turned_ref, ...), custom_call_target="tpu_custom_call" | custom-call | flops 4294967296 | bytes 16777216 | tf_op jit(solution)/shard_map/grad_pieces/pallas_call | solution.py:364
  153.5 27.7 %all_to_all.46.recv_ref = bf16[32,128,128]{2,1,0:T(8,128)(2,1)S(1)} all-to-all(bf16[32,128,128]{2,1,0:T(8,128)(2,1)S(1)} %grad_pieces.1), channel_id=1, replica_groups=mesh['y'=8,'core'=2,'z'=8,'xhi'=2,'xlo'=2] {'xlo','xhi','y'}, dimensions={0} | all-to-all | bytes 2097152 | tf_op jit(solution)/shard_map/all_to_all | solution.py:425
  181.2 0.3 weight_back.1
  181.5 7.3 %collective-permute-start.5 = (bf16[128,128]{1,0:T(8,128)(2,1)S(1)}, bf16[128,128]{1,0:T(8,128)(2,1)S(1)}, u32[]{:S(2)}, u32[]{:S(2)}) collective-permute-start(bf16[128,128]{1,0:T(8,128)(2,1)S(1)} %weight_back.1), channel_id=1, source_target_pairs={{2,32},{32,2},{3,33},{33,3},{6,36},{36,6},{7,37},{37,7},{10,40},{4... | collective-permute-start | bytes 98312 | tf_op jit(solution)/shard_map/ppermute | solution.py:476
  188.8 1.6 collective-permute-done.5
  190.4 16.4 %all-gather = bf16[2048,128]{1,0:T(8,128)(2,1)S(1)} all-gather(bf16[128,128]{1,0:T(8,128)(2,1)S(1)} %broadcast_select_fusion), channel_id=2, replica_groups=mesh['y'=8,'core'=2,'z'=8,'xhi'=2,'xlo'=2] {'y','core'}, dimensions={0}, use_global_device_ids=true | all-gather | bytes 557056 | tf_op jit(solution)/shard_map/all_gather | solution.py:478
  206.8 1.0 join_pieces.1
  (1 shorter events, 0.0 us)
Async XLA Ops:
  2.6 40.2 %all-to-all-start = ((bf16[8,256,256]{2,1,0:T(8,128)(2,1)}), bf16[8,256,256]{2,1,0:T(8,128)(2,1)S(1)}, u32[]{:S(2)}, u32[]{:S(2)}) async-start(bf16[8,256,256]{2,1,0:T(8,128)(2,1)} %masked_rows.1), calls=%async_computation | async-start | bytes 2097152 | tf_op jit(solution)/shard_map/all_to_all | solution.py:425
  13.4 12.6 %collective-permute-start = (bf16[256,1024]{1,0:T(8,128)(2,1)}, bf16[256,1024]{1,0:T(8,128)(2,1)S(1)}, u32[]{:S(2)}, u32[]{:S(2)}) collective-permute-start(bf16[256,1024]{1,0:T(8,128)(2,1)} %own_ref.2), channel_id=1, source_target_pairs={{1,0},{0,1},{33,2},{32,3},{3,32},{2,33},{35,34},{34,35},{5,4},{4,5... | collective-permute-start | bytes 1572872 | tf_op jit(solution)/shard_map/ppermute | solution.py:440
  18.7 13.0 %collective-permute-start.2 = (bf16[256,1024]{1,0:T(8,128)(2,1)}, bf16[256,1024]{1,0:T(8,128)(2,1)S(1)}, u32[]{:S(2)}, u32[]{:S(2)}) collective-permute-start(bf16[256,1024]{1,0:T(8,128)(2,1)} %own_ref.3), channel_id=1, source_target_pairs={{1,0},{0,1},{33,2},{32,3},{3,32},{2,33},{35,34},{34,35},{5,4},{4,5... | collective-permute-start | bytes 1572872 | tf_op jit(solution)/shard_map/ppermute | solution.py:440
  26.0 16.7 %copy-start.2 = (bf16[256,1024]{1,0:T(8,128)(2,1)}, bf16[256,1024]{1,0:T(8,128)(2,1)S(1)}, u32[]{:S(2)}) copy-start(bf16[256,1024]{1,0:T(8,128)(2,1)S(1)} %collective-permute-done.first_ref) | copy-start | bytes 1572868
  26.0 10.2 %collective-permute-start.1 = (bf16[256,1024]{1,0:T(8,128)(2,1)S(1)}, bf16[256,1024]{1,0:T(8,128)(2,1)S(1)}, u32[]{:S(2)}, u32[]{:S(2)}) collective-permute-start(bf16[256,1024]{1,0:T(8,128)(2,1)S(1)} %collective-permute-done.first_ref), channel_id=1, source_target_pairs={{3,2},{2,3},{33,32},{32,33},{7,6},{6,7},{37,36},{36,37},{11,10},{1... | collective-permute-start | bytes 1572872 | tf_op jit(solution)/shard_map/ppermute | solution.py:441
  31.6 15.8 %copy-start = (bf16[256,1024]{1,0:T(8,128)(2,1)}, bf16[256,1024]{1,0:T(8,128)(2,1)S(1)}, u32[]{:S(2)}) copy-start(bf16[256,1024]{1,0:T(8,128)(2,1)S(1)} %collective-permute-done.2.first_ref) | copy-start | bytes 1572868
  31.6 11.1 %collective-permute-start.3 = (bf16[256,1024]{1,0:T(8,128)(2,1)S(1)}, bf16[256,1024]{1,0:T(8,128)(2,1)S(1)}, u32[]{:S(2)}, u32[]{:S(2)}) collective-permute-start(bf16[256,1024]{1,0:T(8,128)(2,1)S(1)} %collective-permute-done.2.first_ref), channel_id=1, source_target_pairs={{1,2},{0,3},{35,32},{34,33},{5,6},{4,7},{39,36},{38,37},{9,10},{8,... | collective-permute-start | bytes 1572872 | tf_op jit(solution)/shard_map/ppermute | solution.py:441
  36.2 6.6 %copy-start.3 = (bf16[256,1024]{1,0:T(8,128)(2,1)}, bf16[256,1024]{1,0:T(8,128)(2,1)S(1)}, u32[]{:S(2)}) copy-start(bf16[256,1024]{1,0:T(8,128)(2,1)S(1)} %collective-permute-done.1.second_ref) | copy-start | bytes 1572868
  42.8 4.7 %copy-start.1 = (bf16[256,1024]{1,0:T(8,128)(2,1)}, bf16[256,1024]{1,0:T(8,128)(2,1)S(1)}, u32[]{:S(2)}) copy-start(bf16[256,1024]{1,0:T(8,128)(2,1)S(1)} %collective-permute-done.3.second_ref) | copy-start | bytes 1572868
  42.8 6.9 %collective-permute-start.4 = (bf16[8,256,256]{2,1,0:T(8,128)(2,1)S(1)}, bf16[8,256,256]{2,1,0:T(8,128)(2,1)S(1)}, u32[]{:S(2)}, u32[]{:S(2)}) collective-permute-start(bf16[8,256,256]{2,1,0:T(8,128)(2,1)S(1)} %all-to-all-done.own_ref), channel_id=1, source_target_pairs={{0,32},{32,0},{1,33},{33,1},{2,34},{34,2},{3,35},{35,3},{4,36},{36... | collective-permute-start | bytes 3145736 | tf_op jit(solution)/shard_map/ppermute | solution.py:459
  181.5 8.9 %collective-permute-start.5 = (bf16[128,128]{1,0:T(8,128)(2,1)S(1)}, bf16[128,128]{1,0:T(8,128)(2,1)S(1)}, u32[]{:S(2)}, u32[]{:S(2)}) collective-permute-start(bf16[128,128]{1,0:T(8,128)(2,1)S(1)} %weight_back.1), channel_id=1, source_target_pairs={{2,32},{32,2},{3,33},{33,3},{6,36},{36,6},{7,37},{37,7},{10,40},{4... | collective-permute-start | bytes 98312 | tf_op jit(solution)/shard_map/ppermute | solution.py:476

commit v10 on v9

--- a/solution.py
+++ b/solution.py
@@ -453,11 +453,9 @@
     stud_first, stud_second = shard_permutes(student_weight, False)
     line = masked_rows(mask_index.reshape(1, -1), teacher_patches, student_patches, size("z"))
     line = exchange(line, "z")
-    line, teach_first, teach_second, stud_first, stud_second = lax.optimization_barrier(
-        (line, teach_first, teach_second, stud_first, stud_second)
-    )
+    (teach_protos,) = prototypes(flags, teacher_weight, teach_first, teach_second)
+    line, teach_protos, stud_first, stud_second = lax.optimization_barrier((line, teach_protos, stud_first, stud_second))
     other = lax.ppermute(line, "core", [(0, 1), (1, 0)])
-    (teach_protos,) = prototypes(flags, teacher_weight, teach_first, teach_second)
     stud_protos, weight = prototypes(flags, student_weight, stud_first, stud_second, shard_pieces)
     other, teach_protos, stud_protos, weight = lax.optimization_barrier((other, teach_protos, stud_protos, weight))
 

time: 209 us -> 207 us (level)
  waiting for transfers between devices: 20.5 us -> 18.4 us
    ppermute x2, waiting for transfers between devices: 9.83 us -> 7.59 us  [shard_permutes(): return (once, lax.ppermute(once, axes, second))]
  transfers between devices with their start and end apart: 7 -> 7, of which waited for: 5 -> 6; matrix products, arithmetic and copies ran while one was open for 0% -> 0% of each run, Pallas kernels for 2% -> 2%
where the time goes in v10:
time: 207 us; the launch traced here: 206 us
  blocking collectives  129 us (62%)
  starting transfers between devices  30.9 us (15%)
  Pallas kernels  26.8 us (13%)
  waiting for transfers between devices  18.4 us (9%)
    all_to_all x7, blocking collectives, exchange(): return lax.all_to_all(values, axes, 0, 0, tiled=True)  113 us
    all_gather x1, blocking collectives, shards(): return join_pieces(lax.all_gather(piece, ('y', 'core'), axis=0))  16.4 us
    all_to_all x1, starting transfers between devices, exchange(): return lax.all_to_all(values, axes, 0, 0, tiled=True)  10.9 us
    ppermute x2, waiting for transfers between devices, shard_permutes(): once = lax.ppermute(weight, axes, first)  9.12 us
    ppermute x2, waiting for transfers between devices, shard_permutes(): return (once, lax.ppermute(once, axes, second))  7.59 us
    ppermute x1, starting transfers between devices, shards(): other = lax.ppermute(mine, ('core', 'xhi'), [(1, 2), (2, 1)])  7.28 us
    ppermute x2, starting transfers between devices, shard_permutes(): once = lax.ppermute(weight, axes, first)  7.14 us
    pallas_call x1, Pallas kernels, grad_pieces(): pl.pallas_call(grad_kernel, in_specs=[IN_VMEM] * 6, out_specs=IN_VMEM, ou...  4.59 us
  transfers between devices with their start and end apart: 7, of which 6 were waited for; matrix products, arithmetic and copies ran while one was open for 0% of the time, Pallas kernels for 2%

profile of v10, /device:TPU:1, one launch (start us, length us, event | category | flops | bytes accessed | tf_op | source)
XLA Modules:
  0.0 205.6 jit_solution(11832042179694849410)
XLA Ops:
  0.0 2.5 %masked_rows.1 = bf16[8,256,256]{2,1,0:T(8,128)(2,1)} custom-call(s32[1,128]{1,0:T(1,128)} %bitcast.7, bf16[256,256]{1,0:T(8,128)(2,1)} %teacher_ref.1, bf16[256,256]{1,0:T(8,128)(2,1)} %student_ref.1), custom_call_target="tpu_custom_call" | custom-call | tf_op jit(solution)/shard_map/masked_rows/pallas_call | solution.py:80
  2.5 10.9 %all-to-all-start = ((bf16[8,256,256]{2,1,0:T(8,128)(2,1)}), bf16[8,256,256]{2,1,0:T(8,128)(2,1)S(1)}, u32[]{:S(2)}, u32[]{:S(2)}) async-start(bf16[8,256,256]{2,1,0:T(8,128)(2,1)} %masked_rows.1), calls=%async_computation | async-start | bytes 2097152 | tf_op jit(solution)/shard_map/all_to_all | solution.py:425
  13.4 5.2 %collective-permute-start = (bf16[256,1024]{1,0:T(8,128)(2,1)}, bf16[256,1024]{1,0:T(8,128)(2,1)S(1)}, u32[]{:S(2)}, u32[]{:S(2)}) collective-permute-start(bf16[256,1024]{1,0:T(8,128)(2,1)} %own_ref.2), channel_id=1, source_target_pairs={{1,0},{0,1},{33,2},{32,3},{3,32},{2,33},{35,34},{34,35},{5,4},{4,5... | collective-permute-start | bytes 1572872 | tf_op jit(solution)/shard_map/ppermute | solution.py:440
  18.7 1.9 collective-permute-start.2
  20.6 5.4 %collective-permute-done.first_ref = bf16[256,1024]{1,0:T(8,128)(2,1)S(1)} collective-permute-done((bf16[256,1024]{1,0:T(8,128)(2,1)}, bf16[256,1024]{1,0:T(8,128)(2,1)S(1)}, u32[]{:S(2)}, u32[]{:S(2)}) %collective-permute-start) | collective-permute-done | bytes 524320 | tf_op jit(solution)/shard_map/ppermute | solution.py:440
  26.0 0.0 copy-start.2
  26.0 1.9 collective-permute-start.1
  27.9 3.7 %collective-permute-done.2.first_ref = bf16[256,1024]{1,0:T(8,128)(2,1)S(1)} collective-permute-done((bf16[256,1024]{1,0:T(8,128)(2,1)}, bf16[256,1024]{1,0:T(8,128)(2,1)S(1)}, u32[]{:S(2)}, u32[]{:S(2)}) %collective-permute-start.2) | collective-permute-done | bytes 524320 | tf_op jit(solution)/shard_map/ppermute | solution.py:440
  31.6 0.0 copy-start
  31.6 1.3 collective-permute-start.3
  32.9 0.1 pad_add_fusion.flags_ref
  33.0 0.0 copy-done.2
  33.0 3.3 %collective-permute-done.1.second_ref = bf16[256,1024]{1,0:T(8,128)(2,1)} collective-permute-done((bf16[256,1024]{1,0:T(8,128)(2,1)S(1)}, bf16[256,1024]{1,0:T(8,128)(2,1)}, u32[]{:S(2)}, u32[]{:S(2)}) %collective-permute-start.1) | collective-permute-done | bytes 524320 | tf_op jit(solution)/shard_map/ppermute | solution.py:441
  36.3 2.1 %prototypes.2.protos_ref = bf16[256,2048]{1,0:T(8,128)(2,1)S(1)} custom-call(s32[4]{0:T(128)S(1)} %pad_add_fusion.flags_ref, bf16[256,1024]{1,0:T(8,128)(2,1)} %own_ref.2, bf16[256,1024]{1,0:T(8,128)(2,1)} %copy-done.2, bf16[256,1024]{1,0:T(8,128)(2,1)} %collective-permute-done.1.second_ref), custom_call_target="tpu_custom_call" | custom-call | flops 1048576 | bytes 2097152 | tf_op jit(solution)/shard_map/prototypes/pallas_call | solution.py:141
  38.5 4.3 %collective-permute-done.3.second_ref = bf16[256,1024]{1,0:T(8,128)(2,1)S(1)} collective-permute-done((bf16[256,1024]{1,0:T(8,128)(2,1)S(1)}, bf16[256,1024]{1,0:T(8,128)(2,1)S(1)}, u32[]{:S(2)}, u32[]{:S(2)}) %collective-permute-start.3) | collective-permute-done | bytes 524320 | tf_op jit(solution)/shard_map/ppermute | solution.py:441
  42.8 0.0 copy-start.1
  42.8 0.0 all-to-all-done.own_ref
  42.8 2.4 %collective-permute-start.4 = (bf16[8,256,256]{2,1,0:T(8,128)(2,1)S(1)}, bf16[8,256,256]{2,1,0:T(8,128)(2,1)S(1)}, u32[]{:S(2)}, u32[]{:S(2)}) collective-permute-start(bf16[8,256,256]{2,1,0:T(8,128)(2,1)S(1)} %all-to-all-done.own_ref), channel_id=1, source_target_pairs={{0,32},{32,0},{1,33},{33,1},{2,34},{34,2},{3,35},{35,3},{4,36},{36... | collective-permute-start | bytes 3145736 | tf_op jit(solution)/shard_map/ppermute | solution.py:458
  45.2 0.0 copy-done
  45.2 0.0 copy-done.1
  45.2 2.2 %prototypes.3 = (bf16[256,2048]{1,0:T(8,128)(2,1)S(1)}, f32[128,128]{1,0:T(8,128)S(1)}) custom-call(s32[4]{0:T(128)S(1)} %pad_add_fusion.flags_ref, bf16[256,1024]{1,0:T(8,128)(2,1)} %own_ref.3, bf16[256,1024]{1,0:T(8,128)(2,1)} %copy-done, bf16[256,1024]{1,0:T(8,128)(2,1)} %copy-done.1), custom_call_target="tpu_custom_call" | custom-call | flops 1048576 | bytes 2097152 | tf_op jit(solution)/shard_map/prototypes/pallas_call | solution.py:141
  47.4 0.1 collective-permute-done.4.other_ref
  47.4 2.9 %first_codes.1 = (bf16[2048,2048]{1,0:T(8,128)(2,1)S(1)}, bf16[32,16,128]{2,1,0:T(8,128)(2,1)S(1)}) custom-call(s32[4]{0:T(128)S(1)} %pad_add_fusion.flags_ref, bf16[8,256,256]{2,1,0:T(8,128)(2,1)S(1)} %all-to-all-done.own_ref, bf16[8,256,256]{2,1,0:T(8,128)(2,1)S(1)} %collective-permute-done.4.other_ref, bf16[256,2048]{1,0:T(8,128)(2,1)S(1)} %prototypes.2.protos_ref), custom_call_target="tpu_custom_call" | custom-call | flops 2147483648 | bytes 8388608 | tf_op jit(solution)/shard_map/first_codes/pallas_call | solution.py:189
  50.4 3.3 %student_expo.1 = (bf16[2048,2048]{1,0:T(8,128)(2,1)S(1)}, f32[16,128]{1,0:T(8,128)S(1)}, bf16[256,2048]{1,0:T(8,128)(2,1)S(1)}) custom-call(s32[4]{0:T(128)S(1)} %pad_add_fusion.flags_ref, bf16[8,256,256]{2,1,0:T(8,128)(2,1)S(1)} %all-to-all-done.own_ref, bf16[8,256,256]{2,1,0:T(8,128)(2,1)S(1)} %collective-permute-done.4.other_ref, ...), custom_call_target="tpu_custom_call" | custom-call | flops 2147483648 | bytes 8388608 | tf_op jit(solution)/shard_map/student_expo/pallas_call | solution.py:326
  53.6 19.5 %all_to_all.40.refs_0_ = bf16[32,16,128]{2,1,0:T(8,128)(2,1)S(1)} all-to-all(bf16[32,16,128]{2,1,0:T(8,128)(2,1)S(1)} %get-tuple-element.37), channel_id=1, replica_groups=mesh['y'=8,'core'=2,'z'=8,'xhi'=2,'xlo'=2] {'y','xhi','xlo'}, dimensions={0} | all-to-all | bytes 262144 | tf_op jit(solution)/shard_map/all_to_all | solution.py:425
  73.1 1.5 row_pass.3
  74.6 16.5 %all_to_all.41.recv_ref.refs_2_ = bf16[16,24,128]{2,1,0:T(8,128)(2,1)S(1)} all-to-all(bf16[16,24,128]{2,1,0:T(8,128)(2,1)S(1)} %row_pass.3), channel_id=1, replica_groups=mesh['y'=8,'core'=2,'z'=8,'xhi'=2,'xlo'=2] {'core','z'}, dimensions={0} | all-to-all | bytes 196608 | tf_op jit(solution)/shard_map/all_to_all | solution.py:425
  91.0 1.7 col_pass.2
  92.8 12.5 %all_to_all.42.refs_0_ = bf16[32,16,128]{2,1,0:T(8,128)(2,1)S(1)} all-to-all(bf16[32,16,128]{2,1,0:T(8,128)(2,1)S(1)} %col_pass.2), channel_id=1, replica_groups=mesh['y'=8,'core'=2,'z'=8,'xhi'=2,'xlo'=2] {'y','xhi','xlo'}, dimensions={0} | all-to-all | bytes 262144 | tf_op jit(solution)/shard_map/all_to_all | solution.py:425
  105.3 1.5 row_pass.4
  106.7 12.2 %all_to_all.43.recv_ref.norm_ref = bf16[16,24,128]{2,1,0:T(8,128)(2,1)S(1)} all-to-all(bf16[16,24,128]{2,1,0:T(8,128)(2,1)S(1)} %row_pass.4), channel_id=1, replica_groups=mesh['y'=8,'core'=2,'z'=8,'xhi'=2,'xlo'=2] {'core','z'}, dimensions={0} | all-to-all | bytes 196608 | tf_op jit(solution)/shard_map/all_to_all | solution.py:425
  118.9 1.8 col_pass.3
  120.7 12.5 %all_to_all.44.refs_0_.cols_ref = bf16[32,16,128]{2,1,0:T(8,128)(2,1)S(1)} all-to-all(bf16[32,16,128]{2,1,0:T(8,128)(2,1)S(1)} %col_pass.3), channel_id=1, replica_groups=mesh['y'=8,'core'=2,'z'=8,'xhi'=2,'xlo'=2] {'y','xhi','xlo'}, dimensions={0} | all-to-all | bytes 262144 | tf_op jit(solution)/shard_map/all_to_all | solution.py:425
  133.2 1.4 row_pass.5
  134.6 12.1 %all_to_all.45.recv_ref = bf16[16,16,128]{2,1,0:T(8,128)(2,1)S(1)} all-to-all(bf16[16,16,128]{2,1,0:T(8,128)(2,1)S(1)} %row_pass.5), channel_id=1, replica_groups=mesh['y'=8,'core'=2,'z'=8,'xhi'=2,'xlo'=2] {'core','z'}, dimensions={0} | all-to-all | bytes 131072 | tf_op jit(solution)/shard_map/all_to_all | solution.py:425
  146.7 4.6 %grad_pieces.1 = bf16[32,128,128]{2,1,0:T(8,128)(2,1)S(1)} custom-call(bf16[16,16,128]{2,1,0:T(8,128)(2,1)S(1)} %all_to_all.45.recv_ref, bf16[16,24,128]{2,1,0:T(8,128)(2,1)S(1)} %all_to_all.43.recv_ref.norm_ref, bf16[32,16,128]{2,1,0:T(8,128)(2,1)S(1)} %all_to_all.44.refs_0_.cols_ref, bf16[256,2048]{1,0:T(8,128)(2,1)S(1)} %get-tuple-element.40.turned_ref, ...), custom_call_target="tpu_custom_call" | custom-call | flops 4294967296 | bytes 16777216 | tf_op jit(solution)/shard_map/grad_pieces/pallas_call | solution.py:364
  151.3 27.7 %all_to_all.46.recv_ref = bf16[32,128,128]{2,1,0:T(8,128)(2,1)S(1)} all-to-all(bf16[32,128,128]{2,1,0:T(8,128)(2,1)S(1)} %grad_pieces.1), channel_id=1, replica_groups=mesh['y'=8,'core'=2,'z'=8,'xhi'=2,'xlo'=2] {'xlo','xhi','y'}, dimensions={0} | all-to-all | bytes 2097152 | tf_op jit(solution)/shard_map/all_to_all | solution.py:425
  179.0 0.3 weight_back.1
  179.3 7.3 %collective-permute-start.5 = (bf16[128,128]{1,0:T(8,128)(2,1)S(1)}, bf16[128,128]{1,0:T(8,128)(2,1)S(1)}, u32[]{:S(2)}, u32[]{:S(2)}) collective-permute-start(bf16[128,128]{1,0:T(8,128)(2,1)S(1)} %weight_back.1), channel_id=1, source_target_pairs={{2,32},{32,2},{3,33},{33,3},{6,36},{36,6},{7,37},{37,7},{10,40},{4... | collective-permute-start | bytes 98312 | tf_op jit(solution)/shard_map/ppermute | solution.py:474
  186.6 1.6 collective-permute-done.5
  188.2 16.4 %all-gather = bf16[2048,128]{1,0:T(8,128)(2,1)S(1)} all-gather(bf16[128,128]{1,0:T(8,128)(2,1)S(1)} %broadcast_select_fusion), channel_id=2, replica_groups=mesh['y'=8,'core'=2,'z'=8,'xhi'=2,'xlo'=2] {'y','core'}, dimensions={0}, use_global_device_ids=true | all-gather | bytes 557056 | tf_op jit(solution)/shard_map/all_gather | solution.py:476
  204.6 1.0 join_pieces.1
  (1 shorter events, 0.0 us)
Async XLA Ops:
  2.5 40.2 %all-to-all-start = ((bf16[8,256,256]{2,1,0:T(8,128)(2,1)}), bf16[8,256,256]{2,1,0:T(8,128)(2,1)S(1)}, u32[]{:S(2)}, u32[]{:S(2)}) async-start(bf16[8,256,256]{2,1,0:T(8,128)(2,1)} %masked_rows.1), calls=%async_computation | async-start | bytes 2097152 | tf_op jit(solution)/shard_map/all_to_all | solution.py:425
  13.4 12.6 %collective-permute-start = (bf16[256,1024]{1,0:T(8,128)(2,1)}, bf16[256,1024]{1,0:T(8,128)(2,1)S(1)}, u32[]{:S(2)}, u32[]{:S(2)}) collective-permute-start(bf16[256,1024]{1,0:T(8,128)(2,1)} %own_ref.2), channel_id=1, source_target_pairs={{1,0},{0,1},{33,2},{32,3},{3,32},{2,33},{35,34},{34,35},{5,4},{4,5... | collective-permute-start | bytes 1572872 | tf_op jit(solution)/shard_map/ppermute | solution.py:440
  18.7 13.0 %collective-permute-start.2 = (bf16[256,1024]{1,0:T(8,128)(2,1)}, bf16[256,1024]{1,0:T(8,128)(2,1)S(1)}, u32[]{:S(2)}, u32[]{:S(2)}) collective-permute-start(bf16[256,1024]{1,0:T(8,128)(2,1)} %own_ref.3), channel_id=1, source_target_pairs={{1,0},{0,1},{33,2},{32,3},{3,32},{2,33},{35,34},{34,35},{5,4},{4,5... | collective-permute-start | bytes 1572872 | tf_op jit(solution)/shard_map/ppermute | solution.py:440
  26.0 7.0 %copy-start.2 = (bf16[256,1024]{1,0:T(8,128)(2,1)}, bf16[256,1024]{1,0:T(8,128)(2,1)S(1)}, u32[]{:S(2)}) copy-start(bf16[256,1024]{1,0:T(8,128)(2,1)S(1)} %collective-permute-done.first_ref) | copy-start | bytes 1572868
  26.0 10.3 %collective-permute-start.1 = (bf16[256,1024]{1,0:T(8,128)(2,1)S(1)}, bf16[256,1024]{1,0:T(8,128)(2,1)}, u32[]{:S(2)}, u32[]{:S(2)}) collective-permute-start(bf16[256,1024]{1,0:T(8,128)(2,1)S(1)} %collective-permute-done.first_ref), channel_id=1, source_target_pairs={{3,2},{2,3},{33,32},{32,33},{7,6},{6,7},{37,36},{36,37},{11,10},{1... | collective-permute-start | bytes 1572872 | tf_op jit(solution)/shard_map/ppermute | solution.py:441
  31.6 13.5 %copy-start = (bf16[256,1024]{1,0:T(8,128)(2,1)}, bf16[256,1024]{1,0:T(8,128)(2,1)S(1)}, u32[]{:S(2)}) copy-start(bf16[256,1024]{1,0:T(8,128)(2,1)S(1)} %collective-permute-done.2.first_ref) | copy-start | bytes 1572868
  31.6 11.1 %collective-permute-start.3 = (bf16[256,1024]{1,0:T(8,128)(2,1)S(1)}, bf16[256,1024]{1,0:T(8,128)(2,1)S(1)}, u32[]{:S(2)}, u32[]{:S(2)}) collective-permute-start(bf16[256,1024]{1,0:T(8,128)(2,1)S(1)} %collective-permute-done.2.first_ref), channel_id=1, source_target_pairs={{1,2},{0,3},{35,32},{34,33},{5,6},{4,7},{39,36},{38,37},{9,10},{8,... | collective-permute-start | bytes 1572872 | tf_op jit(solution)/shard_map/ppermute | solution.py:441
  42.8 2.4 %copy-start.1 = (bf16[256,1024]{1,0:T(8,128)(2,1)}, bf16[256,1024]{1,0:T(8,128)(2,1)S(1)}, u32[]{:S(2)}) copy-start(bf16[256,1024]{1,0:T(8,128)(2,1)S(1)} %collective-permute-done.3.second_ref) | copy-start | bytes 1572868
  42.8 4.7 %collective-permute-start.4 = (bf16[8,256,256]{2,1,0:T(8,128)(2,1)S(1)}, bf16[8,256,256]{2,1,0:T(8,128)(2,1)S(1)}, u32[]{:S(2)}, u32[]{:S(2)}) collective-permute-start(bf16[8,256,256]{2,1,0:T(8,128)(2,1)S(1)} %all-to-all-done.own_ref), channel_id=1, source_target_pairs={{0,32},{32,0},{1,33},{33,1},{2,34},{34,2},{3,35},{35,3},{4,36},{36... | collective-permute-start | bytes 3145736 | tf_op jit(solution)/shard_map/ppermute | solution.py:458
  179.3 8.9 %collective-permute-start.5 = (bf16[128,128]{1,0:T(8,128)(2,1)S(1)}, bf16[128,128]{1,0:T(8,128)(2,1)S(1)}, u32[]{:S(2)}, u32[]{:S(2)}) collective-permute-start(bf16[128,128]{1,0:T(8,128)(2,1)S(1)} %weight_back.1), channel_id=1, source_target_pairs={{2,32},{32,2},{3,33},{33,3},{6,36},{36,6},{7,37},{37,7},{10,40},{4... | collective-permute-start | bytes 98312 | tf_op jit(solution)/shard_map/ppermute | solution.py:474

commit v11 on v10

--- a/solution.py
+++ b/solution.py
@@ -13,7 +13,7 @@
 SHARD = ("z", "xhi", "xlo")
 COLUMN_PEERS = ("y", "xhi", "xlo")
 ROW_PEERS = ("core", "z")
-PIECE_PEERS = ("xlo", "xhi", "y")
+LINE_PEERS = ("xlo", "xhi")
 SHARD_PEERS = ("xhi", "y")
 LANES = 128
 CHUNK = 1024
@@ -372,6 +372,22 @@
     )(recv, norm, cols, turned, codes, expo)
 
 
+def add_kernel(recv_ref, out_ref):
+    for piece in range(out_ref.shape[0]):
+        out_ref[piece] = jnp.sum(recv_ref[:, piece].astype(f32), axis=0).astype(bf16)
+
+
+def add_lines(recv):
+    return pl.pallas_call(
+        add_kernel,
+        in_specs=[IN_VMEM],
+        out_specs=IN_VMEM,
+        out_shape=jax.ShapeDtypeStruct(recv.shape[1:], bf16),
+        compiler_params=params(),
+        name="add_lines",
+    )(recv)
+
+
 def back_kernel(recv_ref, weight_ref, out_ref):
     grad = jnp.sum(recv_ref[...].astype(f32), axis=0)
     weight = weight_ref[...]
@@ -469,7 +485,9 @@
     norm = rows
     cols = exchange(col_pass(rows, codes, column_peers), COLUMN_PEERS)
     rows = exchange(row_pass(cols, codes, row_peers), ROW_PEERS)
-    pieces = exchange(grad_pieces(rows, norm, cols, turned, codes, expo, 2 * shard_pieces), PIECE_PEERS)
+    pieces = grad_pieces(rows, norm, cols, turned, codes, expo, 2 * shard_pieces)
+    pieces = pieces.reshape((size(LINE_PEERS), size("y")) + pieces.shape[1:])
+    pieces = exchange(add_lines(exchange(pieces, LINE_PEERS)), "y")
     mine = weight_back(pieces, weight)
     other = lax.ppermute(mine, ("core", "xhi"), [(1, 2), (2, 1)])
     piece = jnp.where(matched == 1, mine, other)

time: 207 us -> 205 us (level)
    all_to_all x7 -> x8, blocking collectives: 113 us -> 113 us  [exchange(): return lax.all_to_all(values, axes, 0, 0, tiled=True)]
where the time goes in v11:
time: 205 us
  blocking collectives  129 us (63%)
  starting transfers between devices  30.1 us (15%)
  Pallas kernels  26.8 us (13%)
  waiting for transfers between devices  18.4 us (9%)
    all_to_all x8, blocking collectives, exchange(): return lax.all_to_all(values, axes, 0, 0, tiled=True)  113 us
    all_gather x1, blocking collectives, shards(): return join_pieces(lax.all_gather(piece, ('y', 'core'), axis=0))  15.9 us
    all_to_all x1, starting transfers between devices, exchange(): return lax.all_to_all(values, axes, 0, 0, tiled=True)  10.9 us
    ppermute x2, waiting for transfers between devices, shard_permutes(): once = lax.ppermute(weight, axes, first)  9.12 us
    ppermute x2, waiting for transfers between devices, shard_permutes(): return (once, lax.ppermute(once, axes, second))  7.59 us
    ppermute x2, starting transfers between devices, shard_permutes(): once = lax.ppermute(weight, axes, first)  7.14 us
    ppermute x1, starting transfers between devices, shards(): other = lax.ppermute(mine, ('core', 'xhi'), [(1, 2), (2, 1)])  6.51 us
    pallas_call x1, Pallas kernels, grad_pieces(): pl.pallas_call(grad_kernel, in_specs=[IN_VMEM] * 6, out_specs=IN_VMEM, ou...  4.59 us
  transfers between devices with their start and end apart: 7, of which 6 were waited for; matrix products, arithmetic and copies ran while one was open for 0% of the time, Pallas kernels for 2%

profile of v11, /device:TPU:1, one launch (start us, length us, event | category | flops | bytes accessed | tf_op | source)
XLA Modules:
  0.0 204.7 jit_solution(7183506585365884474)
XLA Ops:
  0.0 2.5 %masked_rows.1 = bf16[8,256,256]{2,1,0:T(8,128)(2,1)} custom-call(s32[1,128]{1,0:T(1,128)} %bitcast.9, bf16[256,256]{1,0:T(8,128)(2,1)} %teacher_ref.1, bf16[256,256]{1,0:T(8,128)(2,1)} %student_ref.1), custom_call_target="tpu_custom_call" | custom-call | tf_op jit(solution)/shard_map/masked_rows/pallas_call | solution.py:80
  2.5 10.9 %all-to-all-start = ((bf16[8,256,256]{2,1,0:T(8,128)(2,1)}), bf16[8,256,256]{2,1,0:T(8,128)(2,1)S(1)}, u32[]{:S(2)}, u32[]{:S(2)}) async-start(bf16[8,256,256]{2,1,0:T(8,128)(2,1)} %masked_rows.1), calls=%async_computation | async-start | bytes 2097152 | tf_op jit(solution)/shard_map/all_to_all | solution.py:441
  13.4 5.2 %collective-permute-start = (bf16[256,1024]{1,0:T(8,128)(2,1)}, bf16[256,1024]{1,0:T(8,128)(2,1)S(1)}, u32[]{:S(2)}, u32[]{:S(2)}) collective-permute-start(bf16[256,1024]{1,0:T(8,128)(2,1)} %own_ref.2), channel_id=1, source_target_pairs={{1,0},{0,1},{33,2},{32,3},{3,32},{2,33},{35,34},{34,35},{5,4},{4,5... | collective-permute-start | bytes 1572872 | tf_op jit(solution)/shard_map/ppermute | solution.py:456
  18.7 1.9 collective-permute-start.2
  20.6 5.4 %collective-permute-done.first_ref = bf16[256,1024]{1,0:T(8,128)(2,1)S(1)} collective-permute-done((bf16[256,1024]{1,0:T(8,128)(2,1)}, bf16[256,1024]{1,0:T(8,128)(2,1)S(1)}, u32[]{:S(2)}, u32[]{:S(2)}) %collective-permute-start) | collective-permute-done | bytes 524320 | tf_op jit(solution)/shard_map/ppermute | solution.py:456
  26.0 0.0 copy-start.2
  26.0 1.9 collective-permute-start.1
  27.9 3.7 %collective-permute-done.2.first_ref = bf16[256,1024]{1,0:T(8,128)(2,1)S(1)} collective-permute-done((bf16[256,1024]{1,0:T(8,128)(2,1)}, bf16[256,1024]{1,0:T(8,128)(2,1)S(1)}, u32[]{:S(2)}, u32[]{:S(2)}) %collective-permute-start.2) | collective-permute-done | bytes 524320 | tf_op jit(solution)/shard_map/ppermute | solution.py:456
  31.6 0.0 copy-start
  31.6 1.3 collective-permute-start.3
  32.9 0.1 pad_add_fusion.flags_ref
  33.0 0.0 copy-done.2
  33.0 3.3 %collective-permute-done.1.second_ref = bf16[256,1024]{1,0:T(8,128)(2,1)} collective-permute-done((bf16[256,1024]{1,0:T(8,128)(2,1)S(1)}, bf16[256,1024]{1,0:T(8,128)(2,1)}, u32[]{:S(2)}, u32[]{:S(2)}) %collective-permute-start.1) | collective-permute-done | bytes 524320 | tf_op jit(solution)/shard_map/ppermute | solution.py:457
  36.3 2.1 %prototypes.2.protos_ref = bf16[256,2048]{1,0:T(8,128)(2,1)S(1)} custom-call(s32[4]{0:T(128)S(1)} %pad_add_fusion.flags_ref, bf16[256,1024]{1,0:T(8,128)(2,1)} %own_ref.2, bf16[256,1024]{1,0:T(8,128)(2,1)} %copy-done.2, bf16[256,1024]{1,0:T(8,128)(2,1)} %collective-permute-done.1.second_ref), custom_call_target="tpu_custom_call" | custom-call | flops 1048576 | bytes 2097152 | tf_op jit(solution)/shard_map/prototypes/pallas_call | solution.py:141
  38.5 4.3 %collective-permute-done.3.second_ref = bf16[256,1024]{1,0:T(8,128)(2,1)S(1)} collective-permute-done((bf16[256,1024]{1,0:T(8,128)(2,1)S(1)}, bf16[256,1024]{1,0:T(8,128)(2,1)S(1)}, u32[]{:S(2)}, u32[]{:S(2)}) %collective-permute-start.3) | collective-permute-done | bytes 524320 | tf_op jit(solution)/shard_map/ppermute | solution.py:457
  42.8 0.0 copy-start.1
  42.8 0.0 all-to-all-done.own_ref
  42.8 2.4 %collective-permute-start.4 = (bf16[8,256,256]{2,1,0:T(8,128)(2,1)S(1)}, bf16[8,256,256]{2,1,0:T(8,128)(2,1)S(1)}, u32[]{:S(2)}, u32[]{:S(2)}) collective-permute-start(bf16[8,256,256]{2,1,0:T(8,128)(2,1)S(1)} %all-to-all-done.own_ref), channel_id=1, source_target_pairs={{0,32},{32,0},{1,33},{33,1},{2,34},{34,2},{3,35},{35,3},{4,36},{36... | collective-permute-start | bytes 3145736 | tf_op jit(solution)/shard_map/ppermute | solution.py:474
  45.2 0.0 copy-done
  45.2 0.0 copy-done.1
  45.2 2.2 %prototypes.3 = (bf16[256,2048]{1,0:T(8,128)(2,1)S(1)}, f32[128,128]{1,0:T(8,128)S(1)}) custom-call(s32[4]{0:T(128)S(1)} %pad_add_fusion.flags_ref, bf16[256,1024]{1,0:T(8,128)(2,1)} %own_ref.3, bf16[256,1024]{1,0:T(8,128)(2,1)} %copy-done, bf16[256,1024]{1,0:T(8,128)(2,1)} %copy-done.1), custom_call_target="tpu_custom_call" | custom-call | flops 1048576 | bytes 2097152 | tf_op jit(solution)/shard_map/prototypes/pallas_call | solution.py:141
  47.4 0.1 collective-permute-done.4.other_ref
  47.4 2.9 %first_codes.1 = (bf16[2048,2048]{1,0:T(8,128)(2,1)S(1)}, bf16[32,16,128]{2,1,0:T(8,128)(2,1)S(1)}) custom-call(s32[4]{0:T(128)S(1)} %pad_add_fusion.flags_ref, bf16[8,256,256]{2,1,0:T(8,128)(2,1)S(1)} %all-to-all-done.own_ref, bf16[8,256,256]{2,1,0:T(8,128)(2,1)S(1)} %collective-permute-done.4.other_ref, bf16[256,2048]{1,0:T(8,128)(2,1)S(1)} %prototypes.2.protos_ref), custom_call_target="tpu_custom_call" | custom-call | flops 2147483648 | bytes 8388608 | tf_op jit(solution)/shard_map/first_codes/pallas_call | solution.py:189
  50.4 3.3 %student_expo.1 = (bf16[2048,2048]{1,0:T(8,128)(2,1)S(1)}, f32[16,128]{1,0:T(8,128)S(1)}, bf16[256,2048]{1,0:T(8,128)(2,1)S(1)}) custom-call(s32[4]{0:T(128)S(1)} %pad_add_fusion.flags_ref, bf16[8,256,256]{2,1,0:T(8,128)(2,1)S(1)} %all-to-all-done.own_ref, bf16[8,256,256]{2,1,0:T(8,128)(2,1)S(1)} %collective-permute-done.4.other_ref, ...), custom_call_target="tpu_custom_call" | custom-call | flops 2147483648 | bytes 8388608 | tf_op jit(solution)/shard_map/student_expo/pallas_call | solution.py:326
  53.6 19.5 %all_to_all.45.refs_0_ = bf16[32,16,128]{2,1,0:T(8,128)(2,1)S(1)} all-to-all(bf16[32,16,128]{2,1,0:T(8,128)(2,1)S(1)} %get-tuple-element.37), channel_id=1, replica_groups=mesh['y'=8,'core'=2,'z'=8,'xhi'=2,'xlo'=2] {'y','xhi','xlo'}, dimensions={0} | all-to-all | bytes 262144 | tf_op jit(solution)/shard_map/all_to_all | solution.py:441
  73.1 1.5 row_pass.3
  74.6 16.5 %all_to_all.46.recv_ref.refs_2_ = bf16[16,24,128]{2,1,0:T(8,128)(2,1)S(1)} all-to-all(bf16[16,24,128]{2,1,0:T(8,128)(2,1)S(1)} %row_pass.3), channel_id=1, replica_groups=mesh['y'=8,'core'=2,'z'=8,'xhi'=2,'xlo'=2] {'core','z'}, dimensions={0} | all-to-all | bytes 196608 | tf_op jit(solution)/shard_map/all_to_all | solution.py:441
  91.0 1.7 col_pass.2
  92.8 12.5 %all_to_all.47.refs_0_ = bf16[32,16,128]{2,1,0:T(8,128)(2,1)S(1)} all-to-all(bf16[32,16,128]{2,1,0:T(8,128)(2,1)S(1)} %col_pass.2), channel_id=1, replica_groups=mesh['y'=8,'core'=2,'z'=8,'xhi'=2,'xlo'=2] {'y','xhi','xlo'}, dimensions={0} | all-to-all | bytes 262144 | tf_op jit(solution)/shard_map/all_to_all | solution.py:441
  105.3 1.5 row_pass.4
  106.7 12.2 %all_to_all.48.recv_ref.norm_ref = bf16[16,24,128]{2,1,0:T(8,128)(2,1)S(1)} all-to-all(bf16[16,24,128]{2,1,0:T(8,128)(2,1)S(1)} %row_pass.4), channel_id=1, replica_groups=mesh['y'=8,'core'=2,'z'=8,'xhi'=2,'xlo'=2] {'core','z'}, dimensions={0} | all-to-all | bytes 196608 | tf_op jit(solution)/shard_map/all_to_all | solution.py:441
  118.9 1.8 col_pass.3
  120.7 12.5 %all_to_all.49.refs_0_.cols_ref = bf16[32,16,128]{2,1,0:T(8,128)(2,1)S(1)} all-to-all(bf16[32,16,128]{2,1,0:T(8,128)(2,1)S(1)} %col_pass.3), channel_id=1, replica_groups=mesh['y'=8,'core'=2,'z'=8,'xhi'=2,'xlo'=2] {'y','xhi','xlo'}, dimensions={0} | all-to-all | bytes 262144 | tf_op jit(solution)/shard_map/all_to_all | solution.py:441
  133.2 1.4 row_pass.5
  134.6 12.1 %all_to_all.50.recv_ref = bf16[16,16,128]{2,1,0:T(8,128)(2,1)S(1)} all-to-all(bf16[16,16,128]{2,1,0:T(8,128)(2,1)S(1)} %row_pass.5), channel_id=1, replica_groups=mesh['y'=8,'core'=2,'z'=8,'xhi'=2,'xlo'=2] {'core','z'}, dimensions={0} | all-to-all | bytes 131072 | tf_op jit(solution)/shard_map/all_to_all | solution.py:441
  146.7 4.6 %grad_pieces.1 = bf16[32,128,128]{2,1,0:T(8,128)(2,1)S(1)} custom-call(bf16[16,16,128]{2,1,0:T(8,128)(2,1)S(1)} %all_to_all.50.recv_ref, bf16[16,24,128]{2,1,0:T(8,128)(2,1)S(1)} %all_to_all.48.recv_ref.norm_ref, bf16[32,16,128]{2,1,0:T(8,128)(2,1)S(1)} %all_to_all.49.refs_0_.cols_ref, bf16[256,2048]{1,0:T(8,128)(2,1)S(1)} %get-tuple-element.40.turned_ref, ...), custom_call_target="tpu_custom_call" | custom-call | flops 4294967296 | bytes 16777216 | tf_op jit(solution)/shard_map/grad_pieces/pallas_call | solution.py:364
  151.3 16.3 %all_to_all.51.recv_ref = bf16[4,8,128,128]{3,2,1,0:T(8,128)(2,1)S(1)} all-to-all(bf16[4,8,128,128]{3,2,1,0:T(8,128)(2,1)S(1)} %bitcast.7), channel_id=1, replica_groups=mesh['y'=8,'core'=2,'z'=8,'xhi'=2,'xlo'=2] {'xlo','xhi'}, dimensions={0} | all-to-all | bytes 2097152 | tf_op jit(solution)/shard_map/all_to_all | solution.py:441
  167.7 0.1 add_lines.1
  167.8 11.7 %all_to_all.52.recv_ref = bf16[8,128,128]{2,1,0:T(8,128)(2,1)S(1)} all-to-all(bf16[8,128,128]{2,1,0:T(8,128)(2,1)S(1)} %add_lines.1), channel_id=1, replica_groups=mesh['y'=8,'core'=2,'z'=8,'xhi'=2,'xlo'=2] {'y'}, dimensions={0} | all-to-all | bytes 524288 | tf_op jit(solution)/shard_map/all_to_all | solution.py:441
  179.5 0.1 weight_back.1
  179.6 6.5 %collective-permute-start.5 = (bf16[128,128]{1,0:T(8,128)(2,1)S(1)}, bf16[128,128]{1,0:T(8,128)(2,1)S(1)}, u32[]{:S(2)}, u32[]{:S(2)}) collective-permute-start(bf16[128,128]{1,0:T(8,128)(2,1)S(1)} %weight_back.1), channel_id=1, source_target_pairs={{2,32},{32,2},{3,33},{33,3},{6,36},{36,6},{7,37},{37,7},{10,40},{4... | collective-permute-start | bytes 98312 | tf_op jit(solution)/shard_map/ppermute | solution.py:492
  186.2 1.6 collective-permute-done.5
  187.8 15.9 %all-gather = bf16[2048,128]{1,0:T(8,128)(2,1)S(1)} all-gather(bf16[128,128]{1,0:T(8,128)(2,1)S(1)} %broadcast_select_fusion), channel_id=2, replica_groups=mesh['y'=8,'core'=2,'z'=8,'xhi'=2,'xlo'=2] {'y','core'}, dimensions={0}, use_global_device_ids=true | all-gather | bytes 557056 | tf_op jit(solution)/shard_map/all_gather | solution.py:494
  203.7 1.0 join_pieces.1
  (1 shorter events, 0.0 us)
Async XLA Ops:
  2.5 40.2 %all-to-all-start = ((bf16[8,256,256]{2,1,0:T(8,128)(2,1)}), bf16[8,256,256]{2,1,0:T(8,128)(2,1)S(1)}, u32[]{:S(2)}, u32[]{:S(2)}) async-start(bf16[8,256,256]{2,1,0:T(8,128)(2,1)} %masked_rows.1), calls=%async_computation | async-start | bytes 2097152 | tf_op jit(solution)/shard_map/all_to_all | solution.py:441
  13.4 12.6 %collective-permute-start = (bf16[256,1024]{1,0:T(8,128)(2,1)}, bf16[256,1024]{1,0:T(8,128)(2,1)S(1)}, u32[]{:S(2)}, u32[]{:S(2)}) collective-permute-start(bf16[256,1024]{1,0:T(8,128)(2,1)} %own_ref.2), channel_id=1, source_target_pairs={{1,0},{0,1},{33,2},{32,3},{3,32},{2,33},{35,34},{34,35},{5,4},{4,5... | collective-permute-start | bytes 1572872 | tf_op jit(solution)/shard_map/ppermute | solution.py:456
  18.7 13.0 %collective-permute-start.2 = (bf16[256,1024]{1,0:T(8,128)(2,1)}, bf16[256,1024]{1,0:T(8,128)(2,1)S(1)}, u32[]{:S(2)}, u32[]{:S(2)}) collective-permute-start(bf16[256,1024]{1,0:T(8,128)(2,1)} %own_ref.3), channel_id=1, source_target_pairs={{1,0},{0,1},{33,2},{32,3},{3,32},{2,33},{35,34},{34,35},{5,4},{4,5... | collective-permute-start | bytes 1572872 | tf_op jit(solution)/shard_map/ppermute | solution.py:456
  26.0 7.0 %copy-start.2 = (bf16[256,1024]{1,0:T(8,128)(2,1)}, bf16[256,1024]{1,0:T(8,128)(2,1)S(1)}, u32[]{:S(2)}) copy-start(bf16[256,1024]{1,0:T(8,128)(2,1)S(1)} %collective-permute-done.first_ref) | copy-start | bytes 1572868
  26.0 10.3 %collective-permute-start.1 = (bf16[256,1024]{1,0:T(8,128)(2,1)S(1)}, bf16[256,1024]{1,0:T(8,128)(2,1)}, u32[]{:S(2)}, u32[]{:S(2)}) collective-permute-start(bf16[256,1024]{1,0:T(8,128)(2,1)S(1)} %collective-permute-done.first_ref), channel_id=1, source_target_pairs={{3,2},{2,3},{33,32},{32,33},{7,6},{6,7},{37,36},{36,37},{11,10},{1... | collective-permute-start | bytes 1572872 | tf_op jit(solution)/shard_map/ppermute | solution.py:457
  31.6 13.5 %copy-start = (bf16[256,1024]{1,0:T(8,128)(2,1)}, bf16[256,1024]{1,0:T(8,128)(2,1)S(1)}, u32[]{:S(2)}) copy-start(bf16[256,1024]{1,0:T(8,128)(2,1)S(1)} %collective-permute-done.2.first_ref) | copy-start | bytes 1572868
  31.6 11.1 %collective-permute-start.3 = (bf16[256,1024]{1,0:T(8,128)(2,1)S(1)}, bf16[256,1024]{1,0:T(8,128)(2,1)S(1)}, u32[]{:S(2)}, u32[]{:S(2)}) collective-permute-start(bf16[256,1024]{1,0:T(8,128)(2,1)S(1)} %collective-permute-done.2.first_ref), channel_id=1, source_target_pairs={{1,2},{0,3},{35,32},{34,33},{5,6},{4,7},{39,36},{38,37},{9,10},{8,... | collective-permute-start | bytes 1572872 | tf_op jit(solution)/shard_map/ppermute | solution.py:457
  42.8 2.4 %copy-start.1 = (bf16[256,1024]{1,0:T(8,128)(2,1)}, bf16[256,1024]{1,0:T(8,128)(2,1)S(1)}, u32[]{:S(2)}) copy-start(bf16[256,1024]{1,0:T(8,128)(2,1)S(1)} %collective-permute-done.3.second_ref) | copy-start | bytes 1572868
  42.8 4.7 %collective-permute-start.4 = (bf16[8,256,256]{2,1,0:T(8,128)(2,1)S(1)}, bf16[8,256,256]{2,1,0:T(8,128)(2,1)S(1)}, u32[]{:S(2)}, u32[]{:S(2)}) collective-permute-start(bf16[8,256,256]{2,1,0:T(8,128)(2,1)S(1)} %all-to-all-done.own_ref), channel_id=1, source_target_pairs={{0,32},{32,0},{1,33},{33,1},{2,34},{34,2},{3,35},{35,3},{4,36},{36... | collective-permute-start | bytes 3145736 | tf_op jit(solution)/shard_map/ppermute | solution.py:474
  179.6 8.1 %collective-permute-start.5 = (bf16[128,128]{1,0:T(8,128)(2,1)S(1)}, bf16[128,128]{1,0:T(8,128)(2,1)S(1)}, u32[]{:S(2)}, u32[]{:S(2)}) collective-permute-start(bf16[128,128]{1,0:T(8,128)(2,1)S(1)} %weight_back.1), channel_id=1, source_target_pairs={{2,32},{32,2},{3,33},{33,3},{6,36},{36,6},{7,37},{37,7},{10,40},{4... | collective-permute-start | bytes 98312 | tf_op jit(solution)/shard_map/ppermute | solution.py:492

commit v12 on v11

--- a/solution.py
+++ b/solution.py
@@ -63,14 +63,17 @@
     count = mask_ref.shape[1]
     chosen = lax.broadcasted_iota(jnp.int32, (patches, count), 0) == index_ref[...]
     chosen = chosen.astype(f32).astype(bf16)
+    sends = []
     for part in range(2):
         copies[1 + part].wait()
         rows = lax.dot_general(chosen, held_ref[part], TN, preferred_element_type=f32)
         square = jnp.sum(rows * rows, axis=1, keepdims=True)
-        made_ref[part * count : (part + 1) * count, :] = (rows * lax.rsqrt(square + epsilon)).astype(bf16)
-    sends = [pltpu.make_async_copy(made_ref, out_ref.at[i], sems.at[3 + i]) for i in range(out_ref.shape[0])]
-    for send in sends:
-        send.start()
+        span = pl.ds(part * count, count)
+        made_ref[span, :] = (rows * lax.rsqrt(square + epsilon)).astype(bf16)
+        for i in range(out_ref.shape[0]):
+            sem = sems.at[3 + part * out_ref.shape[0] + i]
+            sends.append(pltpu.make_async_copy(made_ref.at[span, :], out_ref.at[i, span, :], sem))
+            sends[-1].start()
     for send in sends:
         send.wait()
 
@@ -86,7 +89,7 @@
             pltpu.VMEM(mask.shape, jnp.int32),
             pltpu.VMEM((2,) + teacher.shape, bf16),
             pltpu.VMEM((2 * count, width), bf16),
-            pltpu.SemaphoreType.DMA((3 + copies,)),
+            pltpu.SemaphoreType.DMA((3 + 2 * copies,)),
         ],
         compiler_params=params(),
         name="masked_rows",

time: 205 us -> 205 us (level)
  no operation moved by 1% of the time
where the time goes in v12:
time: 205 us
  blocking collectives  129 us (63%)
  starting transfers between devices  30.1 us (15%)
  Pallas kernels  26.7 us (13%)
  waiting for transfers between devices  18.4 us (9%)
    all_to_all x8, blocking collectives, exchange(): return lax.all_to_all(values, axes, 0, 0, tiled=True)  113 us
    all_gather x1, blocking collectives, shards(): return join_pieces(lax.all_gather(piece, ('y', 'core'), axis=0))  15.9 us
    all_to_all x1, starting transfers between devices, exchange(): return lax.all_to_all(values, axes, 0, 0, tiled=True)  10.9 us
    ppermute x2, waiting for transfers between devices, shard_permutes(): once = lax.ppermute(weight, axes, first)  9.12 us
    ppermute x2, waiting for transfers between devices, shard_permutes(): return (once, lax.ppermute(once, axes, second))  7.59 us
    ppermute x2, starting transfers between devices, shard_permutes(): once = lax.ppermute(weight, axes, first)  7.14 us
    ppermute x1, starting transfers between devices, shards(): other = lax.ppermute(mine, ('core', 'xhi'), [(1, 2), (2, 1)])  6.51 us
    pallas_call x1, Pallas kernels, grad_pieces(): pl.pallas_call(grad_kernel, in_specs=[IN_VMEM] * 6, out_specs=IN_VMEM, ou...  4.59 us
  transfers between devices with their start and end apart: 7, of which 6 were waited for; matrix products, arithmetic and copies ran while one was open for 0% of the time, Pallas kernels for 2%

profile of v12, /device:TPU:1, one launch (start us, length us, event | category | flops | bytes accessed | tf_op | source)
XLA Modules:
  0.0 204.6 jit_solution(17633007373001297551)
XLA Ops:
  0.0 2.5 %masked_rows.1 = bf16[8,256,256]{2,1,0:T(8,128)(2,1)} custom-call(s32[1,128]{1,0:T(1,128)} %bitcast.9, bf16[256,256]{1,0:T(8,128)(2,1)} %teacher_ref.1, bf16[256,256]{1,0:T(8,128)(2,1)} %student_ref.1), custom_call_target="tpu_custom_call" | custom-call | tf_op jit(solution)/shard_map/masked_rows/pallas_call | solution.py:83
  2.5 10.9 %all-to-all-start = ((bf16[8,256,256]{2,1,0:T(8,128)(2,1)}), bf16[8,256,256]{2,1,0:T(8,128)(2,1)S(1)}, u32[]{:S(2)}, u32[]{:S(2)}) async-start(bf16[8,256,256]{2,1,0:T(8,128)(2,1)} %masked_rows.1), calls=%async_computation | async-start | bytes 2097152 | tf_op jit(solution)/shard_map/all_to_all | solution.py:444
  13.3 5.2 %collective-permute-start = (bf16[256,1024]{1,0:T(8,128)(2,1)}, bf16[256,1024]{1,0:T(8,128)(2,1)S(1)}, u32[]{:S(2)}, u32[]{:S(2)}) collective-permute-start(bf16[256,1024]{1,0:T(8,128)(2,1)} %own_ref.2), channel_id=1, source_target_pairs={{1,0},{0,1},{33,2},{32,3},{3,32},{2,33},{35,34},{34,35},{5,4},{4,5... | collective-permute-start | bytes 1572872 | tf_op jit(solution)/shard_map/ppermute | solution.py:459
  18.6 1.9 collective-permute-start.2
  20.5 5.4 %collective-permute-done.first_ref = bf16[256,1024]{1,0:T(8,128)(2,1)S(1)} collective-permute-done((bf16[256,1024]{1,0:T(8,128)(2,1)}, bf16[256,1024]{1,0:T(8,128)(2,1)S(1)}, u32[]{:S(2)}, u32[]{:S(2)}) %collective-permute-start) | collective-permute-done | bytes 524320 | tf_op jit(solution)/shard_map/ppermute | solution.py:459
  25.9 0.0 copy-start.2
  25.9 1.9 collective-permute-start.1
  27.8 3.7 %collective-permute-done.2.first_ref = bf16[256,1024]{1,0:T(8,128)(2,1)S(1)} collective-permute-done((bf16[256,1024]{1,0:T(8,128)(2,1)}, bf16[256,1024]{1,0:T(8,128)(2,1)S(1)}, u32[]{:S(2)}, u32[]{:S(2)}) %collective-permute-start.2) | collective-permute-done | bytes 524320 | tf_op jit(solution)/shard_map/ppermute | solution.py:459
  31.5 0.0 copy-start
  31.5 1.3 collective-permute-start.3
  32.8 0.1 pad_add_fusion.flags_ref
  32.9 0.0 copy-done.2
  32.9 3.3 %collective-permute-done.1.second_ref = bf16[256,1024]{1,0:T(8,128)(2,1)} collective-permute-done((bf16[256,1024]{1,0:T(8,128)(2,1)S(1)}, bf16[256,1024]{1,0:T(8,128)(2,1)}, u32[]{:S(2)}, u32[]{:S(2)}) %collective-permute-start.1) | collective-permute-done | bytes 524320 | tf_op jit(solution)/shard_map/ppermute | solution.py:460
  36.2 2.1 %prototypes.2.protos_ref = bf16[256,2048]{1,0:T(8,128)(2,1)S(1)} custom-call(s32[4]{0:T(128)S(1)} %pad_add_fusion.flags_ref, bf16[256,1024]{1,0:T(8,128)(2,1)} %own_ref.2, bf16[256,1024]{1,0:T(8,128)(2,1)} %copy-done.2, bf16[256,1024]{1,0:T(8,128)(2,1)} %collective-permute-done.1.second_ref), custom_call_target="tpu_custom_call" | custom-call | flops 1048576 | bytes 2097152 | tf_op jit(solution)/shard_map/prototypes/pallas_call | solution.py:144
  38.4 4.3 %collective-permute-done.3.second_ref = bf16[256,1024]{1,0:T(8,128)(2,1)S(1)} collective-permute-done((bf16[256,1024]{1,0:T(8,128)(2,1)S(1)}, bf16[256,1024]{1,0:T(8,128)(2,1)S(1)}, u32[]{:S(2)}, u32[]{:S(2)}) %collective-permute-start.3) | collective-permute-done | bytes 524320 | tf_op jit(solution)/shard_map/ppermute | solution.py:460
  42.7 0.0 copy-start.1
  42.7 0.0 all-to-all-done.own_ref
  42.7 2.4 %collective-permute-start.4 = (bf16[8,256,256]{2,1,0:T(8,128)(2,1)S(1)}, bf16[8,256,256]{2,1,0:T(8,128)(2,1)S(1)}, u32[]{:S(2)}, u32[]{:S(2)}) collective-permute-start(bf16[8,256,256]{2,1,0:T(8,128)(2,1)S(1)} %all-to-all-done.own_ref), channel_id=1, source_target_pairs={{0,32},{32,0},{1,33},{33,1},{2,34},{34,2},{3,35},{35,3},{4,36},{36... | collective-permute-start | bytes 3145736 | tf_op jit(solution)/shard_map/ppermute | solution.py:477
  45.1 0.0 copy-done
  45.1 0.0 copy-done.1
  45.1 2.2 %prototypes.3 = (bf16[256,2048]{1,0:T(8,128)(2,1)S(1)}, f32[128,128]{1,0:T(8,128)S(1)}) custom-call(s32[4]{0:T(128)S(1)} %pad_add_fusion.flags_ref, bf16[256,1024]{1,0:T(8,128)(2,1)} %own_ref.3, bf16[256,1024]{1,0:T(8,128)(2,1)} %copy-done, bf16[256,1024]{1,0:T(8,128)(2,1)} %copy-done.1), custom_call_target="tpu_custom_call" | custom-call | flops 1048576 | bytes 2097152 | tf_op jit(solution)/shard_map/prototypes/pallas_call | solution.py:144
  47.3 0.1 collective-permute-done.4.other_ref
  47.4 2.9 %first_codes.1 = (bf16[2048,2048]{1,0:T(8,128)(2,1)S(1)}, bf16[32,16,128]{2,1,0:T(8,128)(2,1)S(1)}) custom-call(s32[4]{0:T(128)S(1)} %pad_add_fusion.flags_ref, bf16[8,256,256]{2,1,0:T(8,128)(2,1)S(1)} %all-to-all-done.own_ref, bf16[8,256,256]{2,1,0:T(8,128)(2,1)S(1)} %collective-permute-done.4.other_ref, bf16[256,2048]{1,0:T(8,128)(2,1)S(1)} %prototypes.2.protos_ref), custom_call_target="tpu_custom_call" | custom-call | flops 2147483648 | bytes 8388608 | tf_op jit(solution)/shard_map/first_codes/pallas_call | solution.py:192
  50.3 3.3 %student_expo.1 = (bf16[2048,2048]{1,0:T(8,128)(2,1)S(1)}, f32[16,128]{1,0:T(8,128)S(1)}, bf16[256,2048]{1,0:T(8,128)(2,1)S(1)}) custom-call(s32[4]{0:T(128)S(1)} %pad_add_fusion.flags_ref, bf16[8,256,256]{2,1,0:T(8,128)(2,1)S(1)} %all-to-all-done.own_ref, bf16[8,256,256]{2,1,0:T(8,128)(2,1)S(1)} %collective-permute-done.4.other_ref, ...), custom_call_target="tpu_custom_call" | custom-call | flops 2147483648 | bytes 8388608 | tf_op jit(solution)/shard_map/student_expo/pallas_call | solution.py:329
  53.6 19.5 %all_to_all.45.refs_0_ = bf16[32,16,128]{2,1,0:T(8,128)(2,1)S(1)} all-to-all(bf16[32,16,128]{2,1,0:T(8,128)(2,1)S(1)} %get-tuple-element.37), channel_id=1, replica_groups=mesh['y'=8,'core'=2,'z'=8,'xhi'=2,'xlo'=2] {'y','xhi','xlo'}, dimensions={0} | all-to-all | bytes 262144 | tf_op jit(solution)/shard_map/all_to_all | solution.py:444
  73.0 1.5 row_pass.3
  74.5 16.5 %all_to_all.46.recv_ref.refs_2_ = bf16[16,24,128]{2,1,0:T(8,128)(2,1)S(1)} all-to-all(bf16[16,24,128]{2,1,0:T(8,128)(2,1)S(1)} %row_pass.3), channel_id=1, replica_groups=mesh['y'=8,'core'=2,'z'=8,'xhi'=2,'xlo'=2] {'core','z'}, dimensions={0} | all-to-all | bytes 196608 | tf_op jit(solution)/shard_map/all_to_all | solution.py:444
  91.0 1.8 col_pass.2
  92.7 12.4 %all_to_all.47.refs_0_ = bf16[32,16,128]{2,1,0:T(8,128)(2,1)S(1)} all-to-all(bf16[32,16,128]{2,1,0:T(8,128)(2,1)S(1)} %col_pass.2), channel_id=1, replica_groups=mesh['y'=8,'core'=2,'z'=8,'xhi'=2,'xlo'=2] {'y','xhi','xlo'}, dimensions={0} | all-to-all | bytes 262144 | tf_op jit(solution)/shard_map/all_to_all | solution.py:444
  105.1 1.5 row_pass.4
  106.5 12.3 %all_to_all.48.recv_ref.norm_ref = bf16[16,24,128]{2,1,0:T(8,128)(2,1)S(1)} all-to-all(bf16[16,24,128]{2,1,0:T(8,128)(2,1)S(1)} %row_pass.4), channel_id=1, replica_groups=mesh['y'=8,'core'=2,'z'=8,'xhi'=2,'xlo'=2] {'core','z'}, dimensions={0} | all-to-all | bytes 196608 | tf_op jit(solution)/shard_map/all_to_all | solution.py:444
  118.9 1.7 col_pass.3
  120.6 12.5 %all_to_all.49.refs_0_.cols_ref = bf16[32,16,128]{2,1,0:T(8,128)(2,1)S(1)} all-to-all(bf16[32,16,128]{2,1,0:T(8,128)(2,1)S(1)} %col_pass.3), channel_id=1, replica_groups=mesh['y'=8,'core'=2,'z'=8,'xhi'=2,'xlo'=2] {'y','xhi','xlo'}, dimensions={0} | all-to-all | bytes 262144 | tf_op jit(solution)/shard_map/all_to_all | solution.py:444
  133.1 1.4 row_pass.5
  134.6 12.1 %all_to_all.50.recv_ref = bf16[16,16,128]{2,1,0:T(8,128)(2,1)S(1)} all-to-all(bf16[16,16,128]{2,1,0:T(8,128)(2,1)S(1)} %row_pass.5), channel_id=1, replica_groups=mesh['y'=8,'core'=2,'z'=8,'xhi'=2,'xlo'=2] {'core','z'}, dimensions={0} | all-to-all | bytes 131072 | tf_op jit(solution)/shard_map/all_to_all | solution.py:444
  146.6 4.6 %grad_pieces.1 = bf16[32,128,128]{2,1,0:T(8,128)(2,1)S(1)} custom-call(bf16[16,16,128]{2,1,0:T(8,128)(2,1)S(1)} %all_to_all.50.recv_ref, bf16[16,24,128]{2,1,0:T(8,128)(2,1)S(1)} %all_to_all.48.recv_ref.norm_ref, bf16[32,16,128]{2,1,0:T(8,128)(2,1)S(1)} %all_to_all.49.refs_0_.cols_ref, bf16[256,2048]{1,0:T(8,128)(2,1)S(1)} %get-tuple-element.40.turned_ref, ...), custom_call_target="tpu_custom_call" | custom-call | flops 4294967296 | bytes 16777216 | tf_op jit(solution)/shard_map/grad_pieces/pallas_call | solution.py:367
  151.2 16.3 %all_to_all.51.recv_ref = bf16[4,8,128,128]{3,2,1,0:T(8,128)(2,1)S(1)} all-to-all(bf16[4,8,128,128]{3,2,1,0:T(8,128)(2,1)S(1)} %bitcast.7), channel_id=1, replica_groups=mesh['y'=8,'core'=2,'z'=8,'xhi'=2,'xlo'=2] {'xlo','xhi'}, dimensions={0} | all-to-all | bytes 2097152 | tf_op jit(solution)/shard_map/all_to_all | solution.py:444
  167.6 0.1 add_lines.1
  167.7 11.7 %all_to_all.52.recv_ref = bf16[8,128,128]{2,1,0:T(8,128)(2,1)S(1)} all-to-all(bf16[8,128,128]{2,1,0:T(8,128)(2,1)S(1)} %add_lines.1), channel_id=1, replica_groups=mesh['y'=8,'core'=2,'z'=8,'xhi'=2,'xlo'=2] {'y'}, dimensions={0} | all-to-all | bytes 524288 | tf_op jit(solution)/shard_map/all_to_all | solution.py:444
  179.4 0.1 weight_back.1
  179.6 6.5 %collective-permute-start.5 = (bf16[128,128]{1,0:T(8,128)(2,1)S(1)}, bf16[128,128]{1,0:T(8,128)(2,1)S(1)}, u32[]{:S(2)}, u32[]{:S(2)}) collective-permute-start(bf16[128,128]{1,0:T(8,128)(2,1)S(1)} %weight_back.1), channel_id=1, source_target_pairs={{2,32},{32,2},{3,33},{33,3},{6,36},{36,6},{7,37},{37,7},{10,40},{4... | collective-permute-start | bytes 98312 | tf_op jit(solution)/shard_map/ppermute | solution.py:495
  186.1 1.6 collective-permute-done.5
  187.7 15.9 %all-gather = bf16[2048,128]{1,0:T(8,128)(2,1)S(1)} all-gather(bf16[128,128]{1,0:T(8,128)(2,1)S(1)} %broadcast_select_fusion), channel_id=2, replica_groups=mesh['y'=8,'core'=2,'z'=8,'xhi'=2,'xlo'=2] {'y','core'}, dimensions={0}, use_global_device_ids=true | all-gather | bytes 557056 | tf_op jit(solution)/shard_map/all_gather | solution.py:497
  203.6 1.0 join_pieces.1
  (1 shorter events, 0.0 us)
Async XLA Ops:
  2.5 40.2 %all-to-all-start = ((bf16[8,256,256]{2,1,0:T(8,128)(2,1)}), bf16[8,256,256]{2,1,0:T(8,128)(2,1)S(1)}, u32[]{:S(2)}, u32[]{:S(2)}) async-start(bf16[8,256,256]{2,1,0:T(8,128)(2,1)} %masked_rows.1), calls=%async_computation | async-start | bytes 2097152 | tf_op jit(solution)/shard_map/all_to_all | solution.py:444
  13.3 12.6 %collective-permute-start = (bf16[256,1024]{1,0:T(8,128)(2,1)}, bf16[256,1024]{1,0:T(8,128)(2,1)S(1)}, u32[]{:S(2)}, u32[]{:S(2)}) collective-permute-start(bf16[256,1024]{1,0:T(8,128)(2,1)} %own_ref.2), channel_id=1, source_target_pairs={{1,0},{0,1},{33,2},{32,3},{3,32},{2,33},{35,34},{34,35},{5,4},{4,5... | collective-permute-start | bytes 1572872 | tf_op jit(solution)/shard_map/ppermute | solution.py:459
  18.6 13.0 %collective-permute-start.2 = (bf16[256,1024]{1,0:T(8,128)(2,1)}, bf16[256,1024]{1,0:T(8,128)(2,1)S(1)}, u32[]{:S(2)}, u32[]{:S(2)}) collective-permute-start(bf16[256,1024]{1,0:T(8,128)(2,1)} %own_ref.3), channel_id=1, source_target_pairs={{1,0},{0,1},{33,2},{32,3},{3,32},{2,33},{35,34},{34,35},{5,4},{4,5... | collective-permute-start | bytes 1572872 | tf_op jit(solution)/shard_map/ppermute | solution.py:459
  25.9 7.0 %copy-start.2 = (bf16[256,1024]{1,0:T(8,128)(2,1)}, bf16[256,1024]{1,0:T(8,128)(2,1)S(1)}, u32[]{:S(2)}) copy-start(bf16[256,1024]{1,0:T(8,128)(2,1)S(1)} %collective-permute-done.first_ref) | copy-start | bytes 1572868
  25.9 10.3 %collective-permute-start.1 = (bf16[256,1024]{1,0:T(8,128)(2,1)S(1)}, bf16[256,1024]{1,0:T(8,128)(2,1)}, u32[]{:S(2)}, u32[]{:S(2)}) collective-permute-start(bf16[256,1024]{1,0:T(8,128)(2,1)S(1)} %collective-permute-done.first_ref), channel_id=1, source_target_pairs={{3,2},{2,3},{33,32},{32,33},{7,6},{6,7},{37,36},{36,37},{11,10},{1... | collective-permute-start | bytes 1572872 | tf_op jit(solution)/shard_map/ppermute | solution.py:460
  31.5 13.5 %copy-start = (bf16[256,1024]{1,0:T(8,128)(2,1)}, bf16[256,1024]{1,0:T(8,128)(2,1)S(1)}, u32[]{:S(2)}) copy-start(bf16[256,1024]{1,0:T(8,128)(2,1)S(1)} %collective-permute-done.2.first_ref) | copy-start | bytes 1572868
  31.5 11.1 %collective-permute-start.3 = (bf16[256,1024]{1,0:T(8,128)(2,1)S(1)}, bf16[256,1024]{1,0:T(8,128)(2,1)S(1)}, u32[]{:S(2)}, u32[]{:S(2)}) collective-permute-start(bf16[256,1024]{1,0:T(8,128)(2,1)S(1)} %collective-permute-done.2.first_ref), channel_id=1, source_target_pairs={{1,2},{0,3},{35,32},{34,33},{5,6},{4,7},{39,36},{38,37},{9,10},{8,... | collective-permute-start | bytes 1572872 | tf_op jit(solution)/shard_map/ppermute | solution.py:460
  42.7 2.4 %copy-start.1 = (bf16[256,1024]{1,0:T(8,128)(2,1)}, bf16[256,1024]{1,0:T(8,128)(2,1)S(1)}, u32[]{:S(2)}) copy-start(bf16[256,1024]{1,0:T(8,128)(2,1)S(1)} %collective-permute-done.3.second_ref) | copy-start | bytes 1572868
  42.7 4.7 %collective-permute-start.4 = (bf16[8,256,256]{2,1,0:T(8,128)(2,1)S(1)}, bf16[8,256,256]{2,1,0:T(8,128)(2,1)S(1)}, u32[]{:S(2)}, u32[]{:S(2)}) collective-permute-start(bf16[8,256,256]{2,1,0:T(8,128)(2,1)S(1)} %all-to-all-done.own_ref), channel_id=1, source_target_pairs={{0,32},{32,0},{1,33},{33,1},{2,34},{34,2},{3,35},{35,3},{4,36},{36... | collective-permute-start | bytes 3145736 | tf_op jit(solution)/shard_map/ppermute | solution.py:477
  179.6 8.1 %collective-permute-start.5 = (bf16[128,128]{1,0:T(8,128)(2,1)S(1)}, bf16[128,128]{1,0:T(8,128)(2,1)S(1)}, u32[]{:S(2)}, u32[]{:S(2)}) collective-permute-start(bf16[128,128]{1,0:T(8,128)(2,1)S(1)} %weight_back.1), channel_id=1, source_target_pairs={{2,32},{32,2},{3,33},{33,3},{6,36},{36,6},{7,37},{37,7},{10,40},{4... | collective-permute-start | bytes 98312 | tf_op jit(solution)/shard_map/ppermute | solution.py:495
